TPU v7x, 512 devices: a whole 4x4x16 slice. The times are simulated.
512 devices in a mesh: seq: 16 (over y, x), head: 32 (over z, core).
Axes of the slice: x: 4, y: 4, z: 16, core: 2. Of those that a mesh axis runs over, the one named last changes fastest.
Arguments:
- q_raw: bfloat16 [6144, 4096], P('seq', 'head'), may hold values from -300 to 300
- k_raw: bfloat16 [6144, 4096], P('seq', 'head'), may hold values from -300 to 300
- values: bfloat16 [6144, 4096], P('seq', 'head'), may hold values from -6 to 6
- out: bfloat16 [6144, 4096], P('seq', 'head'), may hold values from -6 to 6
- d_out: bfloat16 [6144, 4096], P('seq', 'head'), may hold values from -6 to 6
- q_gain: bfloat16 [4096], P('head'), may hold values from 0.25 to 1.75
- k_gain: bfloat16 [4096], P('head'), may hold values from 0.25 to 1.75
- order: int32 [16], replicated, may hold values from 0 to 15, each once
Outputs:
- d_q: bfloat16 [6144, 4096], P('seq', 'head')
- d_k: bfloat16 [6144, 4096], P('seq', 'head')
- d_v: bfloat16 [6144, 4096], P('seq', 'head')
All inputs are finite; a program needn't handle non-finite values.
Results may differ from a plain program's by a relative error of at most 0.025.
Values may be sent and summed in bfloat16 or wider, within the bound.
No kernel may reach another device: no remote copies, remote signals or barrier semaphores. Data moves between devices by JAX's collectives and lax.ppermute only.
A program may use at most 64 MiB of HBM per device.

v0:
```python
import jax
import jax.numpy as jnp
from jax import lax
from jax.sharding import PartitionSpec as P

EPSILON = 1e-06


def from_behind(value, axis, steps):
    count = lax.axis_size(axis)
    pairs = [(source, (source + steps) % count) for source in range(count)]
    return lax.ppermute(value, axis, pairs)


def lookup(table, index):
    return jnp.sum(jnp.where(jnp.arange(table.shape[0], dtype=jnp.int32) == index, table, 0))


def rounded(partial_value):
    return lax.optimization_barrier(partial_value.astype(jnp.bfloat16)).astype(jnp.float32)


def block_total(queries, keys, visible):
    reciprocal_root = keys.shape[1] ** (-0.5)

    def compute():
        scores = jnp.dot(queries, keys.T, preferred_element_type=jnp.float32) * reciprocal_root
        return jnp.sum(jnp.exp(scores), axis=1)

    return compute() * visible.astype(jnp.float32)


def block_grads(queries, grad_out, log_total, delta, keys, vals, visible):
    reciprocal_root = keys.shape[1] ** (-0.5)
    contract = (((0,), (0,)), ((), ()))

    def compute(weight):
        scores = jnp.dot(queries, keys.T, preferred_element_type=jnp.float32) * reciprocal_root
        probs = jnp.exp(scores - log_total[:, None]) * weight
        probs_low = probs.astype(jnp.bfloat16)
        dprobs = jnp.dot(grad_out, vals.T, preferred_element_type=jnp.float32)
        dscores = (probs * (dprobs - delta[:, None])).astype(jnp.bfloat16)
        query_add = jnp.dot(dscores, keys, preferred_element_type=jnp.float32) * reciprocal_root
        key_add = (
            lax.dot_general(dscores, queries, contract, preferred_element_type=jnp.float32)
            * reciprocal_root
        )
        value_add = lax.dot_general(
            probs_low, grad_out, contract, preferred_element_type=jnp.float32
        )
        return (query_add, key_add, value_add)

    return compute(visible.astype(jnp.float32))


def local(q_raw, k_raw, values, out, d_out, q_gain, k_gain, order):
    device = lax.axis_index("seq")
    cycle_size = lax.axis_size("seq")
    feature_count = lax.axis_size("head") * q_raw.shape[1]
    rows_here = q_raw.shape[0]
    head_width = q_raw.shape[1]
    q_float = q_raw.astype(jnp.float32)
    k_float = k_raw.astype(jnp.float32)
    squares = lax.psum(
        (jnp.sum(q_float * q_float, axis=1), jnp.sum(k_float * k_float, axis=1)), "head"
    )
    q_rate = lax.rsqrt(squares[0] / feature_count + EPSILON)
    k_rate = lax.rsqrt(squares[1] / feature_count + EPSILON)
    q_scale = q_gain.astype(jnp.float32)
    k_scale = k_gain.astype(jnp.float32)
    q_norm = (q_float * q_rate[:, None] * q_scale).astype(jnp.bfloat16)
    k_norm = (k_float * k_rate[:, None] * k_scale).astype(jnp.bfloat16)
    own_group = lookup(order, device)
    delta = jnp.sum(d_out.astype(jnp.float32) * out.astype(jnp.float32), axis=1)
    last_source = (device + 1) % cycle_size
    zeros_block = jnp.zeros((rows_here, head_width), jnp.float32)

    def stat_turn(turn, state_tuple):
        held_keys, row_total = state_tuple
        source = (device - turn + cycle_size) % cycle_size
        row_total = row_total + block_total(q_norm, held_keys, lookup(order, source) <= own_group)
        held_keys = from_behind(held_keys, "seq", 1)
        return (held_keys, row_total)

    held_keys, row_total = lax.fori_loop(
        0, cycle_size - 1, stat_turn, (k_norm, jnp.zeros((rows_here,), jnp.float32))
    )
    row_total = row_total + block_total(q_norm, held_keys, lookup(order, last_source) <= own_group)
    log_total = jnp.log(row_total)

    def key_update(state_tuple, source):
        key_block, value_block, key_sums, value_sums, query_sum = state_tuple
        visible = lookup(order, source) <= own_group
        query_add, key_add, value_add = block_grads(
            q_norm, d_out, log_total, delta, key_block, value_block, visible
        )
        return (
            key_block,
            value_block,
            key_sums + rounded(key_add),
            value_sums + rounded(value_add),
            query_sum + query_add,
        )

    def key_turn(turn, state_tuple):
        state_tuple = key_update(state_tuple, (device - turn + cycle_size) % cycle_size)
        key_block, value_block = from_behind((state_tuple[0], state_tuple[1]), "seq", 1)
        key_sums, value_sums = (
            from_behind(state_tuple[2].astype(jnp.bfloat16), "seq", 1).astype(jnp.float32),
            from_behind(state_tuple[3].astype(jnp.bfloat16), "seq", 1).astype(jnp.float32),
        )
        return (key_block, value_block, key_sums, value_sums, state_tuple[4])

    final_state = lax.fori_loop(
        0, cycle_size - 1, key_turn, (k_norm, values, zeros_block, zeros_block, zeros_block)
    )
    final_state = key_update(final_state, last_source)
    key_grad, value_grad = (
        from_behind(final_state[2].astype(jnp.bfloat16), "seq", 1).astype(jnp.float32),
        from_behind(final_state[3].astype(jnp.bfloat16), "seq", 1).astype(jnp.float32),
    )
    query_grad = final_state[4]
    q_grad = query_grad * q_scale
    k_grad = key_grad * k_scale
    inner = lax.psum((jnp.sum(q_grad * q_float, axis=1), jnp.sum(k_grad * k_float, axis=1)), "head")
    d_q = q_rate[:, None] * q_grad - q_float * (q_rate**3 * inner[0] / feature_count)[:, None]
    d_k = k_rate[:, None] * k_grad - k_float * (k_rate**3 * inner[1] / feature_count)[:, None]
    return (d_q.astype(jnp.bfloat16), d_k.astype(jnp.bfloat16), value_grad.astype(jnp.bfloat16))


def solution(mesh):
    in_specs = (
        P("seq", "head"),
        P("seq", "head"),
        P("seq", "head"),
        P("seq", "head"),
        P("seq", "head"),
        P("head"),
        P("head"),
        P(),
    )
    out_specs = (P("seq", "head"), P("seq", "head"), P("seq", "head"))
    return jax.shard_map(local, mesh=mesh, in_specs=in_specs, out_specs=out_specs, check_vma=False)
```

profile of v0, /device:TPU:1, one launch (start us, length us, event | category | flops | bytes accessed | tf_op | source)
XLA Modules:
  0.0 577.2 jit_solution(10525459721698599912)
XLA Ops:
  2.7 53.3 %all-reduce.1 = (f32[384]{0:T(512)S(1)}, f32[384]{0:T(512)S(1)}) all-reduce(f32[384]{0:T(512)S(1)} %fusion.32, f32[384]{0:T(512)S(1)} %fusion.26), channel_id=1, replica_groups=mesh['seq'=16,'head'=32] {'head'}, use_global_device_ids=true, to_apply=%region_3.0 | all-reduce | flops 768 | bytes 6144 | tf_op jit(solution)/shard_map/psum | solution.py:64
  59.2 132.2 %while.42 = (s32[]{:T(128)}, bf16[384,128]{1,0:T(8,128)(2,1)S(1)}, f32[384]{0:T(512)S(1)}, bf16[384,128]{1,0:T(8,128)(2,1)S(1)}, s32[]{:T(128)}, /*index=5*/s32[...) while((s32[]{:T(128)}, bf16[384,128]{1,0:T(8,128)(2,1)S(1)}, ...), condition=%wide.region_8.9_spmd.clone, body=%wide.region_5.8_spmd.clone.sunk | while | flops 38044464 | bytes 792958 | solution.py:85
  59.2 3.1 collective-permute-start
  64.5 3.5 collective-permute-done
  72.2 4.6 collective-permute-done
  80.8 4.6 collective-permute-done
  89.5 4.6 collective-permute-done
  98.2 4.6 collective-permute-done
  106.9 4.7 collective-permute-done
  115.8 5.6 collective-permute-done
  125.5 4.6 collective-permute-done
  134.2 4.6 collective-permute-done
  142.9 4.6 collective-permute-done
  151.6 4.6 collective-permute-done
  160.3 4.6 collective-permute-done
  169.0 4.6 collective-permute-done
  177.7 4.6 collective-permute-done
  186.4 5.0 collective-permute-done
  193.8 275.8 %while.43 = (s32[]{:T(128)}, bf16[384,128]{1,0:T(8,128)(2,1)S(1)}, bf16[384,128]{1,0:T(8,128)(2,1)S(1)}, f32[384,128]{1,0:T(8,128)S(1)}, f32[384,128]{1,0:T(8,12...) while((s32[]{:T(128)}, bf16[384,128]{1,0:T(8,128)(2,1)S(1)}, ...), condition=%wide.region_14.15_spmd.clone, body=%wide.region_12.14_spmd.clone.sunk | while | flops 190562368 | bytes 7278120 | solution.py:114
  204.9 4.2 collective-permute-done.3
  222.6 4.2 collective-permute-done.3
  226.9 3.3 collective-permute-done.4
  241.3 4.2 collective-permute-done.3
  245.5 3.2 collective-permute-done.4
  259.9 4.2 collective-permute-done.3
  264.1 2.9 collective-permute-done.4
  276.0 5.5 collective-permute-start.4
  286.9 2.7 collective-permute-start.2
  294.6 4.0 collective-permute-start.4
  312.4 6.2 %collective-permute-start.4 = (bf16[384,128]{1,0:T(8,128)(2,1)S(1)}, bf16[384,128]{1,0:T(8,128)(2,1)S(1)}, u32[]{:S(2)}, u32[]{:S(2)}) collective-permute-start(bf16[384,128]{1,0:T(8,128)(2,1)S(1)} %fusion.106), channel_id=1, source_target_pairs={{0,32},{32,64},{64,96},{96,128},{128,160},{160,192},{192,224},{224... | collective-permute-start | bytes 294920 | tf_op jit(solution)/shard_map/while/body/eval_jaxpr/ppermute | solution.py:12
  321.2 3.5 collective-permute-start.1
  331.6 5.6 collective-permute-start.4
  340.4 3.5 collective-permute-start.1
  350.8 4.1 collective-permute-start.4
  369.1 3.7 collective-permute-start.4
  375.1 2.7 collective-permute-done.4
  387.4 3.3 collective-permute-start.4
  391.0 2.8 collective-permute-done.3
  405.1 3.8 collective-permute-start.4
  423.1 4.3 collective-permute-start.4
  429.6 3.0 collective-permute-done.4
  439.5 2.9 collective-permute-start.3
  442.8 4.5 collective-permute-start.4
  448.5 3.4 collective-permute-done.4
  460.8 4.1 collective-permute-start.4
  465.2 3.3 collective-permute-done.3
  475.2 6.3 %collective-permute-done.5 = bf16[384,128]{0,1:T(8,128)(2,1)S(1)} collective-permute-done((bf16[384,128]{0,1:T(8,128)(2,1)S(1)}, bf16[384,128]{0,1:T(8,128)(2,1)S(1)}, u32[]{:S(2)}, u32[]{:S(2)}) %collective-permute-start.5) | collective-permute-done | bytes 98336 | tf_op jit(solution)/shard_map/ppermute | solution.py:12
  481.6 93.3 %all-reduce = (f32[384]{0:T(512)S(1)}, f32[384]{0:T(512)S(1)}) all-reduce(f32[384]{0:T(512)S(1)} %get-tuple-element.636, f32[384]{0:T(512)S(1)} %fusion.35), channel_id=1, replica_groups=mesh['seq'=16,'head'=32] {'head'}, use_global_device_ids=true, to_apply=%region_16.17 | all-reduce | flops 768 | bytes 6144 | tf_op jit(solution)/shard_map/psum | solution.py:125
  (403 shorter events, 207.6 us)
Async XLA Ops:
  59.2 8.8 %collective-permute-start = (bf16[384,128]{1,0:T(8,128)(2,1)S(1)}, bf16[384,128]{1,0:T(8,128)(2,1)S(1)}, u32[]{:S(2)}, u32[]{:S(2)}) collective-permute-start(bf16[384,128]{1,0:T(8,128)(2,1)S(1)} %copy.29), channel_id=1, source_target_pairs={{0,32},{32,64},{64,96},{96,128},{128,160},{160,192},{192,224},{224... | collective-permute-start | bytes 294920 | tf_op jit(solution)/shard_map/while/body/eval_jaxpr/ppermute | solution.py:12
  102.8 8.9 %collective-permute-start = (bf16[384,128]{1,0:T(8,128)(2,1)S(1)}, bf16[384,128]{1,0:T(8,128)(2,1)S(1)}, u32[]{:S(2)}, u32[]{:S(2)}) collective-permute-start(bf16[384,128]{1,0:T(8,128)(2,1)S(1)} %copy.29), channel_id=1, source_target_pairs={{0,32},{32,64},{64,96},{96,128},{128,160},{160,192},{192,224},{224... | collective-permute-start | bytes 294920 | tf_op jit(solution)/shard_map/while/body/eval_jaxpr/ppermute | solution.py:12
  111.7 9.7 %collective-permute-start = (bf16[384,128]{1,0:T(8,128)(2,1)S(1)}, bf16[384,128]{1,0:T(8,128)(2,1)S(1)}, u32[]{:S(2)}, u32[]{:S(2)}) collective-permute-start(bf16[384,128]{1,0:T(8,128)(2,1)S(1)} %copy.29), channel_id=1, source_target_pairs={{0,32},{32,64},{64,96},{96,128},{128,160},{160,192},{192,224},{224... | collective-permute-start | bytes 294920 | tf_op jit(solution)/shard_map/while/body/eval_jaxpr/ppermute | solution.py:12
  182.3 9.1 %collective-permute-start = (bf16[384,128]{1,0:T(8,128)(2,1)S(1)}, bf16[384,128]{1,0:T(8,128)(2,1)S(1)}, u32[]{:S(2)}, u32[]{:S(2)}) collective-permute-start(bf16[384,128]{1,0:T(8,128)(2,1)S(1)} %copy.29), channel_id=1, source_target_pairs={{0,32},{32,64},{64,96},{96,128},{128,160},{160,192},{192,224},{224... | collective-permute-start | bytes 294920 | tf_op jit(solution)/shard_map/while/body/eval_jaxpr/ppermute | solution.py:12
  193.8 17.7 %collective-permute-start.1 = (bf16[384,128]{1,0:T(8,128)(2,1)S(1)}, bf16[384,128]{1,0:T(8,128)(2,1)S(1)}, u32[]{:S(2)}, u32[]{:S(2)}) collective-permute-start(bf16[384,128]{1,0:T(8,128)(2,1)S(1)} %copy.41), channel_id=1, source_target_pairs={{0,32},{32,64},{64,96},{96,128},{128,160},{160,192},{192,224},{224... | collective-permute-start | bytes 294920 | tf_op jit(solution)/shard_map/while/body/eval_jaxpr/ppermute | solution.py:12
  195.7 15.8 %collective-permute-start.2 = (bf16[384,128]{1,0:T(8,128)(2,1)S(1)}, bf16[384,128]{1,0:T(8,128)(2,1)S(1)}, u32[]{:S(2)}, u32[]{:S(2)}) collective-permute-start(bf16[384,128]{1,0:T(8,128)(2,1)S(1)} %copy.42), channel_id=1, source_target_pairs={{0,32},{32,64},{64,96},{96,128},{128,160},{160,192},{192,224},{224... | collective-permute-start | bytes 294920 | tf_op jit(solution)/shard_map/while/body/eval_jaxpr/ppermute | solution.py:12
  202.7 8.8 %collective-permute-start.4 = (bf16[384,128]{1,0:T(8,128)(2,1)S(1)}, bf16[384,128]{1,0:T(8,128)(2,1)S(1)}, u32[]{:S(2)}, u32[]{:S(2)}) collective-permute-start(bf16[384,128]{1,0:T(8,128)(2,1)S(1)} %fusion.106), channel_id=1, source_target_pairs={{0,32},{32,64},{64,96},{96,128},{128,160},{160,192},{192,224},{224... | collective-permute-start | bytes 294920 | tf_op jit(solution)/shard_map/while/body/eval_jaxpr/ppermute | solution.py:12
  211.6 18.6 %collective-permute-start.1 = (bf16[384,128]{1,0:T(8,128)(2,1)S(1)}, bf16[384,128]{1,0:T(8,128)(2,1)S(1)}, u32[]{:S(2)}, u32[]{:S(2)}) collective-permute-start(bf16[384,128]{1,0:T(8,128)(2,1)S(1)} %copy.41), channel_id=1, source_target_pairs={{0,32},{32,64},{64,96},{96,128},{128,160},{160,192},{192,224},{224... | collective-permute-start | bytes 294920 | tf_op jit(solution)/shard_map/while/body/eval_jaxpr/ppermute | solution.py:12
  213.5 16.7 %collective-permute-start.2 = (bf16[384,128]{1,0:T(8,128)(2,1)S(1)}, bf16[384,128]{1,0:T(8,128)(2,1)S(1)}, u32[]{:S(2)}, u32[]{:S(2)}) collective-permute-start(bf16[384,128]{1,0:T(8,128)(2,1)S(1)} %copy.42), channel_id=1, source_target_pairs={{0,32},{32,64},{64,96},{96,128},{128,160},{160,192},{192,224},{224... | collective-permute-start | bytes 294920 | tf_op jit(solution)/shard_map/while/body/eval_jaxpr/ppermute | solution.py:12
  218.2 8.7 %collective-permute-start.3 = (bf16[384,128]{1,0:T(8,128)(2,1)S(1)}, bf16[384,128]{1,0:T(8,128)(2,1)S(1)}, u32[]{:S(2)}, u32[]{:S(2)}) collective-permute-start(bf16[384,128]{1,0:T(8,128)(2,1)S(1)} %fusion.105), channel_id=1, source_target_pairs={{0,32},{32,64},{64,96},{96,128},{128,160},{160,192},{192,224},{224... | collective-permute-start | bytes 294920 | tf_op jit(solution)/shard_map/while/body/eval_jaxpr/ppermute | solution.py:12
  220.4 9.7 %collective-permute-start.4 = (bf16[384,128]{1,0:T(8,128)(2,1)S(1)}, bf16[384,128]{1,0:T(8,128)(2,1)S(1)}, u32[]{:S(2)}, u32[]{:S(2)}) collective-permute-start(bf16[384,128]{1,0:T(8,128)(2,1)S(1)} %fusion.106), channel_id=1, source_target_pairs={{0,32},{32,64},{64,96},{96,128},{128,160},{160,192},{192,224},{224... | collective-permute-start | bytes 294920 | tf_op jit(solution)/shard_map/while/body/eval_jaxpr/ppermute | solution.py:12
  230.2 18.5 %collective-permute-start.1 = (bf16[384,128]{1,0:T(8,128)(2,1)S(1)}, bf16[384,128]{1,0:T(8,128)(2,1)S(1)}, u32[]{:S(2)}, u32[]{:S(2)}) collective-permute-start(bf16[384,128]{1,0:T(8,128)(2,1)S(1)} %copy.41), channel_id=1, source_target_pairs={{0,32},{32,64},{64,96},{96,128},{128,160},{160,192},{192,224},{224... | collective-permute-start | bytes 294920 | tf_op jit(solution)/shard_map/while/body/eval_jaxpr/ppermute | solution.py:12
  232.2 16.6 %collective-permute-start.2 = (bf16[384,128]{1,0:T(8,128)(2,1)S(1)}, bf16[384,128]{1,0:T(8,128)(2,1)S(1)}, u32[]{:S(2)}, u32[]{:S(2)}) collective-permute-start(bf16[384,128]{1,0:T(8,128)(2,1)S(1)} %copy.42), channel_id=1, source_target_pairs={{0,32},{32,64},{64,96},{96,128},{128,160},{160,192},{192,224},{224... | collective-permute-start | bytes 294920 | tf_op jit(solution)/shard_map/while/body/eval_jaxpr/ppermute | solution.py:12
  239.1 9.6 %collective-permute-start.4 = (bf16[384,128]{1,0:T(8,128)(2,1)S(1)}, bf16[384,128]{1,0:T(8,128)(2,1)S(1)}, u32[]{:S(2)}, u32[]{:S(2)}) collective-permute-start(bf16[384,128]{1,0:T(8,128)(2,1)S(1)} %fusion.106), channel_id=1, source_target_pairs={{0,32},{32,64},{64,96},{96,128},{128,160},{160,192},{192,224},{224... | collective-permute-start | bytes 294920 | tf_op jit(solution)/shard_map/while/body/eval_jaxpr/ppermute | solution.py:12
  248.8 18.3 %collective-permute-start.1 = (bf16[384,128]{1,0:T(8,128)(2,1)S(1)}, bf16[384,128]{1,0:T(8,128)(2,1)S(1)}, u32[]{:S(2)}, u32[]{:S(2)}) collective-permute-start(bf16[384,128]{1,0:T(8,128)(2,1)S(1)} %copy.41), channel_id=1, source_target_pairs={{0,32},{32,64},{64,96},{96,128},{128,160},{160,192},{192,224},{224... | collective-permute-start | bytes 294920 | tf_op jit(solution)/shard_map/while/body/eval_jaxpr/ppermute | solution.py:12
  250.7 16.3 %collective-permute-start.2 = (bf16[384,128]{1,0:T(8,128)(2,1)S(1)}, bf16[384,128]{1,0:T(8,128)(2,1)S(1)}, u32[]{:S(2)}, u32[]{:S(2)}) collective-permute-start(bf16[384,128]{1,0:T(8,128)(2,1)S(1)} %copy.42), channel_id=1, source_target_pairs={{0,32},{32,64},{64,96},{96,128},{128,160},{160,192},{192,224},{224... | collective-permute-start | bytes 294920 | tf_op jit(solution)/shard_map/while/body/eval_jaxpr/ppermute | solution.py:12
  257.7 9.4 %collective-permute-start.4 = (bf16[384,128]{1,0:T(8,128)(2,1)S(1)}, bf16[384,128]{1,0:T(8,128)(2,1)S(1)}, u32[]{:S(2)}, u32[]{:S(2)}) collective-permute-start(bf16[384,128]{1,0:T(8,128)(2,1)S(1)} %fusion.106), channel_id=1, source_target_pairs={{0,32},{32,64},{64,96},{96,128},{128,160},{160,192},{192,224},{224... | collective-permute-start | bytes 294920 | tf_op jit(solution)/shard_map/while/body/eval_jaxpr/ppermute | solution.py:12
  267.1 17.6 %collective-permute-start.1 = (bf16[384,128]{1,0:T(8,128)(2,1)S(1)}, bf16[384,128]{1,0:T(8,128)(2,1)S(1)}, u32[]{:S(2)}, u32[]{:S(2)}) collective-permute-start(bf16[384,128]{1,0:T(8,128)(2,1)S(1)} %copy.41), channel_id=1, source_target_pairs={{0,32},{32,64},{64,96},{96,128},{128,160},{160,192},{192,224},{224... | collective-permute-start | bytes 294920 | tf_op jit(solution)/shard_map/while/body/eval_jaxpr/ppermute | solution.py:12
  269.1 15.6 %collective-permute-start.2 = (bf16[384,128]{1,0:T(8,128)(2,1)S(1)}, bf16[384,128]{1,0:T(8,128)(2,1)S(1)}, u32[]{:S(2)}, u32[]{:S(2)}) collective-permute-start(bf16[384,128]{1,0:T(8,128)(2,1)S(1)} %copy.42), channel_id=1, source_target_pairs={{0,32},{32,64},{64,96},{96,128},{128,160},{160,192},{192,224},{224... | collective-permute-start | bytes 294920 | tf_op jit(solution)/shard_map/while/body/eval_jaxpr/ppermute | solution.py:12
  284.7 18.6 %collective-permute-start.1 = (bf16[384,128]{1,0:T(8,128)(2,1)S(1)}, bf16[384,128]{1,0:T(8,128)(2,1)S(1)}, u32[]{:S(2)}, u32[]{:S(2)}) collective-permute-start(bf16[384,128]{1,0:T(8,128)(2,1)S(1)} %copy.41), channel_id=1, source_target_pairs={{0,32},{32,64},{64,96},{96,128},{128,160},{160,192},{192,224},{224... | collective-permute-start | bytes 294920 | tf_op jit(solution)/shard_map/while/body/eval_jaxpr/ppermute | solution.py:12
  286.9 16.4 %collective-permute-start.2 = (bf16[384,128]{1,0:T(8,128)(2,1)S(1)}, bf16[384,128]{1,0:T(8,128)(2,1)S(1)}, u32[]{:S(2)}, u32[]{:S(2)}) collective-permute-start(bf16[384,128]{1,0:T(8,128)(2,1)S(1)} %copy.42), channel_id=1, source_target_pairs={{0,32},{32,64},{64,96},{96,128},{128,160},{160,192},{192,224},{224... | collective-permute-start | bytes 294920 | tf_op jit(solution)/shard_map/while/body/eval_jaxpr/ppermute | solution.py:12
  303.3 17.8 %collective-permute-start.1 = (bf16[384,128]{1,0:T(8,128)(2,1)S(1)}, bf16[384,128]{1,0:T(8,128)(2,1)S(1)}, u32[]{:S(2)}, u32[]{:S(2)}) collective-permute-start(bf16[384,128]{1,0:T(8,128)(2,1)S(1)} %copy.41), channel_id=1, source_target_pairs={{0,32},{32,64},{64,96},{96,128},{128,160},{160,192},{192,224},{224... | collective-permute-start | bytes 294920 | tf_op jit(solution)/shard_map/while/body/eval_jaxpr/ppermute | solution.py:12
  305.3 15.9 %collective-permute-start.2 = (bf16[384,128]{1,0:T(8,128)(2,1)S(1)}, bf16[384,128]{1,0:T(8,128)(2,1)S(1)}, u32[]{:S(2)}, u32[]{:S(2)}) collective-permute-start(bf16[384,128]{1,0:T(8,128)(2,1)S(1)} %copy.42), channel_id=1, source_target_pairs={{0,32},{32,64},{64,96},{96,128},{128,160},{160,192},{192,224},{224... | collective-permute-start | bytes 294920 | tf_op jit(solution)/shard_map/while/body/eval_jaxpr/ppermute | solution.py:12
  310.0 9.0 %collective-permute-start.3 = (bf16[384,128]{1,0:T(8,128)(2,1)S(1)}, bf16[384,128]{1,0:T(8,128)(2,1)S(1)}, u32[]{:S(2)}, u32[]{:S(2)}) collective-permute-start(bf16[384,128]{1,0:T(8,128)(2,1)S(1)} %fusion.105), channel_id=1, source_target_pairs={{0,32},{32,64},{64,96},{96,128},{128,160},{160,192},{192,224},{224... | collective-permute-start | bytes 294920 | tf_op jit(solution)/shard_map/while/body/eval_jaxpr/ppermute | solution.py:12
  321.2 19.2 %collective-permute-start.1 = (bf16[384,128]{1,0:T(8,128)(2,1)S(1)}, bf16[384,128]{1,0:T(8,128)(2,1)S(1)}, u32[]{:S(2)}, u32[]{:S(2)}) collective-permute-start(bf16[384,128]{1,0:T(8,128)(2,1)S(1)} %copy.41), channel_id=1, source_target_pairs={{0,32},{32,64},{64,96},{96,128},{128,160},{160,192},{192,224},{224... | collective-permute-start | bytes 294920 | tf_op jit(solution)/shard_map/while/body/eval_jaxpr/ppermute | solution.py:12
  324.7 15.6 %collective-permute-start.2 = (bf16[384,128]{1,0:T(8,128)(2,1)S(1)}, bf16[384,128]{1,0:T(8,128)(2,1)S(1)}, u32[]{:S(2)}, u32[]{:S(2)}) collective-permute-start(bf16[384,128]{1,0:T(8,128)(2,1)S(1)} %copy.42), channel_id=1, source_target_pairs={{0,32},{32,64},{64,96},{96,128},{128,160},{160,192},{192,224},{224... | collective-permute-start | bytes 294920 | tf_op jit(solution)/shard_map/while/body/eval_jaxpr/ppermute | solution.py:12
  340.4 19.1 %collective-permute-start.1 = (bf16[384,128]{1,0:T(8,128)(2,1)S(1)}, bf16[384,128]{1,0:T(8,128)(2,1)S(1)}, u32[]{:S(2)}, u32[]{:S(2)}) collective-permute-start(bf16[384,128]{1,0:T(8,128)(2,1)S(1)} %copy.41), channel_id=1, source_target_pairs={{0,32},{32,64},{64,96},{96,128},{128,160},{160,192},{192,224},{224... | collective-permute-start | bytes 294920 | tf_op jit(solution)/shard_map/while/body/eval_jaxpr/ppermute | solution.py:12
  343.9 15.6 %collective-permute-start.2 = (bf16[384,128]{1,0:T(8,128)(2,1)S(1)}, bf16[384,128]{1,0:T(8,128)(2,1)S(1)}, u32[]{:S(2)}, u32[]{:S(2)}) collective-permute-start(bf16[384,128]{1,0:T(8,128)(2,1)S(1)} %copy.42), channel_id=1, source_target_pairs={{0,32},{32,64},{64,96},{96,128},{128,160},{160,192},{192,224},{224... | collective-permute-start | bytes 294920 | tf_op jit(solution)/shard_map/while/body/eval_jaxpr/ppermute | solution.py:12
  359.6 18.2 %collective-permute-start.1 = (bf16[384,128]{1,0:T(8,128)(2,1)S(1)}, bf16[384,128]{1,0:T(8,128)(2,1)S(1)}, u32[]{:S(2)}, u32[]{:S(2)}) collective-permute-start(bf16[384,128]{1,0:T(8,128)(2,1)S(1)} %copy.41), channel_id=1, source_target_pairs={{0,32},{32,64},{64,96},{96,128},{128,160},{160,192},{192,224},{224... | collective-permute-start | bytes 294920 | tf_op jit(solution)/shard_map/while/body/eval_jaxpr/ppermute | solution.py:12
  361.5 16.3 %collective-permute-start.2 = (bf16[384,128]{1,0:T(8,128)(2,1)S(1)}, bf16[384,128]{1,0:T(8,128)(2,1)S(1)}, u32[]{:S(2)}, u32[]{:S(2)}) collective-permute-start(bf16[384,128]{1,0:T(8,128)(2,1)S(1)} %copy.42), channel_id=1, source_target_pairs={{0,32},{32,64},{64,96},{96,128},{128,160},{160,192},{192,224},{224... | collective-permute-start | bytes 294920 | tf_op jit(solution)/shard_map/while/body/eval_jaxpr/ppermute | solution.py:12
  377.9 18.3 %collective-permute-start.1 = (bf16[384,128]{1,0:T(8,128)(2,1)S(1)}, bf16[384,128]{1,0:T(8,128)(2,1)S(1)}, u32[]{:S(2)}, u32[]{:S(2)}) collective-permute-start(bf16[384,128]{1,0:T(8,128)(2,1)S(1)} %copy.41), channel_id=1, source_target_pairs={{0,32},{32,64},{64,96},{96,128},{128,160},{160,192},{192,224},{224... | collective-permute-start | bytes 294920 | tf_op jit(solution)/shard_map/while/body/eval_jaxpr/ppermute | solution.py:12
  379.8 16.3 %collective-permute-start.2 = (bf16[384,128]{1,0:T(8,128)(2,1)S(1)}, bf16[384,128]{1,0:T(8,128)(2,1)S(1)}, u32[]{:S(2)}, u32[]{:S(2)}) collective-permute-start(bf16[384,128]{1,0:T(8,128)(2,1)S(1)} %copy.42), channel_id=1, source_target_pairs={{0,32},{32,64},{64,96},{96,128},{128,160},{160,192},{192,224},{224... | collective-permute-start | bytes 294920 | tf_op jit(solution)/shard_map/while/body/eval_jaxpr/ppermute | solution.py:12
  396.2 17.6 %collective-permute-start.1 = (bf16[384,128]{1,0:T(8,128)(2,1)S(1)}, bf16[384,128]{1,0:T(8,128)(2,1)S(1)}, u32[]{:S(2)}, u32[]{:S(2)}) collective-permute-start(bf16[384,128]{1,0:T(8,128)(2,1)S(1)} %copy.41), channel_id=1, source_target_pairs={{0,32},{32,64},{64,96},{96,128},{128,160},{160,192},{192,224},{224... | collective-permute-start | bytes 294920 | tf_op jit(solution)/shard_map/while/body/eval_jaxpr/ppermute | solution.py:12
  398.1 15.6 %collective-permute-start.2 = (bf16[384,128]{1,0:T(8,128)(2,1)S(1)}, bf16[384,128]{1,0:T(8,128)(2,1)S(1)}, u32[]{:S(2)}, u32[]{:S(2)}) collective-permute-start(bf16[384,128]{1,0:T(8,128)(2,1)S(1)} %copy.42), channel_id=1, source_target_pairs={{0,32},{32,64},{64,96},{96,128},{128,160},{160,192},{192,224},{224... | collective-permute-start | bytes 294920 | tf_op jit(solution)/shard_map/while/body/eval_jaxpr/ppermute | solution.py:12
  402.8 8.7 %collective-permute-start.3 = (bf16[384,128]{1,0:T(8,128)(2,1)S(1)}, bf16[384,128]{1,0:T(8,128)(2,1)S(1)}, u32[]{:S(2)}, u32[]{:S(2)}) collective-permute-start(bf16[384,128]{1,0:T(8,128)(2,1)S(1)} %fusion.105), channel_id=1, source_target_pairs={{0,32},{32,64},{64,96},{96,128},{128,160},{160,192},{192,224},{224... | collective-permute-start | bytes 294920 | tf_op jit(solution)/shard_map/while/body/eval_jaxpr/ppermute | solution.py:12
  405.1 8.7 %collective-permute-start.4 = (bf16[384,128]{1,0:T(8,128)(2,1)S(1)}, bf16[384,128]{1,0:T(8,128)(2,1)S(1)}, u32[]{:S(2)}, u32[]{:S(2)}) collective-permute-start(bf16[384,128]{1,0:T(8,128)(2,1)S(1)} %fusion.106), channel_id=1, source_target_pairs={{0,32},{32,64},{64,96},{96,128},{128,160},{160,192},{192,224},{224... | collective-permute-start | bytes 294920 | tf_op jit(solution)/shard_map/while/body/eval_jaxpr/ppermute | solution.py:12
  413.8 18.7 %collective-permute-start.1 = (bf16[384,128]{1,0:T(8,128)(2,1)S(1)}, bf16[384,128]{1,0:T(8,128)(2,1)S(1)}, u32[]{:S(2)}, u32[]{:S(2)}) collective-permute-start(bf16[384,128]{1,0:T(8,128)(2,1)S(1)} %copy.41), channel_id=1, source_target_pairs={{0,32},{32,64},{64,96},{96,128},{128,160},{160,192},{192,224},{224... | collective-permute-start | bytes 294920 | tf_op jit(solution)/shard_map/while/body/eval_jaxpr/ppermute | solution.py:12
  415.8 16.8 %collective-permute-start.2 = (bf16[384,128]{1,0:T(8,128)(2,1)S(1)}, bf16[384,128]{1,0:T(8,128)(2,1)S(1)}, u32[]{:S(2)}, u32[]{:S(2)}) collective-permute-start(bf16[384,128]{1,0:T(8,128)(2,1)S(1)} %copy.42), channel_id=1, source_target_pairs={{0,32},{32,64},{64,96},{96,128},{128,160},{160,192},{192,224},{224... | collective-permute-start | bytes 294920 | tf_op jit(solution)/shard_map/while/body/eval_jaxpr/ppermute | solution.py:12
  423.1 9.4 %collective-permute-start.4 = (bf16[384,128]{1,0:T(8,128)(2,1)S(1)}, bf16[384,128]{1,0:T(8,128)(2,1)S(1)}, u32[]{:S(2)}, u32[]{:S(2)}) collective-permute-start(bf16[384,128]{1,0:T(8,128)(2,1)S(1)} %fusion.106), channel_id=1, source_target_pairs={{0,32},{32,64},{64,96},{96,128},{128,160},{160,192},{192,224},{224... | collective-permute-start | bytes 294920 | tf_op jit(solution)/shard_map/while/body/eval_jaxpr/ppermute | solution.py:12
  432.6 19.3 %collective-permute-start.1 = (bf16[384,128]{1,0:T(8,128)(2,1)S(1)}, bf16[384,128]{1,0:T(8,128)(2,1)S(1)}, u32[]{:S(2)}, u32[]{:S(2)}) collective-permute-start(bf16[384,128]{1,0:T(8,128)(2,1)S(1)} %copy.41), channel_id=1, source_target_pairs={{0,32},{32,64},{64,96},{96,128},{128,160},{160,192},{192,224},{224... | collective-permute-start | bytes 294920 | tf_op jit(solution)/shard_map/while/body/eval_jaxpr/ppermute | solution.py:12
  434.5 17.4 %collective-permute-start.2 = (bf16[384,128]{1,0:T(8,128)(2,1)S(1)}, bf16[384,128]{1,0:T(8,128)(2,1)S(1)}, u32[]{:S(2)}, u32[]{:S(2)}) collective-permute-start(bf16[384,128]{1,0:T(8,128)(2,1)S(1)} %copy.42), channel_id=1, source_target_pairs={{0,32},{32,64},{64,96},{96,128},{128,160},{160,192},{192,224},{224... | collective-permute-start | bytes 294920 | tf_op jit(solution)/shard_map/while/body/eval_jaxpr/ppermute | solution.py:12
  439.5 8.9 %collective-permute-start.3 = (bf16[384,128]{1,0:T(8,128)(2,1)S(1)}, bf16[384,128]{1,0:T(8,128)(2,1)S(1)}, u32[]{:S(2)}, u32[]{:S(2)}) collective-permute-start(bf16[384,128]{1,0:T(8,128)(2,1)S(1)} %fusion.105), channel_id=1, source_target_pairs={{0,32},{32,64},{64,96},{96,128},{128,160},{160,192},{192,224},{224... | collective-permute-start | bytes 294920 | tf_op jit(solution)/shard_map/while/body/eval_jaxpr/ppermute | solution.py:12
  442.8 9.1 %collective-permute-start.4 = (bf16[384,128]{1,0:T(8,128)(2,1)S(1)}, bf16[384,128]{1,0:T(8,128)(2,1)S(1)}, u32[]{:S(2)}, u32[]{:S(2)}) collective-permute-start(bf16[384,128]{1,0:T(8,128)(2,1)S(1)} %fusion.106), channel_id=1, source_target_pairs={{0,32},{32,64},{64,96},{96,128},{128,160},{160,192},{192,224},{224... | collective-permute-start | bytes 294920 | tf_op jit(solution)/shard_map/while/body/eval_jaxpr/ppermute | solution.py:12
  452.0 17.6 %collective-permute-start.1 = (bf16[384,128]{1,0:T(8,128)(2,1)S(1)}, bf16[384,128]{1,0:T(8,128)(2,1)S(1)}, u32[]{:S(2)}, u32[]{:S(2)}) collective-permute-start(bf16[384,128]{1,0:T(8,128)(2,1)S(1)} %copy.41), channel_id=1, source_target_pairs={{0,32},{32,64},{64,96},{96,128},{128,160},{160,192},{192,224},{224... | collective-permute-start | bytes 294920 | tf_op jit(solution)/shard_map/while/body/eval_jaxpr/ppermute | solution.py:12
  453.9 15.6 %collective-permute-start.2 = (bf16[384,128]{1,0:T(8,128)(2,1)S(1)}, bf16[384,128]{1,0:T(8,128)(2,1)S(1)}, u32[]{:S(2)}, u32[]{:S(2)}) collective-permute-start(bf16[384,128]{1,0:T(8,128)(2,1)S(1)} %copy.42), channel_id=1, source_target_pairs={{0,32},{32,64},{64,96},{96,128},{128,160},{160,192},{192,224},{224... | collective-permute-start | bytes 294920 | tf_op jit(solution)/shard_map/while/body/eval_jaxpr/ppermute | solution.py:12
  458.6 10.0 %collective-permute-start.3 = (bf16[384,128]{1,0:T(8,128)(2,1)S(1)}, bf16[384,128]{1,0:T(8,128)(2,1)S(1)}, u32[]{:S(2)}, u32[]{:S(2)}) collective-permute-start(bf16[384,128]{1,0:T(8,128)(2,1)S(1)} %fusion.105), channel_id=1, source_target_pairs={{0,32},{32,64},{64,96},{96,128},{128,160},{160,192},{192,224},{224... | collective-permute-start | bytes 294920 | tf_op jit(solution)/shard_map/while/body/eval_jaxpr/ppermute | solution.py:12
  460.8 8.7 %collective-permute-start.4 = (bf16[384,128]{1,0:T(8,128)(2,1)S(1)}, bf16[384,128]{1,0:T(8,128)(2,1)S(1)}, u32[]{:S(2)}, u32[]{:S(2)}) collective-permute-start(bf16[384,128]{1,0:T(8,128)(2,1)S(1)} %fusion.106), channel_id=1, source_target_pairs={{0,32},{32,64},{64,96},{96,128},{128,160},{160,192},{192,224},{224... | collective-permute-start | bytes 294920 | tf_op jit(solution)/shard_map/while/body/eval_jaxpr/ppermute | solution.py:12
  470.1 106.5 %collective-permute-start.6 = (bf16[384,128]{1,0:T(8,128)(2,1)S(1)}, bf16[384,128]{1,0:T(8,128)(2,1)S(1)}, u32[]{:S(2)}, u32[]{:S(2)}) collective-permute-start(bf16[384,128]{1,0:T(8,128)(2,1)S(1)} %add_convert_fusion), channel_id=1, source_target_pairs={{0,32},{32,64},{64,96},{96,128},{128,160},{160,192},{192,224},{224... | collective-permute-start | bytes 294920 | tf_op jit(solution)/shard_map/ppermute | solution.py:12
  (37 other events, 259.5 us)
where the time goes:
time: 580 us; the launch traced here: 577 us
  starting transfers between devices  185 us (32%)
  waiting for transfers between devices  148 us (26%)
  blocking collectives  147 us (25%)
  loops' own time  39.1 us (7%)
  matrix products  26.4 us (5%)
  other arithmetic  22.5 us (4%)
  local copies, waits for them, and re-layouts  7.61 us (1%)
    ppermute x77, starting transfers between devices, from_behind(): return lax.ppermute(value, axis, pairs)  185 us
    ppermute x77, waiting for transfers between devices, from_behind(): return lax.ppermute(value, axis, pairs)  148 us
    psum x1, blocking collectives, local(): lax.psum((jnp.sum(q_grad * q_float, axis=1), jnp.sum(k_grad * k_float, ax...  93.3 us
    psum x1, blocking collectives, local(): lax.psum((jnp.sum(q_float * q_float, axis=1), jnp.sum(k_float * k_float,...  53.3 us
    another operation x1, loops' own time, local(): lax.fori_loop(0, cycle_size - 1, key_turn, (k_norm, values, zeros_block,...  20.4 us
    reduce_sum x31, other arithmetic, lookup(): jnp.sum(jnp.where(jnp.arange(table.shape[0], dtype=jnp.int32) == index, t...  20.1 us
    another operation x1, loops' own time, local(): lax.fori_loop(0, cycle_size - 1, stat_turn, (k_norm, jnp.zeros((rows_here...  18.7 us
  transfers between devices with their start and end apart: 77, of which 45 were waited for; matrix products, arithmetic and copies ran while one was open for 8% of the time, Pallas kernels for 0%

commit v1 on v0

v1 whole, which is shorter than its diff:
```python
import math

import jax
import jax.numpy as jnp
from jax import lax
from jax.experimental import pallas as pl
from jax.experimental.pallas import tpu as pltpu
from jax.sharding import Mesh, PartitionSpec as P

EPSILON = 1e-06
SIDE = 4
ROWS = 384
WIDTH = 128
PIECES = ROWS // WIDTH
HEAD = ("z", "c")
SEQ = ("y", "x")
F32 = jnp.float32
BF16 = jnp.bfloat16
ROOT = WIDTH ** (-0.5)
LOG2E = math.log2(math.e)


def shift(value, axis, steps):
    count = lax.axis_size(axis)
    return lax.ppermute(value, axis, [(i, (i + steps) % count) for i in range(count)])


def struct(shape, dtype):
    return jax.ShapeDtypeStruct(shape, dtype)


def call(kernel, out_shape, scratch=(), smem=0, limit=32):
    def run(*args):
        specs = [
            pl.BlockSpec(memory_space=pltpu.SMEM if i < smem else pltpu.VMEM)
            for i in range(len(args))
        ]
        return pl.pallas_call(
            kernel,
            out_shape=out_shape,
            in_specs=specs,
            out_specs=jax.tree.map(lambda _: pl.BlockSpec(memory_space=pltpu.VMEM), out_shape),
            scratch_shapes=scratch,
            compiler_params=pltpu.CompilerParams(vmem_limit_bytes=limit * 2**20),
        )(*args)

    return run


def column(row):
    return jnp.broadcast_to(row, (WIDTH, WIDTH)).T


def row_sums(block):
    return jnp.sum(block.T, axis=0, keepdims=True)


def dot(a, b, dims=(((1,), (0,)), ((), ()))):
    return lax.dot_general(a, b, dims, preferred_element_type=F32)


NT = (((1,), (1,)), ((), ()))
TN = (((0,), (0,)), ((), ()))


def squares_kernel(q_ref, k_ref, v_ref, o_ref, g_ref, msg_ref, delta_ref, qg_ref, kv_ref):
    part = jnp.zeros((8, WIDTH), F32)
    delta = jnp.zeros((8, WIDTH), F32)
    line = lax.broadcasted_iota(jnp.int32, (8, WIDTH), 0)
    for i in range(PIECES):
        rows = pl.ds(i * WIDTH, WIDTH)
        q = q_ref[rows, :].astype(F32)
        k = k_ref[rows, :].astype(F32)
        g = g_ref[rows, :].astype(F32)
        o = o_ref[rows, :].astype(F32)
        part = jnp.where(line == i, row_sums(q * q), part)
        part = jnp.where(line == PIECES + i, row_sums(k * k), part)
        delta = jnp.where(line == i, row_sums(g * o), delta)
    msg_ref[...] = jnp.broadcast_to(part[None], msg_ref.shape)
    delta_ref[...] = delta
    qg_ref[:ROWS, :] = q_ref[...]
    qg_ref[ROWS:, :] = g_ref[...]
    kv_ref[:ROWS, :] = k_ref[...]
    kv_ref[ROWS:, :] = v_ref[...]


def rates_kernel(sums_ref, delta_ref, msg_ref, own_ref):
    total = jnp.sum(sums_ref[...], axis=0)
    rate = lax.rsqrt(total / (32 * WIDTH) + EPSILON)
    own_ref[...] = rate
    msg_ref[:, :8, :] = jnp.broadcast_to(rate[None], (16, 8, WIDTH))
    msg_ref[:, 8:, :] = jnp.broadcast_to(delta_ref[...][None], (16, 8, WIDTH))


def totals_kernel(
    place_ref, order_ref, rates_ref, qgain_ref, kgain_ref,
    qg0, qg1, qg2, qg3, kv0, kv1, kv2, kv3,
    total_ref, qn_ref, kn_ref,
):
    y = place_ref[0]
    x = place_ref[1]
    q_gain = qgain_ref[...].astype(F32)
    k_gain = kgain_ref[...].astype(F32)
    for d, (qg, kv) in enumerate(zip((qg0, qg1, qg2, qg3), (kv0, kv1, kv2, kv3))):
        xs = lax.rem(x - d + SIDE, SIDE)
        ys = lax.rem(y - d + SIDE, SIDE)
        q_rate = rates_ref[y * SIDE + xs]
        k_rate = rates_ref[ys * SIDE + x]
        for i in range(PIECES):
            rows = pl.ds(i * WIDTH, WIDTH)
            q = qg[rows, :].astype(F32) * column(q_rate[i : i + 1, :]) * q_gain
            k = kv[rows, :].astype(F32) * column(k_rate[PIECES + i : PIECES + i + 1, :]) * k_gain
            qn_ref[xs, rows, :] = q.astype(BF16)
            kn_ref[ys, rows, :] = k.astype(BF16)
    total_ref[...] = jnp.zeros_like(total_ref)

    def tile(t, carry):
        i = t // SIDE
        j = lax.rem(t, SIDE)

        @pl.when(order_ref[j * SIDE + x] <= order_ref[y * SIDE + i])
        def _():
            scores = dot(kn_ref[j], qn_ref[i], NT)
            total_ref[i] += jnp.sum(jnp.exp2(scores * (ROOT * LOG2E)), axis=0, keepdims=True)

        return carry

    lax.fori_loop(0, SIDE * SIDE, tile, 0)


def grads_kernel(
    place_ref, order_ref, rates_ref, total_ref, qn_ref, kn_ref,
    qg0, qg1, qg2, qg3, kv0, kv1, kv2, kv3,
    own_ref, dq1_ref, dq2_ref, dq3_ref, dkv_ref,
    dq_acc, dk_acc, dv_acc, g_all, v_all, log_all, delta_all,
):
    y = place_ref[0]
    x = place_ref[1]
    for d, (qg, kv) in enumerate(zip((qg0, qg1, qg2, qg3), (kv0, kv1, kv2, kv3))):
        xs = lax.rem(x - d + SIDE, SIDE)
        ys = lax.rem(y - d + SIDE, SIDE)
        g_all[xs] = qg[ROWS:, :]
        v_all[ys] = kv[ROWS:, :]
        stats = rates_ref[y * SIDE + xs]
        delta_all[xs] = jnp.concatenate([stats[8 + i : 9 + i, :] for i in range(PIECES)], axis=1)
    log_all[...] = jnp.log2(total_ref[...])
    dq_acc[...] = jnp.zeros_like(dq_acc)

    def key_block(j, carry):
        dk_acc[...] = jnp.zeros_like(dk_acc)
        dv_acc[...] = jnp.zeros_like(dv_acc)

        def query_block(i, inner):
            @pl.when(order_ref[j * SIDE + x] <= order_ref[y * SIDE + i])
            def _():
                keys = kn_ref[j]
                queries = qn_ref[i]
                grad = g_all[i]
                scores = dot(keys, queries, NT)
                probs = jnp.exp2(scores * (ROOT * LOG2E) - log_all[i])
                dprobs = dot(v_all[j], grad, NT)
                dscores = (probs * (dprobs - delta_all[i])).astype(BF16)
                dv_acc[...] += dot(probs.astype(BF16), grad)
                dk_acc[...] += dot(dscores, queries)
                dq_acc[i] += dot(dscores, keys, TN)

            return inner

        lax.fori_loop(0, SIDE, query_block, 0)
        dkv_ref[j, :ROWS, :] = (dk_acc[...] * ROOT).astype(BF16)
        dkv_ref[j, ROWS:, :] = dv_acc[...].astype(BF16)
        return carry

    lax.fori_loop(0, SIDE, key_block, 0)
    own_ref[...] = dq_acc[x] * ROOT
    for d, out_ref in enumerate((dq1_ref, dq2_ref, dq3_ref), 1):
        out_ref[...] = (dq_acc[lax.rem(x + d, SIDE)] * ROOT).astype(BF16)


def sums_kernel(
    own_ref, dq1_ref, dq2_ref, dq3_ref, dkv_ref, q_ref, k_ref, qgain_ref, kgain_ref,
    gq_ref, gk_ref, dv_ref, msg_ref,
):
    q_gain = qgain_ref[...].astype(F32)
    k_gain = kgain_ref[...].astype(F32)
    part = jnp.zeros((8, WIDTH), F32)
    line = lax.broadcasted_iota(jnp.int32, (8, WIDTH), 0)
    for i in range(PIECES):
        rows = pl.ds(i * WIDTH, WIDTH)
        later = pl.ds(ROWS + i * WIDTH, WIDTH)
        gq = own_ref[rows, :]
        for ref in (dq1_ref, dq2_ref, dq3_ref):
            gq = gq + ref[rows, :].astype(F32)
        gq = gq * q_gain
        gk = dkv_ref[0, rows, :].astype(F32)
        dv = dkv_ref[0, later, :].astype(F32)
        for j in range(1, SIDE):
            gk = gk + dkv_ref[j, rows, :].astype(F32)
            dv = dv + dkv_ref[j, later, :].astype(F32)
        gk = gk * k_gain
        gq_ref[rows, :] = gq
        gk_ref[rows, :] = gk
        dv_ref[rows, :] = dv.astype(BF16)
        part = jnp.where(line == i, row_sums(gq * q_ref[rows, :].astype(F32)), part)
        part = jnp.where(line == PIECES + i, row_sums(gk * k_ref[rows, :].astype(F32)), part)
    msg_ref[...] = jnp.broadcast_to(part[None], msg_ref.shape)


def final_kernel(sums_ref, own_ref, gq_ref, gk_ref, q_ref, k_ref, dq_ref, dk_ref):
    inner = jnp.sum(sums_ref[...], axis=0)
    rate = own_ref[...]
    weight = rate * rate * rate * inner / (32 * WIDTH)
    for first, g_ref, raw_ref, out_ref in ((0, gq_ref, q_ref, dq_ref), (PIECES, gk_ref, k_ref, dk_ref)):
        for i in range(PIECES):
            rows = pl.ds(i * WIDTH, WIDTH)
            line = slice(first + i, first + i + 1)
            raw = raw_ref[rows, :].astype(F32)
            out = column(rate[line, :]) * g_ref[rows, :] - raw * column(weight[line, :])
            out_ref[rows, :] = out.astype(BF16)


def local(q_raw, k_raw, values, out, d_out, q_gain, k_gain, order):
    block = struct((ROWS, WIDTH), BF16)
    wide = struct((ROWS, WIDTH), F32)
    pair = struct((2 * ROWS, WIDTH), BF16)
    message = struct((32, 8, WIDTH), F32)
    place = jnp.stack([lax.axis_index("y"), lax.axis_index("x")]).astype(jnp.int32)
    q_gain = q_gain.reshape(1, WIDTH)
    k_gain = k_gain.reshape(1, WIDTH)

    squares, delta, qg, kv = call(
        squares_kernel, (message, struct((8, WIDTH), F32), pair, pair)
    )(q_raw, k_raw, values, out, d_out)
    squares = lax.all_to_all(squares, HEAD, 0, 0)
    qgs = [qg] + [shift(qg, "x", d) for d in range(1, SIDE)]
    kvs = [kv] + [shift(kv, "y", d) for d in range(1, SIDE)]
    rates, own_rate = call(
        rates_kernel, (struct((16, 16, WIDTH), F32), struct((8, WIDTH), F32))
    )(squares, delta)
    rates = lax.all_to_all(rates, SEQ, 0, 0)

    blocks = struct((SIDE, ROWS, WIDTH), BF16)
    totals, qn, kn = call(
        totals_kernel, (struct((SIDE, 1, ROWS), F32), blocks, blocks), smem=2
    )(place, order, rates, q_gain, k_gain, *qgs, *kvs)
    totals = lax.psum(totals, "x")

    own, dq1, dq2, dq3, dkv = call(
        grads_kernel,
        (wide, block, block, block, struct((SIDE, 2 * ROWS, WIDTH), BF16)),
        scratch=(
            pltpu.VMEM((SIDE, ROWS, WIDTH), F32),
            pltpu.VMEM((ROWS, WIDTH), F32),
            pltpu.VMEM((ROWS, WIDTH), F32),
            pltpu.VMEM((SIDE, ROWS, WIDTH), BF16),
            pltpu.VMEM((SIDE, ROWS, WIDTH), BF16),
            pltpu.VMEM((SIDE, 1, ROWS), F32),
            pltpu.VMEM((SIDE, 1, ROWS), F32),
        ),
        smem=2,
    )(place, order, rates, totals, qn, kn, *qgs, *kvs)
    dkv = lax.all_to_all(dkv, "y", 0, 0)
    dq1, dq2, dq3 = (shift(part, "x", d) for d, part in enumerate((dq1, dq2, dq3), 1))

    gq, gk, dv, inner = call(sums_kernel, (wide, wide, block, message))(
        own, dq1, dq2, dq3, dkv, q_raw, k_raw, q_gain, k_gain
    )
    inner = lax.all_to_all(inner, HEAD, 0, 0)
    d_q, d_k = call(final_kernel, (block, block))(inner, own_rate, gq, gk, q_raw, k_raw)
    return d_q, d_k, dv


def solution(mesh):
    fine = Mesh(mesh.devices.reshape(SIDE, SIDE, 16, 2), ("y", "x", "z", "c"))
    both = P(SEQ, HEAD)
    return jax.shard_map(
        local,
        mesh=fine,
        in_specs=(both,) * 5 + (P(HEAD), P(HEAD), P()),
        out_specs=(both,) * 3,
        check_vma=False,
    )
```

time: 580 us -> 129 us (0.22)
  waiting for transfers between devices: 148 us -> 9.66 us
  starting transfers between devices: 185 us -> 52.9 us
  blocking collectives: 147 us -> 40.2 us
  loops' own time: 39.1 us -> 0 us
  matrix products: 26.4 us -> 0 us
  other arithmetic: 22.5 us -> 0.08 us
  Pallas kernels: 0 us -> 18.1 us
    ppermute x77 -> x9, starting transfers between devices: 185 us -> 27.2 us  [shift(): lax.ppermute(value, axis, [(i, (i + steps) % count) for i in range(count)])]
    ppermute x77 -> x9, waiting for transfers between devices: 148 us -> 5.57 us  [shift(): lax.ppermute(value, axis, [(i, (i + steps) % count) for i in range(count)])]
    psum x2 -> x1, blocking collectives: 147 us -> 6.12 us  [local(): totals = lax.psum(totals, 'x')]
    another operation x2 -> x0, loops' own time: 39.1 us -> none  [the longest x1 20.4 us: local(): lax.fori_loop(0, cycle_size - 1, key_turn, (k_norm, values, zeros_block,...]
    all_to_all x0 -> x1, blocking collectives: none -> 34.1 us  [local(): inner = lax.all_to_all(inner, HEAD, 0, 0)]
    dot_general x96 -> x0, matrix products: 26.4 us -> none  [the longest x32 8.85 us: compute(): jnp.dot(queries, keys.T, preferred_element_type=jnp.float32)]
    all_to_all x0 -> x3, starting transfers between devices: none -> 25.6 us  [the longest x1 16.7 us: local(): squares = lax.all_to_all(squares, HEAD, 0, 0)]
    reduce_sum x35 -> x0, other arithmetic: 20.4 us -> none  [the longest x31 20.1 us: lookup(): jnp.sum(jnp.where(jnp.arange(table.shape[0], dtype=jnp.int32) == index, t...]
  transfers between devices with their start and end apart: 77 -> 12, of which waited for: 45 -> 4; matrix products, arithmetic and copies ran while one was open for 8% -> 0% of each run, Pallas kernels for 0% -> 1%
where the time goes in v1:
time: 129 us; the launch traced here: 127 us
  starting transfers between devices  52.9 us (41%)
  blocking collectives  40.2 us (31%)
  Pallas kernels  18.1 us (14%)
  waiting for transfers between devices  9.66 us (7%)
  local copies, waits for them, and re-layouts  5.15 us (4%)
    all_to_all x1, blocking collectives, local(): inner = lax.all_to_all(inner, HEAD, 0, 0)  34.1 us
    ppermute x9, starting transfers between devices, shift(): lax.ppermute(value, axis, [(i, (i + steps) % count) for i in range(count)])  27.2 us
    pallas_call x6, Pallas kernels, run(): pl.pallas_call(kernel, out_shape=out_shape, in_specs=specs, out_specs=jax...  18.1 us
    all_to_all x1, starting transfers between devices, local(): squares = lax.all_to_all(squares, HEAD, 0, 0)  16.7 us
    psum x1, blocking collectives, local(): totals = lax.psum(totals, 'x')  6.12 us
    ppermute x9, waiting for transfers between devices, shift(): lax.ppermute(value, axis, [(i, (i + steps) % count) for i in range(count)])  5.57 us
    all_to_all x1, starting transfers between devices, local(): rates = lax.all_to_all(rates, SEQ, 0, 0)  5.15 us
    unnamed x20, local copies, waits for them, and re-layouts  5.15 us
  transfers between devices with their start and end apart: 12, of which 4 were waited for; matrix products, arithmetic and copies ran while one was open for 0% of the time, Pallas kernels for 1%

profile of v1, /device:TPU:1, one launch (start us, length us, event | category | flops | bytes accessed | tf_op | source)
XLA Modules:
  0.0 126.9 jit_solution(5597099601198947906)
XLA Ops:
  0.6 0.0 copy-start
  0.6 0.9 copy-done
  1.5 0.0 copy-start.2
  1.5 0.9 copy-done.2
  2.4 0.0 copy-start.4
  2.4 0.9 copy-done.4
  3.3 0.0 copy-start.5
  3.3 0.9 copy-done.5
  4.2 0.0 copy-start.6
  4.2 0.9 copy-done.6
  5.1 0.9 shard_map.103
  6.0 16.7 %all-to-all-start = ((f32[32,8,128]{2,1,0:T(8,128)}), f32[32,8,128]{2,1,0:T(8,128)S(1)}, u32[]{:S(2)}, u32[]{:S(2)}) async-start(f32[32,8,128]{2,1,0:T(8,128)} %get-tuple-element.23), calls=%async_computation | async-start | bytes 262144 | tf_op jit(solution)/shard_map/all_to_all | solution.py:234
  22.7 4.4 %collective-permute-start.2 = (bf16[768,128]{1,0:T(8,128)(2,1)S(1)}, bf16[768,128]{1,0:T(8,128)(2,1)S(1)}, u32[]{:S(2)}, u32[]{:S(2)}) collective-permute-start(bf16[768,128]{1,0:T(8,128)(2,1)S(1)} %get-tuple-element.26.qg0), channel_id=1, source_target_pairs={{0,96},{32,0},{64,32},{96,64},{1,97},{33,1},{65,33},{97,65},{2,98}... | collective-permute-start | bytes 589832 | tf_op jit(solution)/shard_map/ppermute | solution.py:25
  27.1 2.4 %collective-permute-start.1 = (bf16[768,128]{1,0:T(8,128)(2,1)S(1)}, bf16[768,128]{1,0:T(8,128)(2,1)S(1)}, u32[]{:S(2)}, u32[]{:S(2)}) collective-permute-start(bf16[768,128]{1,0:T(8,128)(2,1)S(1)} %get-tuple-element.26.qg0), channel_id=1, source_target_pairs={{0,64},{32,96},{64,0},{96,32},{1,65},{33,97},{65,1},{97,33},{2,66}... | collective-permute-start | bytes 589832 | tf_op jit(solution)/shard_map/ppermute | solution.py:25
  29.6 2.5 %collective-permute-start = (bf16[768,128]{1,0:T(8,128)(2,1)S(1)}, bf16[768,128]{1,0:T(8,128)(2,1)S(1)}, u32[]{:S(2)}, u32[]{:S(2)}) collective-permute-start(bf16[768,128]{1,0:T(8,128)(2,1)S(1)} %get-tuple-element.26.qg0), channel_id=1, source_target_pairs={{0,32},{32,64},{64,96},{96,0},{1,33},{33,65},{65,97},{97,1},{2,34}... | collective-permute-start | bytes 589832 | tf_op jit(solution)/shard_map/ppermute | solution.py:25
  32.1 4.6 %collective-permute-start.5 = (bf16[768,128]{1,0:T(8,128)(2,1)S(1)}, bf16[768,128]{1,0:T(8,128)(2,1)S(1)}, u32[]{:S(2)}, u32[]{:S(2)}) collective-permute-start(bf16[768,128]{1,0:T(8,128)(2,1)S(1)} %get-tuple-element.27.kv0), channel_id=1, source_target_pairs={{0,384},{128,0},{256,128},{384,256},{1,385},{129,1},{257,129},{385... | collective-permute-start | bytes 589832 | tf_op jit(solution)/shard_map/ppermute | solution.py:25
  36.7 2.3 %collective-permute-start.4 = (bf16[768,128]{1,0:T(8,128)(2,1)S(1)}, bf16[768,128]{1,0:T(8,128)(2,1)S(1)}, u32[]{:S(2)}, u32[]{:S(2)}) collective-permute-start(bf16[768,128]{1,0:T(8,128)(2,1)S(1)} %get-tuple-element.27.kv0), channel_id=1, source_target_pairs={{0,256},{128,384},{256,0},{384,128},{1,257},{129,385},{257,1},{385... | collective-permute-start | bytes 589832 | tf_op jit(solution)/shard_map/ppermute | solution.py:25
  39.0 0.0 collective-permute-done.2.qg3
  39.0 2.6 %collective-permute-start.3 = (bf16[768,128]{1,0:T(8,128)(2,1)S(1)}, bf16[768,128]{1,0:T(8,128)(2,1)S(1)}, u32[]{:S(2)}, u32[]{:S(2)}) collective-permute-start(bf16[768,128]{1,0:T(8,128)(2,1)S(1)} %get-tuple-element.27.kv0), channel_id=1, source_target_pairs={{0,128},{128,256},{256,384},{384,0},{1,129},{129,257},{257,385},{3... | collective-permute-start | bytes 589832 | tf_op jit(solution)/shard_map/ppermute | solution.py:25
  41.6 0.0 all-to-all-done.sums_ref
  41.6 0.7 shard_map.104
  42.4 5.2 %all-to-all-start.1 = ((f32[16,16,128]{2,1,0:T(8,128)}), f32[16,16,128]{2,1,0:T(8,128)S(1)}, u32[]{:S(2)}, u32[]{:S(2)}) async-start(f32[16,16,128]{2,1,0:T(8,128)} %get-tuple-element.25), calls=%async_computation.1 | async-start | bytes 262144 | tf_op jit(solution)/shard_map/all_to_all | solution.py:240
  47.5 0.1 pad_add_fusion.place_ref
  47.6 0.0 collective-permute-done.1.qg2
  47.6 0.0 collective-permute-done.qg1
  47.6 0.0 collective-permute-done.5.kv3
  47.6 0.0 collective-permute-done.4.kv2
  47.6 2.7 %collective-permute-done.3.kv1 = bf16[768,128]{1,0:T(8,128)(2,1)S(1)} collective-permute-done((bf16[768,128]{1,0:T(8,128)(2,1)S(1)}, bf16[768,128]{1,0:T(8,128)(2,1)S(1)}, u32[]{:S(2)}, u32[]{:S(2)}) %collective-permute-start.3) | collective-permute-done | bytes 196640 | tf_op jit(solution)/shard_map/ppermute | solution.py:25
  50.3 4.1 %all-to-all-done.1.rates_ref = f32[16,16,128]{2,1,0:T(8,128)S(1)} async-done(((f32[16,16,128]{2,1,0:T(8,128)}), f32[16,16,128]{2,1,0:T(8,128)S(1)}, u32[]{:S(2)}, u32[]{:S(2)}) %all-to-all-start.1) | async-done | bytes 131104 | tf_op jit(solution)/shard_map/all_to_all | solution.py:240
  54.4 0.6 copy-done.7
  55.1 0.0 copy-done.8
  55.1 0.0 copy-done.9
  55.1 4.9 %shard_map.105 = (f32[4,1,384]{2,1,0:T(1,128)S(1)}, bf16[4,384,128]{2,1,0:T(8,128)(2,1)S(1)}, bf16[4,384,128]{2,1,0:T(8,128)(2,1)S(1)}) custom-call(s32[2]{0:T(128)S(1)} %pad_add_fusion.place_ref, s32[16]{0:T(128)S(1)} %copy-done.9, f32[16,16,128]{2,1,0:T(8,128)S(1)} %all-to-all-done.1.rates_ref, bf16[1,128]{1,0:T(2,128)(2,1)S(1)} %bitcast.4, ...), custom_call_target="tpu_custom_call" | custom-call | tf_op jit(solution)/shard_map/pallas_call | solution.py:38
  60.0 6.1 %psum.7.total_ref = f32[4,1,384]{2,1,0:T(1,128)S(1)} all-reduce(f32[4,1,384]{2,1,0:T(1,128)S(1)} %get-tuple-element.28), channel_id=1, replica_groups=mesh['y'=4,'x'=4,'z'=16,'c'=2] {'x'}, use_global_device_ids=true, to_apply=%region_0.0 | all-reduce | flops 1536 | bytes 12288 | tf_op jit(solution)/shard_map/psum | solution.py:246
  66.1 9.8 %shard_map.106 = (f32[384,128]{1,0:T(8,128)S(1)}, bf16[384,128]{1,0:T(8,128)(2,1)S(1)}, bf16[384,128]{1,0:T(8,128)(2,1)S(1)}, bf16[384,128]{1,0:T(8,128)(2,1)S(1)}, bf16[4,768,128]{2,1,0:T(8,128)(2,1)}) custom-call(s32[2]{0:T(128)S(1)} %pad_add_fusion.place_ref, s32[16]{0:T(128)S(1)} %copy-done.9, f32[16,16,128]{2,1,0:T(8,128)S(1)} %all-to-all-done.1.rates_ref, ...), custom_call_target="tpu_custom_call" | custom-call | tf_op jit(solution)/shard_map/pallas_call | solution.py:38
  76.0 3.7 %all-to-all-start.2 = ((bf16[4,768,128]{2,1,0:T(8,128)(2,1)}), bf16[4,768,128]{2,1,0:T(8,128)(2,1)S(1)}, u32[]{:S(2)}, u32[]{:S(2)}) async-start(bf16[4,768,128]{2,1,0:T(8,128)(2,1)} %get-tuple-element.35), calls=%async_computation.2 | async-start | bytes 1572864 | tf_op jit(solution)/shard_map/all_to_all | solution.py:262
  79.7 1.9 %collective-permute-start.6 = (bf16[384,128]{1,0:T(8,128)(2,1)S(1)}, bf16[384,128]{1,0:T(8,128)(2,1)S(1)}, u32[]{:S(2)}, u32[]{:S(2)}) collective-permute-start(bf16[384,128]{1,0:T(8,128)(2,1)S(1)} %get-tuple-element.32), channel_id=1, source_target_pairs={{0,32},{32,64},{64,96},{96,0},{1,33},{33,65},{65,97},{97,1},{2,34}... | collective-permute-start | bytes 294920 | tf_op jit(solution)/shard_map/ppermute | solution.py:25
  81.6 3.2 %collective-permute-start.7 = (bf16[384,128]{1,0:T(8,128)(2,1)S(1)}, bf16[384,128]{1,0:T(8,128)(2,1)S(1)}, u32[]{:S(2)}, u32[]{:S(2)}) collective-permute-start(bf16[384,128]{1,0:T(8,128)(2,1)S(1)} %get-tuple-element.33), channel_id=1, source_target_pairs={{0,64},{32,96},{64,0},{96,32},{1,65},{33,97},{65,1},{97,33},{2,66}... | collective-permute-start | bytes 294920 | tf_op jit(solution)/shard_map/ppermute | solution.py:25
  84.8 3.3 %collective-permute-start.8 = (bf16[384,128]{1,0:T(8,128)(2,1)S(1)}, bf16[384,128]{1,0:T(8,128)(2,1)S(1)}, u32[]{:S(2)}, u32[]{:S(2)}) collective-permute-start(bf16[384,128]{1,0:T(8,128)(2,1)S(1)} %get-tuple-element.34), channel_id=1, source_target_pairs={{0,96},{32,0},{64,32},{96,64},{1,97},{33,1},{65,33},{97,65},{2,98}... | collective-permute-start | bytes 294920 | tf_op jit(solution)/shard_map/ppermute | solution.py:25
  88.1 0.0 collective-permute-done.6.dq1_ref
  88.2 0.3 collective-permute-done.7.dq2_ref
  88.5 2.5 %collective-permute-done.8.dq3_ref = bf16[384,128]{1,0:T(8,128)(2,1)S(1)} collective-permute-done((bf16[384,128]{1,0:T(8,128)(2,1)S(1)}, bf16[384,128]{1,0:T(8,128)(2,1)S(1)}, u32[]{:S(2)}, u32[]{:S(2)}) %collective-permute-start.8) | collective-permute-done | bytes 98336 | tf_op jit(solution)/shard_map/ppermute | solution.py:25
  91.0 0.0 all-to-all-done.2.dkv_ref
  91.0 0.0 copy-done.1
  91.0 0.0 copy-done.3
  91.0 0.8 shard_map.107
  91.8 34.1 %all_to_all.20.sums_ref = f32[32,8,128]{2,1,0:T(8,128)S(1)} all-to-all(f32[32,8,128]{2,1,0:T(8,128)S(1)} %get-tuple-element.36), channel_id=1, replica_groups=mesh['y'=4,'x'=4,'z'=16,'c'=2] {'z','c'}, dimensions={0} | all-to-all | bytes 262144 | tf_op jit(solution)/shard_map/all_to_all | solution.py:268
  125.9 1.0 shard_map.108
  (5 shorter events, 0.0 us)
Async XLA Ops:
  0.6 0.9 copy-start
  1.5 0.9 copy-start.2
  2.4 0.9 copy-start.4
  3.3 0.9 copy-start.5
  4.2 0.9 copy-start.6
  6.0 35.6 %all-to-all-start = ((f32[32,8,128]{2,1,0:T(8,128)}), f32[32,8,128]{2,1,0:T(8,128)S(1)}, u32[]{:S(2)}, u32[]{:S(2)}) async-start(f32[32,8,128]{2,1,0:T(8,128)} %get-tuple-element.23), calls=%async_computation | async-start | bytes 262144 | tf_op jit(solution)/shard_map/all_to_all | solution.py:234
  22.7 16.3 %collective-permute-start.2 = (bf16[768,128]{1,0:T(8,128)(2,1)S(1)}, bf16[768,128]{1,0:T(8,128)(2,1)S(1)}, u32[]{:S(2)}, u32[]{:S(2)}) collective-permute-start(bf16[768,128]{1,0:T(8,128)(2,1)S(1)} %get-tuple-element.26.qg0), channel_id=1, source_target_pairs={{0,96},{32,0},{64,32},{96,64},{1,97},{33,1},{65,33},{97,65},{2,98}... | collective-permute-start | bytes 589832 | tf_op jit(solution)/shard_map/ppermute | solution.py:25
  27.1 20.5 %collective-permute-start.1 = (bf16[768,128]{1,0:T(8,128)(2,1)S(1)}, bf16[768,128]{1,0:T(8,128)(2,1)S(1)}, u32[]{:S(2)}, u32[]{:S(2)}) collective-permute-start(bf16[768,128]{1,0:T(8,128)(2,1)S(1)} %get-tuple-element.26.qg0), channel_id=1, source_target_pairs={{0,64},{32,96},{64,0},{96,32},{1,65},{33,97},{65,1},{97,33},{2,66}... | collective-permute-start | bytes 589832 | tf_op jit(solution)/shard_map/ppermute | solution.py:25
  29.6 18.0 %collective-permute-start = (bf16[768,128]{1,0:T(8,128)(2,1)S(1)}, bf16[768,128]{1,0:T(8,128)(2,1)S(1)}, u32[]{:S(2)}, u32[]{:S(2)}) collective-permute-start(bf16[768,128]{1,0:T(8,128)(2,1)S(1)} %get-tuple-element.26.qg0), channel_id=1, source_target_pairs={{0,32},{32,64},{64,96},{96,0},{1,33},{33,65},{65,97},{97,1},{2,34}... | collective-permute-start | bytes 589832 | tf_op jit(solution)/shard_map/ppermute | solution.py:25
  32.1 15.5 %collective-permute-start.5 = (bf16[768,128]{1,0:T(8,128)(2,1)S(1)}, bf16[768,128]{1,0:T(8,128)(2,1)S(1)}, u32[]{:S(2)}, u32[]{:S(2)}) collective-permute-start(bf16[768,128]{1,0:T(8,128)(2,1)S(1)} %get-tuple-element.27.kv0), channel_id=1, source_target_pairs={{0,384},{128,0},{256,128},{384,256},{1,385},{129,1},{257,129},{385... | collective-permute-start | bytes 589832 | tf_op jit(solution)/shard_map/ppermute | solution.py:25
  36.7 10.9 %collective-permute-start.4 = (bf16[768,128]{1,0:T(8,128)(2,1)S(1)}, bf16[768,128]{1,0:T(8,128)(2,1)S(1)}, u32[]{:S(2)}, u32[]{:S(2)}) collective-permute-start(bf16[768,128]{1,0:T(8,128)(2,1)S(1)} %get-tuple-element.27.kv0), channel_id=1, source_target_pairs={{0,256},{128,384},{256,0},{384,128},{1,257},{129,385},{257,1},{385... | collective-permute-start | bytes 589832 | tf_op jit(solution)/shard_map/ppermute | solution.py:25
  39.0 11.3 %collective-permute-start.3 = (bf16[768,128]{1,0:T(8,128)(2,1)S(1)}, bf16[768,128]{1,0:T(8,128)(2,1)S(1)}, u32[]{:S(2)}, u32[]{:S(2)}) collective-permute-start(bf16[768,128]{1,0:T(8,128)(2,1)S(1)} %get-tuple-element.27.kv0), channel_id=1, source_target_pairs={{0,128},{128,256},{256,384},{384,0},{1,129},{129,257},{257,385},{3... | collective-permute-start | bytes 589832 | tf_op jit(solution)/shard_map/ppermute | solution.py:25
  42.4 12.1 %all-to-all-start.1 = ((f32[16,16,128]{2,1,0:T(8,128)}), f32[16,16,128]{2,1,0:T(8,128)S(1)}, u32[]{:S(2)}, u32[]{:S(2)}) async-start(f32[16,16,128]{2,1,0:T(8,128)} %get-tuple-element.25), calls=%async_computation.1 | async-start | bytes 262144 | tf_op jit(solution)/shard_map/all_to_all | solution.py:240
  54.4 0.7 copy-start.7
  54.4 0.7 copy-start.8
  54.4 0.7 copy-start.9
  76.0 15.0 %copy-start.1 = (bf16[384,128]{1,0:T(8,128)(2,1)S(1)}, bf16[384,128]{1,0:T(8,128)(2,1)}, u32[]{:S(2)}) copy-start(bf16[384,128]{1,0:T(8,128)(2,1)} %q_ref.5) | copy-start | bytes 294916
  76.0 15.0 %copy-start.3 = (bf16[384,128]{1,0:T(8,128)(2,1)S(1)}, bf16[384,128]{1,0:T(8,128)(2,1)}, u32[]{:S(2)}) copy-start(bf16[384,128]{1,0:T(8,128)(2,1)} %k_ref.5) | copy-start | bytes 294916
  76.0 15.0 %all-to-all-start.2 = ((bf16[4,768,128]{2,1,0:T(8,128)(2,1)}), bf16[4,768,128]{2,1,0:T(8,128)(2,1)S(1)}, u32[]{:S(2)}, u32[]{:S(2)}) async-start(bf16[4,768,128]{2,1,0:T(8,128)(2,1)} %get-tuple-element.35), calls=%async_computation.2 | async-start | bytes 1572864 | tf_op jit(solution)/shard_map/all_to_all | solution.py:262
  79.7 8.4 %collective-permute-start.6 = (bf16[384,128]{1,0:T(8,128)(2,1)S(1)}, bf16[384,128]{1,0:T(8,128)(2,1)S(1)}, u32[]{:S(2)}, u32[]{:S(2)}) collective-permute-start(bf16[384,128]{1,0:T(8,128)(2,1)S(1)} %get-tuple-element.32), channel_id=1, source_target_pairs={{0,32},{32,64},{64,96},{96,0},{1,33},{33,65},{65,97},{97,1},{2,34}... | collective-permute-start | bytes 294920 | tf_op jit(solution)/shard_map/ppermute | solution.py:25
  81.6 6.9 %collective-permute-start.7 = (bf16[384,128]{1,0:T(8,128)(2,1)S(1)}, bf16[384,128]{1,0:T(8,128)(2,1)S(1)}, u32[]{:S(2)}, u32[]{:S(2)}) collective-permute-start(bf16[384,128]{1,0:T(8,128)(2,1)S(1)} %get-tuple-element.33), channel_id=1, source_target_pairs={{0,64},{32,96},{64,0},{96,32},{1,65},{33,97},{65,1},{97,33},{2,66}... | collective-permute-start | bytes 294920 | tf_op jit(solution)/shard_map/ppermute | solution.py:25
  84.8 6.2 %collective-permute-start.8 = (bf16[384,128]{1,0:T(8,128)(2,1)S(1)}, bf16[384,128]{1,0:T(8,128)(2,1)S(1)}, u32[]{:S(2)}, u32[]{:S(2)}) collective-permute-start(bf16[384,128]{1,0:T(8,128)(2,1)S(1)} %get-tuple-element.34), channel_id=1, source_target_pairs={{0,96},{32,0},{64,32},{96,64},{1,97},{33,1},{65,33},{97,65},{2,98}... | collective-permute-start | bytes 294920 | tf_op jit(solution)/shard_map/ppermute | solution.py:25

commit v2 on v1

v2 whole, which is shorter than its diff:
```python
import math

import jax
import jax.numpy as jnp
from jax import lax
from jax.experimental import pallas as pl
from jax.experimental.pallas import tpu as pltpu
from jax.sharding import Mesh, PartitionSpec as P

EPSILON = 1e-06
SIDE = 4
ROWS = 384
WIDTH = 128
PIECES = ROWS // WIDTH
HEAD = ("z", "c")
SEQ = ("y", "x")
F32 = jnp.float32
BF16 = jnp.bfloat16
ROOT = WIDTH ** (-0.5)
LOG2E = math.log2(math.e)


def swap(value, axis, mask):
    return lax.ppermute(value, axis, [(i, i ^ mask) for i in range(SIDE)])


def struct(shape, dtype):
    return jax.ShapeDtypeStruct(shape, dtype)


def call(kernel, out_shape, scratch=(), spaces=None, limit=32):
    def run(*args):
        places = {"s": pltpu.SMEM, "a": pl.ANY, "v": pltpu.VMEM}
        specs = [
            pl.BlockSpec(memory_space=places[letter])
            for letter in (spaces or "").ljust(len(args), "v")
        ]
        return pl.pallas_call(
            kernel,
            out_shape=out_shape,
            in_specs=specs,
            out_specs=jax.tree.map(lambda _: pl.BlockSpec(memory_space=pltpu.VMEM), out_shape),
            scratch_shapes=scratch,
            compiler_params=pltpu.CompilerParams(vmem_limit_bytes=limit * 2**20),
        )(*args)

    return run


def column(row):
    return jnp.broadcast_to(row, (WIDTH, WIDTH)).T


def row_sums(block):
    return jnp.sum(block.T, axis=0, keepdims=True)


def dot(a, b, dims=(((1,), (0,)), ((), ()))):
    return lax.dot_general(a, b, dims, preferred_element_type=F32)


NT = (((1,), (1,)), ((), ()))
TN = (((0,), (0,)), ((), ()))


def squares_kernel(q_ref, k_ref, v_ref, g_ref, msg_ref, qg_ref, kv_ref, sems):
    first, second = pl.ds(0, ROWS), pl.ds(ROWS, ROWS)
    copies = [
        pltpu.make_async_copy(source, target, sems.at[i])
        for i, (source, target) in enumerate((
            (q_ref, qg_ref.at[first, :]),
            (k_ref, kv_ref.at[first, :]),
            (g_ref, qg_ref.at[second, :]),
            (v_ref, kv_ref.at[second, :]),
        ))
    ]
    for copy in copies:
        copy.start()
    parts = []
    for copy, ref in zip(copies[:2], (qg_ref, kv_ref)):
        copy.wait()
        for i in range(PIECES):
            block = ref[pl.ds(i * WIDTH, WIDTH), :].astype(F32)
            parts.append(row_sums(block * block))
    part = jnp.concatenate(parts, axis=1)
    for h in range(32):
        msg_ref[h] = part
    for copy in copies[2:]:
        copy.wait()


def delta_kernel(out_ref, qg_ref, qgain_ref, kgain_ref, delta_ref, qscale_ref, kscale_ref):
    delta = jnp.zeros((8, WIDTH), F32)
    line = lax.broadcasted_iota(jnp.int32, (8, WIDTH), 0)
    for i in range(PIECES):
        o = out_ref[pl.ds(i * WIDTH, WIDTH), :].astype(F32)
        g = qg_ref[pl.ds(ROWS + i * WIDTH, WIDTH), :].astype(F32)
        delta = jnp.where(line == i, row_sums(g * o), delta)
    delta_ref[...] = delta
    qscale_ref[...] = qgain_ref[...].astype(F32)
    kscale_ref[...] = kgain_ref[...].astype(F32)


def rates_kernel(sums_ref, delta_ref, msg_ref, own_ref):
    total = sums_ref[0]
    for h in range(1, 32):
        total = total + sums_ref[h]
    rate = lax.rsqrt(total / (32 * WIDTH) + EPSILON)
    line = lax.broadcasted_iota(jnp.int32, (8, WIDTH), 0)
    lines = jnp.zeros((8, WIDTH), F32)
    for i in range(2 * PIECES):
        lines = jnp.where(line == i, rate[:, i * WIDTH : (i + 1) * WIDTH], lines)
    own_ref[...] = lines
    msg_ref[:, :8, :] = jnp.broadcast_to(lines[None], (16, 8, WIDTH))
    msg_ref[:, 8:, :] = jnp.broadcast_to(delta_ref[...][None], (16, 8, WIDTH))


def totals_kernel(
    place_ref, order_hbm, rates_ref, qgain_ref, kgain_ref,
    qg0, qg1, qg2, qg3, kv0, kv1, kv2, kv3,
    total_ref, qn_ref, kn_ref, order_ref, sem,
):
    fetch = pltpu.make_async_copy(order_hbm, order_ref, sem)
    fetch.start()
    y = place_ref[0]
    x = place_ref[1]
    q_gain = qgain_ref[...]
    k_gain = kgain_ref[...]
    for d, (qg, kv) in enumerate(zip((qg0, qg1, qg2, qg3), (kv0, kv1, kv2, kv3))):
        xs = x ^ d
        ys = y ^ d
        q_rate = rates_ref[y * SIDE + xs]
        k_rate = rates_ref[ys * SIDE + x]
        for i in range(PIECES):
            rows = pl.ds(i * WIDTH, WIDTH)
            q = qg[rows, :].astype(F32) * column(q_rate[i : i + 1, :]) * q_gain
            k = kv[rows, :].astype(F32) * column(k_rate[PIECES + i : PIECES + i + 1, :]) * k_gain
            qn_ref[xs, rows, :] = q.astype(BF16)
            kn_ref[ys, rows, :] = k.astype(BF16)
    total_ref[...] = jnp.zeros_like(total_ref)
    fetch.wait()

    def tile(t, carry):
        i = t // SIDE
        j = lax.rem(t, SIDE)

        @pl.when(order_ref[j * SIDE + x] <= order_ref[y * SIDE + i])
        def _():
            scores = dot(kn_ref[j], qn_ref[i], NT)
            total_ref[i] += jnp.sum(jnp.exp2(scores * (ROOT * LOG2E)), axis=0, keepdims=True)

        return carry

    lax.fori_loop(0, SIDE * SIDE, tile, 0)


def grads_kernel(
    place_ref, order_hbm, rates_ref, qgain_ref, kgain_ref, total_ref, qn_ref, kn_ref,
    qg0, qg1, qg2, qg3, kv0, kv1, kv2, kv3,
    msg_ref, dq0_ref, dq1_ref, dq2_ref, dq3_ref, dkv0_ref, dkv1_ref, dkv2_ref, dkv3_ref,
    dq_acc, dk_acc, dv_acc, g_all, v_all, log_all, delta_all, order_ref, sem,
):
    fetch = pltpu.make_async_copy(order_hbm, order_ref, sem)
    fetch.start()
    y = place_ref[0]
    x = place_ref[1]
    for d, (qg, kv) in enumerate(zip((qg0, qg1, qg2, qg3), (kv0, kv1, kv2, kv3))):
        xs = x ^ d
        ys = y ^ d
        g_all[xs] = qg[ROWS:, :]
        v_all[ys] = kv[ROWS:, :]
        stats = rates_ref[y * SIDE + xs]
        delta_all[xs] = jnp.concatenate([stats[8 + i : 9 + i, :] for i in range(PIECES)], axis=1)
    log_all[...] = jnp.log2(total_ref[...])
    dq_acc[...] = jnp.zeros_like(dq_acc)
    dk_acc[...] = jnp.zeros_like(dk_acc)
    dv_acc[...] = jnp.zeros_like(dv_acc)
    msg_ref[...] = jnp.zeros_like(msg_ref)
    fetch.wait()

    def tile(t, carry):
        i = t // SIDE
        j = lax.rem(t, SIDE)

        @pl.when(order_ref[j * SIDE + x] <= order_ref[y * SIDE + i])
        def _():
            keys = kn_ref[j]
            queries = qn_ref[i]
            grad = g_all[i]
            scores = dot(keys, queries, NT)
            probs = jnp.exp2(scores * (ROOT * LOG2E) - log_all[i])
            dprobs = dot(v_all[j], grad, NT)
            dscores = (probs * (dprobs - delta_all[i])).astype(BF16)
            dv_acc[j] += dot(probs.astype(BF16), grad)
            dk_acc[j] += dot(dscores, queries)
            dq_acc[i] += dot(dscores, keys, TN)

        return carry

    lax.fori_loop(0, SIDE * SIDE, tile, 0)
    q_gain = qgain_ref[...] * ROOT
    k_gain = kgain_ref[...] * ROOT
    q_parts = (dq0_ref, dq1_ref, dq2_ref, dq3_ref)
    k_parts = (dkv0_ref, dkv1_ref, dkv2_ref, dkv3_ref)
    line = lax.broadcasted_iota(jnp.int32, (8, WIDTH), 0)
    for d, (qg, kv) in enumerate(zip((qg0, qg1, qg2, qg3), (kv0, kv1, kv2, kv3))):
        xs = x ^ d
        ys = y ^ d
        q_lines = jnp.zeros((8, WIDTH), F32)
        k_lines = jnp.zeros((8, WIDTH), F32)
        for i in range(PIECES):
            rows = pl.ds(i * WIDTH, WIDTH)
            later = pl.ds(ROWS + i * WIDTH, WIDTH)
            gq = dq_acc[xs, rows, :] * q_gain
            gk = dk_acc[ys, rows, :] * k_gain
            q_lines = jnp.where(line == i, row_sums(gq * qg[rows, :].astype(F32)), q_lines)
            k_lines = jnp.where(line == PIECES + i, row_sums(gk * kv[rows, :].astype(F32)), k_lines)
            q_parts[d][rows, :] = gq.astype(q_parts[d].dtype)
            k_parts[d][rows, :] = gk.astype(k_parts[d].dtype)
            k_parts[d][later, :] = dv_acc[ys, rows, :].astype(k_parts[d].dtype)
        msg_ref[y * SIDE + xs] = q_lines
        msg_ref[ys * SIDE + x] = k_lines + jnp.where(d == 0, q_lines, jnp.zeros_like(q_lines))


def inner_kernel(place_ref, sums_ref, dq1_ref, dq2_ref, dq3_ref, msg_ref, out1_ref, out2_ref, out3_ref):
    y = place_ref[0]
    x = place_ref[1]
    own = sums_ref[y * SIDE + x]
    q_lines = own
    k_lines = own
    for d in range(1, SIDE):
        q_lines = q_lines + sums_ref[y * SIDE + (x ^ d)]
        k_lines = k_lines + sums_ref[(y ^ d) * SIDE + x]
    line = lax.broadcasted_iota(jnp.int32, (8, WIDTH), 0)
    total = jnp.where(line < PIECES, q_lines, k_lines).astype(BF16)
    msg_ref[...] = jnp.broadcast_to(total[None], msg_ref.shape)
    out1_ref[...] = dq1_ref[...]
    out2_ref[...] = dq2_ref[...]
    out3_ref[...] = dq3_ref[...]


def final_kernel(
    sums_ref, own_ref, qg_ref, kv_ref,
    dq0_ref, dq1_ref, dq2_ref, dq3_ref, dkv0_ref, dkv1_ref, dkv2_ref, dkv3_ref,
    dq_ref, dk_ref, dv_ref,
):
    inner = jnp.sum(sums_ref[...].astype(F32), axis=0)
    rate = own_ref[...]
    weight = rate * rate * rate * inner / (32 * WIDTH)

    def total(refs, rows):
        value = refs[0][rows, :]
        for ref in refs[1:]:
            value = value + ref[rows, :].astype(F32)
        return value

    q_parts = (dq0_ref, dq1_ref, dq2_ref, dq3_ref)
    k_parts = (dkv0_ref, dkv1_ref, dkv2_ref, dkv3_ref)
    for i in range(PIECES):
        rows = pl.ds(i * WIDTH, WIDTH)
        later = pl.ds(ROWS + i * WIDTH, WIDTH)
        for first, parts, raw_ref, out_ref in ((0, q_parts, qg_ref, dq_ref), (PIECES, k_parts, kv_ref, dk_ref)):
            line = slice(first + i, first + i + 1)
            raw = raw_ref[rows, :].astype(F32)
            out = column(rate[line, :]) * total(parts, rows) - raw * column(weight[line, :])
            out_ref[rows, :] = out.astype(BF16)
        dv_ref[rows, :] = total(k_parts, later).astype(BF16)


def local(q_raw, k_raw, values, out, d_out, q_gain, k_gain, order):
    block = struct((ROWS, WIDTH), BF16)
    pair = struct((2 * ROWS, WIDTH), BF16)
    lines = struct((8, WIDTH), F32)
    gain = struct((1, WIDTH), F32)
    place = jnp.stack([lax.axis_index("y"), lax.axis_index("x")]).astype(jnp.int32)

    squares, qg, kv = call(
        squares_kernel,
        (struct((32, 1, 2 * ROWS), F32), pair, pair),
        scratch=(pltpu.SemaphoreType.DMA((4,)),),
        spaces="aaaa",
    )(q_raw, k_raw, values, d_out)
    squares = lax.all_to_all(squares, HEAD, 0, 0)
    qgs = [qg] + [swap(qg, "x", d) for d in range(1, SIDE)]
    kvs = [kv] + [swap(kv, "y", d) for d in range(1, SIDE)]
    delta, q_scale, k_scale = call(delta_kernel, (lines, gain, gain))(
        out, qg, q_gain.reshape(1, WIDTH), k_gain.reshape(1, WIDTH)
    )
    rates, own_rate = call(rates_kernel, (struct((16, 16, WIDTH), F32), lines))(squares, delta)
    rates = lax.all_to_all(rates, SEQ, 0, 0)

    blocks = struct((SIDE, ROWS, WIDTH), BF16)
    known = (pltpu.SMEM((16,), jnp.int32), pltpu.SemaphoreType.DMA)
    totals, qn, kn = call(
        totals_kernel,
        (struct((SIDE, 1, ROWS), F32), blocks, blocks),
        scratch=known,
        spaces="sa",
    )(place, order, rates, q_scale, k_scale, *qgs, *kvs)
    totals = lax.psum(totals, "x")

    own = (struct((ROWS, WIDTH), F32), block, block, block)
    own_pair = (struct((2 * ROWS, WIDTH), F32), pair, pair, pair)
    inner, *parts = call(
        grads_kernel,
        (struct((16, 8, WIDTH), F32),) + own + own_pair,
        scratch=(
            pltpu.VMEM((SIDE, ROWS, WIDTH), F32),
            pltpu.VMEM((SIDE, ROWS, WIDTH), F32),
            pltpu.VMEM((SIDE, ROWS, WIDTH), F32),
            pltpu.VMEM((SIDE, ROWS, WIDTH), BF16),
            pltpu.VMEM((SIDE, ROWS, WIDTH), BF16),
            pltpu.VMEM((SIDE, 1, ROWS), F32),
            pltpu.VMEM((SIDE, 1, ROWS), F32),
        ) + known,
        spaces="sa",
    )(place, order, rates, q_scale, k_scale, totals, qn, kn, *qgs, *kvs)
    dqs, dkvs = parts[:SIDE], parts[SIDE:]
    inner = lax.all_to_all(inner, SEQ, 0, 0)
    dkvs[1:] = [swap(part, "y", d) for d, part in enumerate(dkvs[1:], 1)]
    inner, *dqs[1:] = call(
        inner_kernel, (struct((32, 8, WIDTH), BF16), block, block, block), spaces="s"
    )(place, inner, *dqs[1:])
    inner = lax.all_to_all(inner, HEAD, 0, 0)
    dqs[1:] = [swap(part, "x", d) for d, part in enumerate(dqs[1:], 1)]
    return call(final_kernel, (block, block, block))(inner, own_rate, qg, kv, *dqs, *dkvs)


def solution(mesh):
    fine = Mesh(mesh.devices.reshape(SIDE, SIDE, 16, 2), ("y", "x", "z", "c"))
    both = P(SEQ, HEAD)
    return jax.shard_map(
        local,
        mesh=fine,
        in_specs=(both,) * 5 + (P(HEAD), P(HEAD), P()),
        out_specs=(both,) * 3,
        check_vma=False,
    )
```

time: 129 us -> 133 us (1.031)
  starting transfers between devices: 52.9 us -> 79.5 us
  blocking collectives: 40.2 us -> 19.7 us
  Pallas kernels: 18.1 us -> 15.2 us
    all_to_all x1, blocking collectives: 34.1 us -> 12.6 us  [local(): inner = lax.all_to_all(inner, SEQ, 0, 0)]
    all_to_all x1, starting transfers between devices: 3.73 us -> 18.7 us  [local(): inner = lax.all_to_all(inner, HEAD, 0, 0)]
    ppermute x9 -> x12, starting transfers between devices: 27.2 us -> 37.2 us  [swap(): return lax.ppermute(value, axis, [(i, i ^ mask) for i in range(SIDE)])]
    pallas_call x6 -> x7, Pallas kernels: 18.1 us -> 15.2 us  [run(): pl.pallas_call(kernel, out_shape=out_shape, in_specs=specs, out_specs=jax...]
    all_to_all x1, waiting for transfers between devices: 4.08 us -> 6.79 us  [local(): rates = lax.all_to_all(rates, SEQ, 0, 0)]
    ppermute x9 -> x12, waiting for transfers between devices: 5.57 us -> 2.89 us  [swap(): return lax.ppermute(value, axis, [(i, i ^ mask) for i in range(SIDE)])]
    all_to_all x1, starting transfers between devices: 5.15 us -> 6.68 us  [local(): rates = lax.all_to_all(rates, SEQ, 0, 0)]
  transfers between devices with their start and end apart: 12 -> 15, of which waited for: 4 -> 2; matrix products, arithmetic and copies ran while one was open for 0% -> 0% of each run, Pallas kernels for 1% -> 1%
where the time goes in v2:
time: 133 us; the launch traced here: 131 us
  starting transfers between devices  79.5 us (60%)
  blocking collectives  19.7 us (15%)
  Pallas kernels  15.2 us (11%)
  waiting for transfers between devices  9.68 us (7%)
  local copies, waits for them, and re-layouts  5.54 us (4%)
    ppermute x12, starting transfers between devices, swap(): return lax.ppermute(value, axis, [(i, i ^ mask) for i in range(SIDE)])  37.2 us
    all_to_all x1, starting transfers between devices, local(): inner = lax.all_to_all(inner, HEAD, 0, 0)  18.7 us
    all_to_all x1, starting transfers between devices, local(): squares = lax.all_to_all(squares, HEAD, 0, 0)  16.9 us
    pallas_call x7, Pallas kernels, run(): pl.pallas_call(kernel, out_shape=out_shape, in_specs=specs, out_specs=jax...  15.2 us
    all_to_all x1, blocking collectives, local(): inner = lax.all_to_all(inner, SEQ, 0, 0)  12.6 us
    psum x1, blocking collectives, local(): totals = lax.psum(totals, 'x')  7.14 us
    all_to_all x1, waiting for transfers between devices, local(): rates = lax.all_to_all(rates, SEQ, 0, 0)  6.79 us
    all_to_all x1, starting transfers between devices, local(): rates = lax.all_to_all(rates, SEQ, 0, 0)  6.68 us
  transfers between devices with their start and end apart: 15, of which 2 were waited for; matrix products, arithmetic and copies ran while one was open for 0% of the time, Pallas kernels for 1%

profile of v2, /device:TPU:1, one launch (start us, length us, event | category | flops | bytes accessed | tf_op | source)
XLA Modules:
  0.0 130.6 jit_solution(1156890138972021439)
XLA Ops:
  0.6 0.9 copy-done
  1.5 0.9 copy-done.1
  2.4 0.9 copy-done.2
  3.3 0.9 copy-done.3
  4.2 1.5 %shard_map.103 = (f32[32,1,768]{2,1,0:T(1,128)}, bf16[768,128]{1,0:T(8,128)(2,1)S(1)}, bf16[768,128]{1,0:T(8,128)(2,1)S(1)}) custom-call(bf16[384,128]{1,0:T(8,128)(2,1)S(1)} %copy-done, bf16[384,128]{1,0:T(8,128)(2,1)S(1)} %copy-done.1, bf16[384,128]{1,0:T(8,128)(2,1)S(1)} %copy-done.2, bf16[384,128]{1,0:T(8,128)(2,1)S(1)} %copy-done.3), custom_call_target="tpu_custom_call" | custom-call | tf_op jit(solution)/shard_map/pallas_call | solution.py:38
  5.7 0.0 copy-start.4
  5.7 16.9 %all-to-all-start = ((f32[32,1,768]{2,1,0:T(1,128)}), f32[32,1,768]{2,1,0:T(1,128)S(1)}, u32[]{:S(2)}, u32[]{:S(2)}) async-start(f32[32,1,768]{2,1,0:T(1,128)} %get-tuple-element.27), calls=%async_computation | async-start | bytes 196608 | tf_op jit(solution)/shard_map/all_to_all | solution.py:283
  22.6 4.6 %collective-permute-start.5 = (bf16[768,128]{1,0:T(8,128)(2,1)S(1)}, bf16[768,128]{1,0:T(8,128)(2,1)S(1)}, u32[]{:S(2)}, u32[]{:S(2)}) collective-permute-start(bf16[768,128]{1,0:T(8,128)(2,1)S(1)} %get-tuple-element.33.kv0.kv_ref), channel_id=1, source_target_pairs={{0,384},{128,256},{256,128},{384,0},{1,385},{129,257},{257,129},{3... | collective-permute-start | bytes 589832 | tf_op jit(solution)/shard_map/ppermute | solution.py:24
  27.2 2.3 %collective-permute-start.4 = (bf16[768,128]{1,0:T(8,128)(2,1)S(1)}, bf16[768,128]{1,0:T(8,128)(2,1)S(1)}, u32[]{:S(2)}, u32[]{:S(2)}) collective-permute-start(bf16[768,128]{1,0:T(8,128)(2,1)S(1)} %get-tuple-element.33.kv0.kv_ref), channel_id=1, source_target_pairs={{0,256},{128,384},{256,0},{384,128},{1,257},{129,385},{257,1},{385... | collective-permute-start | bytes 589832 | tf_op jit(solution)/shard_map/ppermute | solution.py:24
  29.5 2.1 %collective-permute-start.3 = (bf16[768,128]{1,0:T(8,128)(2,1)S(1)}, bf16[768,128]{1,0:T(8,128)(2,1)S(1)}, u32[]{:S(2)}, u32[]{:S(2)}) collective-permute-start(bf16[768,128]{1,0:T(8,128)(2,1)S(1)} %get-tuple-element.33.kv0.kv_ref), channel_id=1, source_target_pairs={{0,128},{128,0},{256,384},{384,256},{1,129},{129,1},{257,385},{385... | collective-permute-start | bytes 589832 | tf_op jit(solution)/shard_map/ppermute | solution.py:24
  31.7 4.4 %collective-permute-start.2 = (bf16[768,128]{1,0:T(8,128)(2,1)S(1)}, bf16[768,128]{1,0:T(8,128)(2,1)S(1)}, u32[]{:S(2)}, u32[]{:S(2)}) collective-permute-start(bf16[768,128]{1,0:T(8,128)(2,1)S(1)} %get-tuple-element.28.qg_ref.qg0), channel_id=1, source_target_pairs={{0,96},{32,64},{64,32},{96,0},{1,97},{33,65},{65,33},{97,1},{2,98}... | collective-permute-start | bytes 589832 | tf_op jit(solution)/shard_map/ppermute | solution.py:24
  36.0 2.4 %collective-permute-start.1 = (bf16[768,128]{1,0:T(8,128)(2,1)S(1)}, bf16[768,128]{1,0:T(8,128)(2,1)S(1)}, u32[]{:S(2)}, u32[]{:S(2)}) collective-permute-start(bf16[768,128]{1,0:T(8,128)(2,1)S(1)} %get-tuple-element.28.qg_ref.qg0), channel_id=1, source_target_pairs={{0,64},{32,96},{64,0},{96,32},{1,65},{33,97},{65,1},{97,33},{2,66}... | collective-permute-start | bytes 589832 | tf_op jit(solution)/shard_map/ppermute | solution.py:24
  38.5 0.0 collective-permute-done.5.kv3
  38.5 2.2 %collective-permute-start = (bf16[768,128]{1,0:T(8,128)(2,1)S(1)}, bf16[768,128]{1,0:T(8,128)(2,1)S(1)}, u32[]{:S(2)}, u32[]{:S(2)}) collective-permute-start(bf16[768,128]{1,0:T(8,128)(2,1)S(1)} %get-tuple-element.28.qg_ref.qg0), channel_id=1, source_target_pairs={{0,32},{32,0},{64,96},{96,64},{1,33},{33,1},{65,97},{97,65},{2,34}... | collective-permute-start | bytes 589832 | tf_op jit(solution)/shard_map/ppermute | solution.py:24
  40.7 0.0 copy-start.6
  40.7 0.0 copy-start.7
  40.7 0.6 copy-done.6
  41.3 0.0 copy-done.7
  41.3 0.1 shard_map.104
  41.5 0.0 all-to-all-done.sums_ref
  41.5 0.7 shard_map.105
  42.2 6.7 %all-to-all-start.1 = ((f32[16,16,128]{2,1,0:T(8,128)}), f32[16,16,128]{2,1,0:T(8,128)S(1)}, u32[]{:S(2)}, u32[]{:S(2)}) async-start(f32[16,16,128]{2,1,0:T(8,128)} %get-tuple-element.30), calls=%async_computation.1 | async-start | bytes 262144 | tf_op jit(solution)/shard_map/all_to_all | solution.py:290
  48.9 0.1 pad_add_fusion.place_ref
  49.0 0.0 collective-permute-done.4.kv2
  49.0 0.0 collective-permute-done.3.kv1
  49.0 0.0 collective-permute-done.2.qg3
  49.0 0.0 collective-permute-done.1.qg2
  49.0 0.0 collective-permute-done.qg1
  49.0 6.8 %all-to-all-done.1.rates_ref = f32[16,16,128]{2,1,0:T(8,128)S(1)} async-done(((f32[16,16,128]{2,1,0:T(8,128)}), f32[16,16,128]{2,1,0:T(8,128)S(1)}, u32[]{:S(2)}, u32[]{:S(2)}) %all-to-all-start.1) | async-done | bytes 131104 | tf_op jit(solution)/shard_map/all_to_all | solution.py:290
  55.8 0.7 copy-done.5
  56.4 4.0 %shard_map.106 = (f32[4,1,384]{2,1,0:T(1,128)S(1)}, bf16[4,384,128]{2,1,0:T(8,128)(2,1)S(1)}, bf16[4,384,128]{2,1,0:T(8,128)(2,1)S(1)}) custom-call(s32[2]{0:T(128)S(1)} %pad_add_fusion.place_ref, s32[16]{0:T(128)S(1)} %copy-done.5, f32[16,16,128]{2,1,0:T(8,128)S(1)} %all-to-all-done.1.rates_ref, f32[1,128]{1,0:T(1,128)S(1)} %get-tuple-element.31.qgain_ref, ...), custom_call_target="tpu_custom_call" | custom-call | tf_op jit(solution)/shard_map/pallas_call | solution.py:38
  60.4 7.1 %psum.7.total_ref = f32[4,1,384]{2,1,0:T(1,128)S(1)} all-reduce(f32[4,1,384]{2,1,0:T(1,128)S(1)} %get-tuple-element.34), channel_id=1, replica_groups=mesh['y'=4,'x'=4,'z'=16,'c'=2] {'x'}, use_global_device_ids=true, to_apply=%region_0.0 | all-reduce | flops 1536 | bytes 12288 | tf_op jit(solution)/shard_map/psum | solution.py:300
  67.6 6.7 %shard_map.107 = (f32[16,8,128]{2,1,0:T(8,128)S(1)}, f32[384,128]{1,0:T(8,128)S(1)}, bf16[384,128]{1,0:T(8,128)(2,1)S(1)}, bf16[384,128]{1,0:T(8,128)(2,1)S(1)},...) custom-call(s32[2]{0:T(128)S(1)} %pad_add_fusion.place_ref, ...), custom_call_target="tpu_custom_call" | custom-call | tf_op jit(solution)/shard_map/pallas_call | solution.py:38
  74.3 0.7 copy-done.8
  75.0 12.6 %all_to_all.20.sums_ref = f32[16,8,128]{2,1,0:T(8,128)S(1)} all-to-all(f32[16,8,128]{2,1,0:T(8,128)S(1)} %get-tuple-element.37), channel_id=1, replica_groups=mesh['y'=4,'x'=4,'z'=16,'c'=2] {'y','x'}, dimensions={0} | all-to-all | bytes 131072 | tf_op jit(solution)/shard_map/all_to_all | solution.py:319
  87.6 1.2 shard_map.108
  88.8 18.7 %all-to-all-start.3 = ((bf16[32,8,128]{2,1,0:T(8,128)(2,1)}), bf16[32,8,128]{2,1,0:T(8,128)(2,1)S(1)}, u32[]{:S(2)}, u32[]{:S(2)}) async-start(bf16[32,8,128]{2,1,0:T(8,128)(2,1)} %get-tuple-element.41), calls=%async_computation.3 | async-start | bytes 131072 | tf_op jit(solution)/shard_map/all_to_all | solution.py:324
  107.5 2.2 %collective-permute-start.6 = (bf16[384,128]{1,0:T(8,128)(2,1)S(1)}, bf16[384,128]{1,0:T(8,128)(2,1)S(1)}, u32[]{:S(2)}, u32[]{:S(2)}) collective-permute-start(bf16[384,128]{1,0:T(8,128)(2,1)S(1)} %get-tuple-element.44), channel_id=1, source_target_pairs={{0,32},{32,0},{64,96},{96,64},{1,33},{33,1},{65,97},{97,65},{2,34}... | collective-permute-start | bytes 294920 | tf_op jit(solution)/shard_map/ppermute | solution.py:24
  109.7 2.2 %collective-permute-start.9 = (bf16[768,128]{1,0:T(8,128)(2,1)S(1)}, bf16[768,128]{1,0:T(8,128)(2,1)S(1)}, u32[]{:S(2)}, u32[]{:S(2)}) collective-permute-start(bf16[768,128]{1,0:T(8,128)(2,1)S(1)} %copy-done.9), channel_id=1, source_target_pairs={{0,128},{128,0},{256,384},{384,256},{1,129},{129,1},{257,385},{385... | collective-permute-start | bytes 589832 | tf_op jit(solution)/shard_map/ppermute | solution.py:24
  111.9 3.7 %collective-permute-start.10 = (bf16[768,128]{1,0:T(8,128)(2,1)S(1)}, bf16[768,128]{1,0:T(8,128)(2,1)S(1)}, u32[]{:S(2)}, u32[]{:S(2)}) collective-permute-start(bf16[768,128]{1,0:T(8,128)(2,1)S(1)} %get-tuple-element.49), channel_id=1, source_target_pairs={{0,256},{128,384},{256,0},{384,128},{1,257},{129,385},{257,1},{385... | collective-permute-start | bytes 589832 | tf_op jit(solution)/shard_map/ppermute | solution.py:24
  115.6 3.7 %collective-permute-start.11 = (bf16[768,128]{1,0:T(8,128)(2,1)S(1)}, bf16[768,128]{1,0:T(8,128)(2,1)S(1)}, u32[]{:S(2)}, u32[]{:S(2)}) collective-permute-start(bf16[768,128]{1,0:T(8,128)(2,1)S(1)} %get-tuple-element.50), channel_id=1, source_target_pairs={{0,384},{128,256},{256,128},{384,0},{1,385},{129,257},{257,129},{3... | collective-permute-start | bytes 589832 | tf_op jit(solution)/shard_map/ppermute | solution.py:24
  119.3 3.7 %collective-permute-start.7 = (bf16[384,128]{1,0:T(8,128)(2,1)S(1)}, bf16[384,128]{1,0:T(8,128)(2,1)S(1)}, u32[]{:S(2)}, u32[]{:S(2)}) collective-permute-start(bf16[384,128]{1,0:T(8,128)(2,1)S(1)} %get-tuple-element.45), channel_id=1, source_target_pairs={{0,64},{32,96},{64,0},{96,32},{1,65},{33,97},{65,1},{97,33},{2,66}... | collective-permute-start | bytes 294920 | tf_op jit(solution)/shard_map/ppermute | solution.py:24
  123.0 0.0 collective-permute-done.6.dq1_ref
  123.0 3.7 %collective-permute-start.8 = (bf16[384,128]{1,0:T(8,128)(2,1)S(1)}, bf16[384,128]{1,0:T(8,128)(2,1)S(1)}, u32[]{:S(2)}, u32[]{:S(2)}) collective-permute-start(bf16[384,128]{1,0:T(8,128)(2,1)S(1)} %get-tuple-element.46), channel_id=1, source_target_pairs={{0,96},{32,64},{64,32},{96,0},{1,97},{33,65},{65,33},{97,1},{2,98}... | collective-permute-start | bytes 294920 | tf_op jit(solution)/shard_map/ppermute | solution.py:24
  126.7 0.0 collective-permute-done.7.dq2_ref
  126.8 2.9 %collective-permute-done.8.dq3_ref = bf16[384,128]{1,0:T(8,128)(2,1)S(1)} collective-permute-done((bf16[384,128]{1,0:T(8,128)(2,1)S(1)}, bf16[384,128]{1,0:T(8,128)(2,1)S(1)}, u32[]{:S(2)}, u32[]{:S(2)}) %collective-permute-start.8) | collective-permute-done | bytes 98336 | tf_op jit(solution)/shard_map/ppermute | solution.py:24
  129.6 0.0 all-to-all-done.3.sums_ref
  129.6 1.0 shard_map.109
  (12 shorter events, 0.0 us)
Async XLA Ops:
  0.6 0.9 copy-start
  1.5 0.9 copy-start.1
  2.4 0.9 copy-start.2
  3.3 0.9 copy-start.3
  5.7 35.0 %copy-start.4 = (bf16[384,128]{1,0:T(8,128)(2,1)S(1)}, bf16[384,128]{1,0:T(8,128)(2,1)}, u32[]{:S(2)}) copy-start(bf16[384,128]{1,0:T(8,128)(2,1)} %out_ref.1) | copy-start | bytes 294916
  5.7 35.8 %all-to-all-start = ((f32[32,1,768]{2,1,0:T(1,128)}), f32[32,1,768]{2,1,0:T(1,128)S(1)}, u32[]{:S(2)}, u32[]{:S(2)}) async-start(f32[32,1,768]{2,1,0:T(1,128)} %get-tuple-element.27), calls=%async_computation | async-start | bytes 196608 | tf_op jit(solution)/shard_map/all_to_all | solution.py:283
  22.6 15.9 %collective-permute-start.5 = (bf16[768,128]{1,0:T(8,128)(2,1)S(1)}, bf16[768,128]{1,0:T(8,128)(2,1)S(1)}, u32[]{:S(2)}, u32[]{:S(2)}) collective-permute-start(bf16[768,128]{1,0:T(8,128)(2,1)S(1)} %get-tuple-element.33.kv0.kv_ref), channel_id=1, source_target_pairs={{0,384},{128,256},{256,128},{384,0},{1,385},{129,257},{257,129},{3... | collective-permute-start | bytes 589832 | tf_op jit(solution)/shard_map/ppermute | solution.py:24
  27.2 21.7 %collective-permute-start.4 = (bf16[768,128]{1,0:T(8,128)(2,1)S(1)}, bf16[768,128]{1,0:T(8,128)(2,1)S(1)}, u32[]{:S(2)}, u32[]{:S(2)}) collective-permute-start(bf16[768,128]{1,0:T(8,128)(2,1)S(1)} %get-tuple-element.33.kv0.kv_ref), channel_id=1, source_target_pairs={{0,256},{128,384},{256,0},{384,128},{1,257},{129,385},{257,1},{385... | collective-permute-start | bytes 589832 | tf_op jit(solution)/shard_map/ppermute | solution.py:24
  29.5 19.5 %collective-permute-start.3 = (bf16[768,128]{1,0:T(8,128)(2,1)S(1)}, bf16[768,128]{1,0:T(8,128)(2,1)S(1)}, u32[]{:S(2)}, u32[]{:S(2)}) collective-permute-start(bf16[768,128]{1,0:T(8,128)(2,1)S(1)} %get-tuple-element.33.kv0.kv_ref), channel_id=1, source_target_pairs={{0,128},{128,0},{256,384},{384,256},{1,129},{129,1},{257,385},{385... | collective-permute-start | bytes 589832 | tf_op jit(solution)/shard_map/ppermute | solution.py:24
  31.7 17.3 %collective-permute-start.2 = (bf16[768,128]{1,0:T(8,128)(2,1)S(1)}, bf16[768,128]{1,0:T(8,128)(2,1)S(1)}, u32[]{:S(2)}, u32[]{:S(2)}) collective-permute-start(bf16[768,128]{1,0:T(8,128)(2,1)S(1)} %get-tuple-element.28.qg_ref.qg0), channel_id=1, source_target_pairs={{0,96},{32,64},{64,32},{96,0},{1,97},{33,65},{65,33},{97,1},{2,98}... | collective-permute-start | bytes 589832 | tf_op jit(solution)/shard_map/ppermute | solution.py:24
  36.0 12.9 %collective-permute-start.1 = (bf16[768,128]{1,0:T(8,128)(2,1)S(1)}, bf16[768,128]{1,0:T(8,128)(2,1)S(1)}, u32[]{:S(2)}, u32[]{:S(2)}) collective-permute-start(bf16[768,128]{1,0:T(8,128)(2,1)S(1)} %get-tuple-element.28.qg_ref.qg0), channel_id=1, source_target_pairs={{0,64},{32,96},{64,0},{96,32},{1,65},{33,97},{65,1},{97,33},{2,66}... | collective-permute-start | bytes 589832 | tf_op jit(solution)/shard_map/ppermute | solution.py:24
  38.5 10.5 %collective-permute-start = (bf16[768,128]{1,0:T(8,128)(2,1)S(1)}, bf16[768,128]{1,0:T(8,128)(2,1)S(1)}, u32[]{:S(2)}, u32[]{:S(2)}) collective-permute-start(bf16[768,128]{1,0:T(8,128)(2,1)S(1)} %get-tuple-element.28.qg_ref.qg0), channel_id=1, source_target_pairs={{0,32},{32,0},{64,96},{96,64},{1,33},{33,1},{65,97},{97,65},{2,34}... | collective-permute-start | bytes 589832 | tf_op jit(solution)/shard_map/ppermute | solution.py:24
  40.7 0.7 copy-start.6
  40.7 0.7 copy-start.7
  42.2 13.6 %all-to-all-start.1 = ((f32[16,16,128]{2,1,0:T(8,128)}), f32[16,16,128]{2,1,0:T(8,128)S(1)}, u32[]{:S(2)}, u32[]{:S(2)}) async-start(f32[16,16,128]{2,1,0:T(8,128)} %get-tuple-element.30), calls=%async_computation.1 | async-start | bytes 262144 | tf_op jit(solution)/shard_map/all_to_all | solution.py:290
  55.8 0.7 copy-start.5
  74.3 0.7 copy-start.8
  87.6 22.2 %copy-start.9 = (bf16[768,128]{1,0:T(8,128)(2,1)S(1)}, bf16[768,128]{1,0:T(8,128)(2,1)}, u32[]{:S(2)}) copy-start(bf16[768,128]{1,0:T(8,128)(2,1)} %copy-done.8) | copy-start | bytes 589828
  88.8 40.9 %all-to-all-start.3 = ((bf16[32,8,128]{2,1,0:T(8,128)(2,1)}), bf16[32,8,128]{2,1,0:T(8,128)(2,1)S(1)}, u32[]{:S(2)}, u32[]{:S(2)}) async-start(bf16[32,8,128]{2,1,0:T(8,128)(2,1)} %get-tuple-element.41), calls=%async_computation.3 | async-start | bytes 131072 | tf_op jit(solution)/shard_map/all_to_all | solution.py:324
  107.5 15.5 %collective-permute-start.6 = (bf16[384,128]{1,0:T(8,128)(2,1)S(1)}, bf16[384,128]{1,0:T(8,128)(2,1)S(1)}, u32[]{:S(2)}, u32[]{:S(2)}) collective-permute-start(bf16[384,128]{1,0:T(8,128)(2,1)S(1)} %get-tuple-element.44), channel_id=1, source_target_pairs={{0,32},{32,0},{64,96},{96,64},{1,33},{33,1},{65,97},{97,65},{2,34}... | collective-permute-start | bytes 294920 | tf_op jit(solution)/shard_map/ppermute | solution.py:24
  109.7 19.9 %collective-permute-start.9 = (bf16[768,128]{1,0:T(8,128)(2,1)S(1)}, bf16[768,128]{1,0:T(8,128)(2,1)S(1)}, u32[]{:S(2)}, u32[]{:S(2)}) collective-permute-start(bf16[768,128]{1,0:T(8,128)(2,1)S(1)} %copy-done.9), channel_id=1, source_target_pairs={{0,128},{128,0},{256,384},{384,256},{1,129},{129,1},{257,385},{385... | collective-permute-start | bytes 589832 | tf_op jit(solution)/shard_map/ppermute | solution.py:24
  111.9 17.7 %collective-permute-start.10 = (bf16[768,128]{1,0:T(8,128)(2,1)S(1)}, bf16[768,128]{1,0:T(8,128)(2,1)S(1)}, u32[]{:S(2)}, u32[]{:S(2)}) collective-permute-start(bf16[768,128]{1,0:T(8,128)(2,1)S(1)} %get-tuple-element.49), channel_id=1, source_target_pairs={{0,256},{128,384},{256,0},{384,128},{1,257},{129,385},{257,1},{385... | collective-permute-start | bytes 589832 | tf_op jit(solution)/shard_map/ppermute | solution.py:24
  115.6 14.0 %collective-permute-start.11 = (bf16[768,128]{1,0:T(8,128)(2,1)S(1)}, bf16[768,128]{1,0:T(8,128)(2,1)S(1)}, u32[]{:S(2)}, u32[]{:S(2)}) collective-permute-start(bf16[768,128]{1,0:T(8,128)(2,1)S(1)} %get-tuple-element.50), channel_id=1, source_target_pairs={{0,384},{128,256},{256,128},{384,0},{1,385},{129,257},{257,129},{3... | collective-permute-start | bytes 589832 | tf_op jit(solution)/shard_map/ppermute | solution.py:24
  119.3 7.4 %collective-permute-start.7 = (bf16[384,128]{1,0:T(8,128)(2,1)S(1)}, bf16[384,128]{1,0:T(8,128)(2,1)S(1)}, u32[]{:S(2)}, u32[]{:S(2)}) collective-permute-start(bf16[384,128]{1,0:T(8,128)(2,1)S(1)} %get-tuple-element.45), channel_id=1, source_target_pairs={{0,64},{32,96},{64,0},{96,32},{1,65},{33,97},{65,1},{97,33},{2,66}... | collective-permute-start | bytes 294920 | tf_op jit(solution)/shard_map/ppermute | solution.py:24
  123.0 6.6 %collective-permute-start.8 = (bf16[384,128]{1,0:T(8,128)(2,1)S(1)}, bf16[384,128]{1,0:T(8,128)(2,1)S(1)}, u32[]{:S(2)}, u32[]{:S(2)}) collective-permute-start(bf16[384,128]{1,0:T(8,128)(2,1)S(1)} %get-tuple-element.46), channel_id=1, source_target_pairs={{0,96},{32,64},{64,32},{96,0},{1,97},{33,65},{65,33},{97,1},{2,98}... | collective-permute-start | bytes 294920 | tf_op jit(solution)/shard_map/ppermute | solution.py:24

commit v3 on v2

v3 whole, which is shorter than its diff:
```python
import math

import jax
import jax.numpy as jnp
from jax import lax
from jax.experimental import pallas as pl
from jax.experimental.pallas import tpu as pltpu
from jax.sharding import Mesh, PartitionSpec as P

EPSILON = 1e-06
SIDE = 4
HEADS = 32
ROWS = 384
WIDTH = 128
PIECES = ROWS // WIDTH
LINES = 16
HEAD = ("z", "c")
SEQ = ("y", "x")
F32 = jnp.float32
BF16 = jnp.bfloat16
ROOT = WIDTH ** (-0.5)
LOG2E = math.log2(math.e)
NT = (((1,), (1,)), ((), ()))
TN = (((0,), (0,)), ((), ()))


def swap(value, axis, mask):
    return lax.ppermute(value, axis, [(i, i ^ mask) for i in range(SIDE)])


def struct(shape, dtype):
    return jax.ShapeDtypeStruct(shape, dtype)


def call(kernel, out_shape, scratch=(), spaces="", limit=32):
    def run(*args):
        places = {"s": pltpu.SMEM, "h": pltpu.HBM, "v": pltpu.VMEM}
        specs = [pl.BlockSpec(memory_space=places[s]) for s in spaces.ljust(len(args), "v")]
        return pl.pallas_call(
            kernel,
            out_shape=out_shape,
            in_specs=specs,
            out_specs=jax.tree.map(lambda _: pl.BlockSpec(memory_space=pltpu.VMEM), out_shape),
            scratch_shapes=scratch,
            compiler_params=pltpu.CompilerParams(vmem_limit_bytes=limit * 2**20),
        )(*args)

    return run


def column(row):
    return jnp.broadcast_to(row, (WIDTH, WIDTH)).T


def row_sums(block):
    return jnp.sum(block.T, axis=0, keepdims=True)


def dot(a, b, dims=(((1,), (0,)), ((), ()))):
    return lax.dot_general(a, b, dims, preferred_element_type=F32)


def squares_kernel(q_hbm, k_hbm, msg_ref, q_ref, k_ref, sems):
    copies = [
        pltpu.make_async_copy(source, target, sems.at[i])
        for i, (source, target) in enumerate(((q_hbm, q_ref), (k_hbm, k_ref)))
    ]
    for copy in copies:
        copy.start()
    parts = []
    for copy, ref in zip(copies, (q_ref, k_ref)):
        copy.wait()
        for i in range(PIECES):
            block = ref[pl.ds(i * WIDTH, WIDTH), :].astype(F32)
            parts.append(row_sums(block * block))
    part = jnp.concatenate(parts, axis=1)
    for h in range(HEADS):
        msg_ref[h] = part


def delta_kernel(out_ref, grad_ref, qgain_ref, kgain_ref, delta_ref, qscale_ref, kscale_ref):
    line = lax.broadcasted_iota(jnp.int32, (LINES, WIDTH), 0)
    lines = jnp.zeros((LINES, WIDTH), F32)
    for i in range(PIECES):
        rows = pl.ds(i * WIDTH, WIDTH)
        delta = row_sums(out_ref[rows, :].astype(F32) * grad_ref[rows, :].astype(F32))
        high = delta.astype(BF16).astype(F32)
        lines = jnp.where(line == i, high, lines)
        lines = jnp.where(line == PIECES + i, delta - high, lines)
    delta_ref[...] = lines.astype(BF16)
    qscale_ref[...] = qgain_ref[...].astype(F32)
    kscale_ref[...] = kgain_ref[...].astype(F32)


def norms_kernel(
    sums_ref, q_ref, k_ref, grad_ref, values_ref, delta_ref, qscale_ref, kscale_ref,
    rate_ref, qmsg_ref, kmsg_ref,
):
    total = sums_ref[0]
    for h in range(1, HEADS):
        total = total + sums_ref[h]
    rate = lax.rsqrt(total / (HEADS * WIDTH) + EPSILON)
    line = lax.broadcasted_iota(jnp.int32, (8, WIDTH), 0)
    lines = jnp.zeros((8, WIDTH), F32)
    for i in range(2 * PIECES):
        lines = jnp.where(line == i, rate[:, i * WIDTH : (i + 1) * WIDTH], lines)
    rate_ref[...] = lines
    for i in range(PIECES):
        rows = pl.ds(i * WIDTH, WIDTH)
        later = pl.ds(ROWS + i * WIDTH, WIDTH)
        q = q_ref[rows, :].astype(F32) * column(lines[i : i + 1, :]) * qscale_ref[...]
        k = k_ref[rows, :].astype(F32) * column(lines[PIECES + i : PIECES + i + 1, :]) * kscale_ref[...]
        q = q.astype(BF16)
        for x in range(SIDE):
            qmsg_ref[x, rows, :] = q
            qmsg_ref[x, later, :] = grad_ref[rows, :]
        kmsg_ref[rows, :] = k.astype(BF16)
        kmsg_ref[later, :] = values_ref[rows, :]
    for x in range(SIDE):
        qmsg_ref[x, 2 * ROWS :, :] = delta_ref[...]


def totals_kernel(place_ref, order_hbm, qall_ref, kall_ref, total_ref, order_ref, sem):
    fetch = pltpu.make_async_copy(order_hbm, order_ref, sem)
    fetch.start()
    y = place_ref[0]
    x = place_ref[1]
    total_ref[...] = jnp.zeros_like(total_ref)
    fetch.wait()

    def tile(t, carry):
        j = t // SIDE
        i = lax.rem(t, SIDE)

        @pl.when(order_ref[j * SIDE + x] <= order_ref[y * SIDE + i])
        def _():
            scores = dot(kall_ref[j, :ROWS, :], qall_ref[i, :ROWS, :], NT)
            total_ref[i] += jnp.sum(jnp.exp2(scores * (ROOT * LOG2E)), axis=0, keepdims=True)

        return carry

    lax.fori_loop(0, SIDE * SIDE, tile, 0)


def grads_kernel(
    place_ref, order_hbm, total_ref, qall_ref, kall_ref,
    dkv_ref, dq0_ref, dq1_ref, dq2_ref, dq3_ref,
    dq_acc, dk_acc, dv_acc, log_all, delta_all, order_ref, sem,
):
    fetch = pltpu.make_async_copy(order_hbm, order_ref, sem)
    fetch.start()
    y = place_ref[0]
    x = place_ref[1]
    log_all[...] = jnp.log2(total_ref[...])
    for i in range(SIDE):
        lines = qall_ref[i, 2 * ROWS :, :].astype(F32)
        high = jnp.concatenate([lines[p : p + 1, :] for p in range(PIECES)], axis=1)
        low = jnp.concatenate([lines[PIECES + p : PIECES + p + 1, :] for p in range(PIECES)], axis=1)
        delta_all[i] = high + low
    dq_acc[...] = jnp.zeros_like(dq_acc)
    dk_acc[...] = jnp.zeros_like(dk_acc)
    dv_acc[...] = jnp.zeros_like(dv_acc)
    fetch.wait()

    def tile(t, carry):
        j = t // SIDE
        i = lax.rem(t, SIDE)

        @pl.when(order_ref[j * SIDE + x] <= order_ref[y * SIDE + i])
        def _():
            keys = kall_ref[j, :ROWS, :]
            queries = qall_ref[i, :ROWS, :]
            grad = qall_ref[i, ROWS : 2 * ROWS, :]
            scores = dot(keys, queries, NT)
            probs = jnp.exp2(scores * (ROOT * LOG2E) - log_all[i])
            dprobs = dot(kall_ref[j, ROWS:, :], grad, NT)
            dscores = (probs * (dprobs - delta_all[i])).astype(BF16)
            dv_acc[j] += dot(probs.astype(BF16), grad)
            dk_acc[j] += dot(dscores, queries)
            dq_acc[i] += dot(dscores, keys, TN)

        return carry

    lax.fori_loop(0, SIDE * SIDE, tile, 0)
    dkv_ref[:, :ROWS, :] = (dk_acc[...] * ROOT).astype(BF16)
    dkv_ref[:, ROWS:, :] = dv_acc[...].astype(BF16)
    for d, ref in enumerate((dq0_ref, dq1_ref, dq2_ref, dq3_ref)):
        ref[...] = (dq_acc[x ^ d] * ROOT).astype(BF16)


def sums_kernel(
    dkv_ref, dq0_ref, dq1_ref, dq2_ref, dq3_ref, q_ref, k_ref, qscale_ref, kscale_ref,
    gq_ref, gk_ref, dv_ref, msg_ref,
):
    parts = (dq0_ref, dq1_ref, dq2_ref, dq3_ref)
    line = lax.broadcasted_iota(jnp.int32, (8, WIDTH), 0)
    lines = jnp.zeros((8, WIDTH), F32)
    for i in range(PIECES):
        rows = pl.ds(i * WIDTH, WIDTH)
        later = pl.ds(ROWS + i * WIDTH, WIDTH)
        gq = sum(part[rows, :].astype(F32) for part in parts) * qscale_ref[...]
        gk = sum(dkv_ref[j, rows, :].astype(F32) for j in range(SIDE)) * kscale_ref[...]
        gq_ref[rows, :] = gq
        gk_ref[rows, :] = gk
        dv_ref[rows, :] = sum(dkv_ref[j, later, :].astype(F32) for j in range(SIDE)).astype(BF16)
        lines = jnp.where(line == i, row_sums(gq * q_ref[rows, :].astype(F32)), lines)
        lines = jnp.where(line == PIECES + i, row_sums(gk * k_ref[rows, :].astype(F32)), lines)
    msg_ref[...] = jnp.broadcast_to(lines.astype(BF16)[None], msg_ref.shape)


def final_kernel(sums_ref, rate_ref, gq_ref, gk_ref, q_ref, k_ref, dq_ref, dk_ref):
    inner = jnp.sum(sums_ref[...].astype(F32), axis=0)
    rate = rate_ref[...]
    weight = rate * rate * rate * inner / (HEADS * WIDTH)
    for first, g_ref, raw_ref, out_ref in ((0, gq_ref, q_ref, dq_ref), (PIECES, gk_ref, k_ref, dk_ref)):
        for i in range(PIECES):
            rows = pl.ds(i * WIDTH, WIDTH)
            line = slice(first + i, first + i + 1)
            raw = raw_ref[rows, :].astype(F32)
            out = column(rate[line, :]) * g_ref[rows, :] - raw * column(weight[line, :])
            out_ref[rows, :] = out.astype(BF16)


def local(q_raw, k_raw, values, out, d_out, q_gain, k_gain, order):
    block = struct((ROWS, WIDTH), BF16)
    wide = struct((ROWS, WIDTH), F32)
    pair = struct((2 * ROWS, WIDTH), BF16)
    lines = struct((8, WIDTH), F32)
    gain = struct((1, WIDTH), F32)
    known = (pltpu.SMEM((16,), jnp.int32), pltpu.SemaphoreType.DMA)
    place = jnp.stack([lax.axis_index("y"), lax.axis_index("x")]).astype(jnp.int32)

    squares, q_raw, k_raw = call(
        squares_kernel,
        (struct((HEADS, 1, 2 * ROWS), F32), block, block),
        scratch=(pltpu.SemaphoreType.DMA((2,)),),
        spaces="hh",
        limit=60,
    )(q_raw, k_raw)
    squares = lax.all_to_all(squares, HEAD, 0, 0)
    delta, q_scale, k_scale = call(delta_kernel, (struct((LINES, WIDTH), BF16), gain, gain))(
        out, d_out, q_gain.reshape(1, WIDTH), k_gain.reshape(1, WIDTH)
    )
    rate, queries, keys = call(
        norms_kernel, (lines, struct((SIDE, 2 * ROWS + LINES, WIDTH), BF16), pair)
    )(squares, q_raw, k_raw, d_out, values, delta, q_scale, k_scale)
    queries = lax.all_to_all(queries, "x", 0, 0)
    keys = lax.all_gather(keys, "y", axis=0, tiled=True).reshape(SIDE, 2 * ROWS, WIDTH)

    totals = call(
        totals_kernel, struct((SIDE, 1, ROWS), F32), scratch=known, spaces="sh"
    )(place, order, queries, keys)
    totals = lax.psum(totals, "x")

    keys, *queries = call(
        grads_kernel,
        (struct((SIDE, 2 * ROWS, WIDTH), BF16), block, block, block, block),
        scratch=(
            pltpu.VMEM((SIDE, ROWS, WIDTH), F32),
            pltpu.VMEM((SIDE, ROWS, WIDTH), F32),
            pltpu.VMEM((SIDE, ROWS, WIDTH), F32),
            pltpu.VMEM((SIDE, 1, ROWS), F32),
            pltpu.VMEM((SIDE, 1, ROWS), F32),
        ) + known,
        spaces="sh",
    )(place, order, totals, queries, keys)
    keys = lax.all_to_all(keys, "y", 0, 0)
    queries[1:] = [swap(part, "x", d) for d, part in enumerate(queries[1:], 1)]

    gq, gk, dv, inner = call(
        sums_kernel, (wide, wide, block, struct((HEADS, 8, WIDTH), BF16))
    )(keys, *queries, q_raw, k_raw, q_scale, k_scale)
    inner = lax.all_to_all(inner, HEAD, 0, 0)
    d_q, d_k = call(final_kernel, (block, block))(inner, rate, gq, gk, q_raw, k_raw)
    return d_q, d_k, dv


def solution(mesh):
    fine = Mesh(mesh.devices.reshape(SIDE, SIDE, 16, 2), ("y", "x", "z", "c"))
    both = P(SEQ, HEAD)
    return jax.shard_map(
        local,
        mesh=fine,
        in_specs=(both,) * 5 + (P(HEAD), P(HEAD), P()),
        out_specs=(both,) * 3,
        check_vma=False,
    )
```

time: 133 us -> 117 us (0.88)
  starting transfers between devices: 79.5 us -> 35.3 us
  blocking collectives: 19.7 us -> 42.7 us
  waiting for transfers between devices: 9.68 us -> 16 us
  local copies, waits for them, and re-layouts: 5.54 us -> 1.31 us
  Pallas kernels: 15.2 us -> 19.3 us
    ppermute x12 -> x3, starting transfers between devices: 37.2 us -> 9.57 us  [swap(): return lax.ppermute(value, axis, [(i, i ^ mask) for i in range(SIDE)])]
    all_to_all x2, starting transfers between devices: 25.4 us -> 8.86 us  [the longest x1 4.85 us: local(): keys = lax.all_to_all(keys, 'y', 0, 0)]
    all_to_all x1, waiting for transfers between devices: 0.01 us -> 13.8 us  [local(): squares = lax.all_to_all(squares, HEAD, 0, 0)]
    all_gather x0 -> x1, blocking collectives: none -> 12.3 us  [local(): lax.all_gather(keys, 'y', axis=0, tiled=True).reshape(SIDE, 2 * ROWS, WIDTH)]
    all_to_all x1, blocking collectives: 12.6 us -> 23.5 us  [local(): inner = lax.all_to_all(inner, HEAD, 0, 0)]
    all_to_all x2, waiting for transfers between devices: 6.79 us -> 0.01 us  [the longest x1 0.01 us: local(): queries = lax.all_to_all(queries, 'x', 0, 0)]
    unnamed x20 -> x16, local copies, waits for them, and re-layouts: 5.54 us -> 1.31 us
    pallas_call x7, Pallas kernels: 15.2 us -> 19.3 us  [run(): pl.pallas_call(kernel, out_shape=out_shape, in_specs=specs, out_specs=jax...]
  transfers between devices with their start and end apart: 15 -> 6, of which waited for: 2 -> 2; matrix products, arithmetic and copies ran while one was open for 0% -> 0% of each run, Pallas kernels for 1% -> 0%
where the time goes in v3:
time: 117 us; the launch traced here: 116 us
  blocking collectives  42.7 us (36%)
  starting transfers between devices  35.3 us (30%)
  Pallas kernels  19.3 us (16%)
  waiting for transfers between devices  16 us (14%)
  local copies, waits for them, and re-layouts  1.31 us (1%)
    all_to_all x1, blocking collectives, local(): inner = lax.all_to_all(inner, HEAD, 0, 0)  23.5 us
    pallas_call x7, Pallas kernels, run(): pl.pallas_call(kernel, out_shape=out_shape, in_specs=specs, out_specs=jax...  19.3 us
    all_to_all x1, starting transfers between devices, local(): squares = lax.all_to_all(squares, HEAD, 0, 0)  16.9 us
    all_to_all x1, waiting for transfers between devices, local(): squares = lax.all_to_all(squares, HEAD, 0, 0)  13.8 us
    all_gather x1, blocking collectives, local(): lax.all_gather(keys, 'y', axis=0, tiled=True).reshape(SIDE, 2 * ROWS, WIDTH)  12.3 us
    ppermute x3, starting transfers between devices, swap(): return lax.ppermute(value, axis, [(i, i ^ mask) for i in range(SIDE)])  9.57 us
    psum x1, blocking collectives, local(): totals = lax.psum(totals, 'x')  6.98 us
    all_to_all x1, starting transfers between devices, local(): keys = lax.all_to_all(keys, 'y', 0, 0)  4.85 us
  transfers between devices with their start and end apart: 6, of which 2 were waited for; matrix products, arithmetic and copies ran while one was open for 0% of the time, Pallas kernels for 0%

profile of v3, /device:TPU:1, one launch (start us, length us, event | category | flops | bytes accessed | tf_op | source)
XLA Modules:
  0.0 115.6 jit_solution(16214820867248808337)
XLA Ops:
  0.6 0.0 copy-start.4
  0.6 1.9 %shard_map.103 = (f32[32,1,768]{2,1,0:T(1,128)}, bf16[384,128]{1,0:T(8,128)(2,1)}, bf16[384,128]{1,0:T(8,128)(2,1)}) custom-call(bf16[384,128]{1,0:T(8,128)(2,1)} %q_hbm.1, bf16[384,128]{1,0:T(8,128)(2,1)} %k_hbm.1), custom_call_target="tpu_custom_call" | custom-call | tf_op jit(solution)/shard_map/pallas_call | solution.py:39
  2.5 0.0 copy-start.2
  2.5 0.0 copy-start.3
  2.6 16.9 %all-to-all-start = ((f32[32,1,768]{2,1,0:T(1,128)}), f32[32,1,768]{2,1,0:T(1,128)S(1)}, u32[]{:S(2)}, u32[]{:S(2)}) async-start(f32[32,1,768]{2,1,0:T(1,128)} %get-tuple-element.23), calls=%async_computation | async-start | bytes 196608 | tf_op jit(solution)/shard_map/all_to_all | solution.py:240
  19.5 0.0 copy-start.6
  19.5 0.0 copy-start.7
  19.5 0.0 copy-done.2
  19.5 0.0 copy-done.3
  19.5 0.6 copy-done.6
  20.1 0.0 copy-done.7
  20.1 0.0 copy-start
  20.1 0.0 copy-start.1
  20.1 0.1 shard_map.104
  20.3 13.8 %all-to-all-done.sums_ref = f32[32,1,768]{2,1,0:T(1,128)S(1)} async-done(((f32[32,1,768]{2,1,0:T(1,128)}), f32[32,1,768]{2,1,0:T(1,128)S(1)}, u32[]{:S(2)}, u32[]{:S(2)}) %all-to-all-start) | async-done | bytes 98336 | tf_op jit(solution)/shard_map/all_to_all | solution.py:240
  34.1 0.0 copy-done.4
  34.1 0.0 copy-done
  34.1 0.0 copy-done.1
  34.1 1.1 shard_map.105
  35.2 4.0 %all-to-all-start.1 = ((bf16[4,784,128]{2,1,0:T(8,128)(2,1)}), bf16[4,784,128]{2,1,0:T(8,128)(2,1)S(1)}, u32[]{:S(2)}, u32[]{:S(2)}) async-start(bf16[4,784,128]{2,1,0:T(8,128)(2,1)} %get-tuple-element.29), calls=%async_computation.1 | async-start | bytes 1605632 | tf_op jit(solution)/shard_map/all_to_all | solution.py:247
  39.2 0.1 pad_add_fusion.place_ref
  39.3 12.3 %all_gather.3 = bf16[3072,128]{1,0:T(8,128)(2,1)S(1)} all-gather(bf16[768,128]{1,0:T(8,128)(2,1)S(1)} %get-tuple-element.30), channel_id=1, replica_groups=mesh['y'=4,'x'=4,'z'=16,'c'=2] {'y'}, dimensions={0}, use_global_device_ids=true | all-gather | bytes 983040 | tf_op jit(solution)/shard_map/all_gather | solution.py:248
  51.6 0.0 copy-start.5
  51.6 0.0 all-to-all-done.1.qall_ref
  51.6 0.7 copy-done.5
  52.2 4.7 %shard_map.106 = f32[4,1,384]{2,1,0:T(1,128)S(1)} custom-call(s32[2]{0:T(128)S(1)} %pad_add_fusion.place_ref, s32[16]{0:T(128)S(1)} %copy-done.5, bf16[4,784,128]{2,1,0:T(8,128)(2,1)S(1)} %all-to-all-done.1.qall_ref, bf16[4,768,128]{2,1,0:T(8,128)(2,1)S(1)} %bitcast.5), custom_call_target="tpu_custom_call" | custom-call | tf_op jit(solution)/shard_map/pallas_call | solution.py:39
  56.9 7.0 %psum.7.total_ref = f32[4,1,384]{2,1,0:T(1,128)S(1)} all-reduce(f32[4,1,384]{2,1,0:T(1,128)S(1)} %shard_map.106), channel_id=1, replica_groups=mesh['y'=4,'x'=4,'z'=16,'c'=2] {'x'}, use_global_device_ids=true, to_apply=%region_0.0 | all-reduce | flops 1536 | bytes 12288 | tf_op jit(solution)/shard_map/psum | solution.py:253
  63.9 9.7 %shard_map.107 = (bf16[4,768,128]{2,1,0:T(8,128)(2,1)}, bf16[384,128]{1,0:T(8,128)(2,1)S(1)}, bf16[384,128]{1,0:T(8,128)(2,1)S(1)}, bf16[384,128]{1,0:T(8,128)(2,1)S(1)}, bf16[384,128]{1,0:T(8,128)(2,1)S(1)}) custom-call(s32[2]{0:T(128)S(1)} %pad_add_fusion.place_ref, s32[16]{0:T(128)S(1)} %copy-done.5, f32[4,1,384]{2,1,0:T(1,128)S(1)} %psum.7.total_ref, ...), custom_call_target="tpu_custom_call" | custom-call | tf_op jit(solution)/shard_map/pallas_call | solution.py:39
  73.6 4.9 %all-to-all-start.2 = ((bf16[4,768,128]{2,1,0:T(8,128)(2,1)}), bf16[4,768,128]{2,1,0:T(8,128)(2,1)S(1)}, u32[]{:S(2)}, u32[]{:S(2)}) async-start(bf16[4,768,128]{2,1,0:T(8,128)(2,1)} %get-tuple-element.31), calls=%async_computation.2 | async-start | bytes 1572864 | tf_op jit(solution)/shard_map/all_to_all | solution.py:267
  78.5 1.9 %collective-permute-start = (bf16[384,128]{1,0:T(8,128)(2,1)S(1)}, bf16[384,128]{1,0:T(8,128)(2,1)S(1)}, u32[]{:S(2)}, u32[]{:S(2)}) collective-permute-start(bf16[384,128]{1,0:T(8,128)(2,1)S(1)} %get-tuple-element.33), channel_id=1, source_target_pairs={{0,32},{32,0},{64,96},{96,64},{1,33},{33,1},{65,97},{97,65},{2,34}... | collective-permute-start | bytes 294920 | tf_op jit(solution)/shard_map/ppermute | solution.py:28
  80.4 2.5 %collective-permute-start.1 = (bf16[384,128]{1,0:T(8,128)(2,1)S(1)}, bf16[384,128]{1,0:T(8,128)(2,1)S(1)}, u32[]{:S(2)}, u32[]{:S(2)}) collective-permute-start(bf16[384,128]{1,0:T(8,128)(2,1)S(1)} %get-tuple-element.34), channel_id=1, source_target_pairs={{0,64},{32,96},{64,0},{96,32},{1,65},{33,97},{65,1},{97,33},{2,66}... | collective-permute-start | bytes 294920 | tf_op jit(solution)/shard_map/ppermute | solution.py:28
  82.9 5.2 %collective-permute-start.2 = (bf16[384,128]{1,0:T(8,128)(2,1)S(1)}, bf16[384,128]{1,0:T(8,128)(2,1)S(1)}, u32[]{:S(2)}, u32[]{:S(2)}) collective-permute-start(bf16[384,128]{1,0:T(8,128)(2,1)S(1)} %get-tuple-element.35), channel_id=1, source_target_pairs={{0,96},{32,64},{64,32},{96,0},{1,97},{33,65},{65,33},{97,1},{2,98}... | collective-permute-start | bytes 294920 | tf_op jit(solution)/shard_map/ppermute | solution.py:28
  88.1 0.0 collective-permute-done.dq1_ref
  88.1 0.0 collective-permute-done.1.dq2_ref
  88.1 2.3 %collective-permute-done.2.dq3_ref = bf16[384,128]{1,0:T(8,128)(2,1)S(1)} collective-permute-done((bf16[384,128]{1,0:T(8,128)(2,1)S(1)}, bf16[384,128]{1,0:T(8,128)(2,1)S(1)}, u32[]{:S(2)}, u32[]{:S(2)}) %collective-permute-start.2) | collective-permute-done | bytes 98336 | tf_op jit(solution)/shard_map/ppermute | solution.py:28
  90.3 0.0 all-to-all-done.2.dkv_ref
  90.3 0.8 shard_map.108
  91.2 23.5 %all_to_all.20.sums_ref = bf16[32,8,128]{2,1,0:T(8,128)(2,1)S(1)} all-to-all(bf16[32,8,128]{2,1,0:T(8,128)(2,1)S(1)} %get-tuple-element.36), channel_id=1, replica_groups=mesh['y'=4,'x'=4,'z'=16,'c'=2] {'z','c'}, dimensions={0} | all-to-all | bytes 131072 | tf_op jit(solution)/shard_map/all_to_all | solution.py:273
  114.7 1.0 shard_map.109
Async XLA Ops:
  0.6 33.4 %copy-start.4 = (bf16[384,128]{1,0:T(8,128)(2,1)S(1)}, bf16[384,128]{1,0:T(8,128)(2,1)}, u32[]{:S(2)}) copy-start(bf16[384,128]{1,0:T(8,128)(2,1)} %values_ref.1) | copy-start | bytes 294916
  2.5 17.0 %copy-start.2 = (bf16[384,128]{1,0:T(8,128)(2,1)S(1)}, bf16[384,128]{1,0:T(8,128)(2,1)}, u32[]{:S(2)}) copy-start(bf16[384,128]{1,0:T(8,128)(2,1)} %grad_ref.3) | copy-start | bytes 294916
  2.5 17.0 %copy-start.3 = (bf16[384,128]{1,0:T(8,128)(2,1)S(1)}, bf16[384,128]{1,0:T(8,128)(2,1)}, u32[]{:S(2)}) copy-start(bf16[384,128]{1,0:T(8,128)(2,1)} %out_ref.1) | copy-start | bytes 294916
  2.6 31.5 %all-to-all-start = ((f32[32,1,768]{2,1,0:T(1,128)}), f32[32,1,768]{2,1,0:T(1,128)S(1)}, u32[]{:S(2)}, u32[]{:S(2)}) async-start(f32[32,1,768]{2,1,0:T(1,128)} %get-tuple-element.23), calls=%async_computation | async-start | bytes 196608 | tf_op jit(solution)/shard_map/all_to_all | solution.py:240
  19.5 0.7 copy-start.6
  19.5 0.7 copy-start.7
  20.1 13.9 %copy-start = (bf16[384,128]{1,0:T(8,128)(2,1)S(1)}, bf16[384,128]{1,0:T(8,128)(2,1)}, u32[]{:S(2)}) copy-start(bf16[384,128]{1,0:T(8,128)(2,1)} %get-tuple-element.24.q_ref) | copy-start | bytes 294916
  20.1 13.9 %copy-start.1 = (bf16[384,128]{1,0:T(8,128)(2,1)S(1)}, bf16[384,128]{1,0:T(8,128)(2,1)}, u32[]{:S(2)}) copy-start(bf16[384,128]{1,0:T(8,128)(2,1)} %get-tuple-element.25.k_ref) | copy-start | bytes 294916
  35.2 16.4 %all-to-all-start.1 = ((bf16[4,784,128]{2,1,0:T(8,128)(2,1)}), bf16[4,784,128]{2,1,0:T(8,128)(2,1)S(1)}, u32[]{:S(2)}, u32[]{:S(2)}) async-start(bf16[4,784,128]{2,1,0:T(8,128)(2,1)} %get-tuple-element.29), calls=%async_computation.1 | async-start | bytes 1605632 | tf_op jit(solution)/shard_map/all_to_all | solution.py:247
  51.6 0.7 copy-start.5
  73.6 16.7 %all-to-all-start.2 = ((bf16[4,768,128]{2,1,0:T(8,128)(2,1)}), bf16[4,768,128]{2,1,0:T(8,128)(2,1)S(1)}, u32[]{:S(2)}, u32[]{:S(2)}) async-start(bf16[4,768,128]{2,1,0:T(8,128)(2,1)} %get-tuple-element.31), calls=%async_computation.2 | async-start | bytes 1572864 | tf_op jit(solution)/shard_map/all_to_all | solution.py:267
  78.5 9.6 %collective-permute-start = (bf16[384,128]{1,0:T(8,128)(2,1)S(1)}, bf16[384,128]{1,0:T(8,128)(2,1)S(1)}, u32[]{:S(2)}, u32[]{:S(2)}) collective-permute-start(bf16[384,128]{1,0:T(8,128)(2,1)S(1)} %get-tuple-element.33), channel_id=1, source_target_pairs={{0,32},{32,0},{64,96},{96,64},{1,33},{33,1},{65,97},{97,65},{2,34}... | collective-permute-start | bytes 294920 | tf_op jit(solution)/shard_map/ppermute | solution.py:28
  80.4 7.7 %collective-permute-start.1 = (bf16[384,128]{1,0:T(8,128)(2,1)S(1)}, bf16[384,128]{1,0:T(8,128)(2,1)S(1)}, u32[]{:S(2)}, u32[]{:S(2)}) collective-permute-start(bf16[384,128]{1,0:T(8,128)(2,1)S(1)} %get-tuple-element.34), channel_id=1, source_target_pairs={{0,64},{32,96},{64,0},{96,32},{1,65},{33,97},{65,1},{97,33},{2,66}... | collective-permute-start | bytes 294920 | tf_op jit(solution)/shard_map/ppermute | solution.py:28
  82.9 7.5 %collective-permute-start.2 = (bf16[384,128]{1,0:T(8,128)(2,1)S(1)}, bf16[384,128]{1,0:T(8,128)(2,1)S(1)}, u32[]{:S(2)}, u32[]{:S(2)}) collective-permute-start(bf16[384,128]{1,0:T(8,128)(2,1)S(1)} %get-tuple-element.35), channel_id=1, source_target_pairs={{0,96},{32,64},{64,32},{96,0},{1,97},{33,65},{65,33},{97,1},{2,98}... | collective-permute-start | bytes 294920 | tf_op jit(solution)/shard_map/ppermute | solution.py:28

commit v4 on v3

v4 whole, which is shorter than its diff:
```python
import math

import jax
import jax.numpy as jnp
from jax import lax
from jax.experimental import pallas as pl
from jax.experimental.pallas import tpu as pltpu
from jax.sharding import Mesh, PartitionSpec as P

EPSILON = 1e-06
SIDE = 4
HEADS = 32
ROWS = 384
WIDTH = 128
PIECES = ROWS // WIDTH
LINES = 16
HEAD = ("z", "c")
SEQ = ("y", "x")
F32 = jnp.float32
BF16 = jnp.bfloat16
ROOT = WIDTH ** (-0.5)
LOG2E = math.log2(math.e)
NT = (((1,), (1,)), ((), ()))
TN = (((0,), (0,)), ((), ()))


def swap(value, axis, mask):
    return lax.ppermute(value, axis, [(i, i ^ mask) for i in range(SIDE)])


def struct(shape, dtype):
    return jax.ShapeDtypeStruct(shape, dtype)


def call(kernel, out_shape, scratch=(), spaces="", limit=32):
    def run(*args):
        memory = {"s": pltpu.SMEM, "v": pltpu.VMEM}
        specs = [pl.BlockSpec(memory_space=memory[s]) for s in spaces.ljust(len(args), "v")]
        return pl.pallas_call(
            kernel,
            out_shape=out_shape,
            in_specs=specs,
            out_specs=jax.tree.map(lambda _: pl.BlockSpec(memory_space=pltpu.VMEM), out_shape),
            scratch_shapes=scratch,
            compiler_params=pltpu.CompilerParams(vmem_limit_bytes=limit * 2**20),
        )(*args)

    return run


def column(row):
    return jnp.broadcast_to(row, (WIDTH, WIDTH)).T


def row_sums(block):
    return jnp.sum(block.T, axis=0, keepdims=True)


def dot(a, b, dims=(((1,), (0,)), ((), ()))):
    return lax.dot_general(a, b, dims, preferred_element_type=F32)


def squares_kernel(q_ref, k_ref, msg_ref):
    sums = []
    for ref in (q_ref, k_ref):
        parts = []
        for i in range(PIECES):
            block = ref[pl.ds(i * WIDTH, WIDTH), :].astype(F32)
            parts.append(row_sums(block * block))
        sums.append(jnp.concatenate(parts, axis=1))
    both = jnp.concatenate(sums, axis=0)
    square = both * both
    coded = (square * square).astype(BF16)
    for h in range(HEADS):
        msg_ref[h] = coded


def ready_kernel(
    place_ref, order_ref, q_ref, k_ref, g_ref, v_ref, o_ref, qgain_ref, kgain_ref,
    q_out, k_out, g_out, v_out, lines_ref, qscale_ref, kscale_ref,
):
    group = order_ref[place_ref[0] * SIDE + place_ref[1]].astype(F32)
    line = lax.broadcasted_iota(jnp.int32, (LINES, WIDTH), 0)
    lines = jnp.full((LINES, WIDTH), group, F32)
    for i in range(PIECES):
        rows = pl.ds(i * WIDTH, WIDTH)
        delta = row_sums(o_ref[rows, :].astype(F32) * g_ref[rows, :].astype(F32))
        high = delta.astype(BF16).astype(F32)
        lines = jnp.where(line == i, high, lines)
        lines = jnp.where(line == PIECES + i, delta - high, lines)
    lines_ref[...] = lines.astype(BF16)
    for source, target in ((q_ref, q_out), (k_ref, k_out), (g_ref, g_out), (v_ref, v_out)):
        target[...] = source[...]
    qscale_ref[...] = qgain_ref[...].astype(F32)
    kscale_ref[...] = kgain_ref[...].astype(F32)


def norms_kernel(
    sums_ref, q_ref, k_ref, g_ref, v_ref, lines_ref, qscale_ref, kscale_ref,
    rate_ref, qmsg_ref, kmsg_ref,
):
    total = jnp.zeros((2, ROWS), F32)
    for h in range(HEADS):
        total = total + jnp.sqrt(jnp.sqrt(jnp.maximum(sums_ref[h].astype(F32), 1e-36)))
    rate = lax.rsqrt(total / (HEADS * WIDTH) + EPSILON)
    rate_ref[...] = rate
    for i in range(PIECES):
        rows = pl.ds(i * WIDTH, WIDTH)
        later = pl.ds(ROWS + i * WIDTH, WIDTH)
        span = slice(i * WIDTH, (i + 1) * WIDTH)
        q = q_ref[rows, :].astype(F32) * column(rate[0:1, span]) * qscale_ref[...]
        k = k_ref[rows, :].astype(F32) * column(rate[1:2, span]) * kscale_ref[...]
        q = q.astype(BF16)
        for x in range(SIDE):
            qmsg_ref[x, rows, :] = q
            qmsg_ref[x, later, :] = g_ref[rows, :]
        kmsg_ref[rows, :] = k.astype(BF16)
        kmsg_ref[later, :] = v_ref[rows, :]
    for x in range(SIDE):
        qmsg_ref[x, 2 * ROWS :, :] = lines_ref[...]
    kmsg_ref[2 * ROWS :, :] = lines_ref[...]


def across(lines, first):
    return jnp.concatenate([lines[first + p : first + p + 1, :] for p in range(PIECES)], axis=1)


def query_groups(qall_ref):
    rows = [qall_ref[i, 2 * ROWS :, :].astype(F32)[2 * PIECES : 2 * PIECES + 1, :] for i in range(SIDE)]
    return jnp.concatenate([row for row in rows for _ in range(PIECES)], axis=1)


def key_group(kall_ref, j):
    row = kall_ref[j, 2 * ROWS :, :].astype(F32)[2 * PIECES : 2 * PIECES + 1, :]
    return jnp.concatenate([row] * (SIDE * PIECES), axis=1)


def totals_kernel(qall_ref, kall_ref, total_ref, q_all):
    for i in range(SIDE):
        q_all[i * ROWS : (i + 1) * ROWS, :] = qall_ref[i, :ROWS, :]
    groups = query_groups(qall_ref)

    def key_block(j, total):
        scores = dot(kall_ref[j, :ROWS, :], q_all[...], NT)
        part = jnp.sum(jnp.exp2(scores * (ROOT * LOG2E)), axis=0, keepdims=True)
        return total + jnp.where(key_group(kall_ref, j) <= groups, part, 0.0)

    total = lax.fori_loop(0, SIDE, key_block, jnp.zeros((1, SIDE * ROWS), F32))
    for i in range(SIDE):
        total_ref[i] = total[:, i * ROWS : (i + 1) * ROWS]


def grads_kernel(
    place_ref, total_ref, qall_ref, kall_ref,
    dkv_ref, dq0_ref, dq1_ref, dq2_ref, dq3_ref,
    q_all, g_all, k_all, v_all, logs, deltas, groups, dq_acc,
):
    for i in range(SIDE):
        span = slice(i * ROWS, (i + 1) * ROWS)
        q_all[span, :] = qall_ref[i, :ROWS, :]
        g_all[span, :] = qall_ref[i, ROWS : 2 * ROWS, :]
        k_all[span, :] = kall_ref[i, :ROWS, :]
        v_all[span, :] = kall_ref[i, ROWS : 2 * ROWS, :]
        lines = qall_ref[i, 2 * ROWS :, :].astype(F32)
        deltas[:, span] = across(lines, 0) + across(lines, PIECES)
        logs[:, span] = jnp.log2(total_ref[i])
    groups[...] = query_groups(qall_ref)
    dq_acc[...] = jnp.zeros_like(dq_acc)
    half = SIDE * ROWS // 2

    def key_pair(m, carry):
        rows = pl.ds(pl.multiple_of(m * half, half), half)
        keys = k_all[rows, :]
        vals = v_all[rows, :]
        shifts = [
            jnp.where(key_group(kall_ref, 2 * m + n) <= groups[...], logs[...], 1e30) for n in range(2)
        ]

        def part(h):
            span = slice(h * half, (h + 1) * half)
            queries = q_all[span, :]
            grad = g_all[span, :]
            scores = dot(keys, queries, NT) * (ROOT * LOG2E)
            upper = scores[:ROWS] - shifts[0][:, span]
            lower = scores[ROWS:] - shifts[1][:, span]
            probs = jnp.exp2(jnp.concatenate([upper, lower], axis=0))
            dprobs = dot(vals, grad, NT)
            dscores = (probs * (dprobs - deltas[:, span])).astype(BF16)
            dq_acc[:, span] += dot(keys, dscores, TN)
            return dot(dscores, queries), dot(probs.astype(BF16), grad)

        first, second = part(0), part(1)
        dk = ((first[0] + second[0]) * ROOT).astype(BF16)
        dv = (first[1] + second[1]).astype(BF16)
        for n in range(2):
            dkv_ref[2 * m + n, :ROWS, :] = dk[n * ROWS : (n + 1) * ROWS]
            dkv_ref[2 * m + n, ROWS:, :] = dv[n * ROWS : (n + 1) * ROWS]
        return carry

    lax.fori_loop(0, SIDE // 2, key_pair, 0)
    x = place_ref[1]
    for d, ref in enumerate((dq0_ref, dq1_ref, dq2_ref, dq3_ref)):
        span = pl.ds(pl.multiple_of((x ^ d) * ROWS, ROWS), ROWS)
        ref[...] = (dq_acc[:, span].T * ROOT).astype(BF16)


def sums_kernel(
    dkv_ref, dq0_ref, dq1_ref, dq2_ref, dq3_ref, q_ref, k_ref, qscale_ref, kscale_ref,
    gq_ref, gk_ref, dv_ref, msg_ref,
):
    parts = (dq0_ref, dq1_ref, dq2_ref, dq3_ref)
    q_lines = []
    k_lines = []
    for i in range(PIECES):
        rows = pl.ds(i * WIDTH, WIDTH)
        later = pl.ds(ROWS + i * WIDTH, WIDTH)
        gq = sum(part[rows, :].astype(F32) for part in parts) * qscale_ref[...]
        gk = sum(dkv_ref[j, rows, :].astype(F32) for j in range(SIDE)) * kscale_ref[...]
        gq_ref[rows, :] = gq
        gk_ref[rows, :] = gk
        dv_ref[rows, :] = sum(dkv_ref[j, later, :].astype(F32) for j in range(SIDE)).astype(BF16)
        q_lines.append(row_sums(gq * q_ref[rows, :].astype(F32)))
        k_lines.append(row_sums(gk * k_ref[rows, :].astype(F32)))
    both = [jnp.concatenate(lines, axis=1) for lines in (q_lines, k_lines)]
    coded = jnp.concatenate(both, axis=0).astype(BF16)
    for h in range(HEADS):
        msg_ref[h] = coded


def final_kernel(sums_ref, rate_ref, gq_ref, gk_ref, q_ref, k_ref, dq_ref, dk_ref):
    inner = jnp.zeros((2, ROWS), F32)
    for h in range(HEADS):
        inner = inner + sums_ref[h].astype(F32)
    rate = rate_ref[...]
    weight = rate * rate * rate * inner / (HEADS * WIDTH)
    for n, (g_ref, raw_ref, out_ref) in enumerate(((gq_ref, q_ref, dq_ref), (gk_ref, k_ref, dk_ref))):
        for i in range(PIECES):
            rows = pl.ds(i * WIDTH, WIDTH)
            span = slice(i * WIDTH, (i + 1) * WIDTH)
            raw = raw_ref[rows, :].astype(F32)
            out = column(rate[n : n + 1, span]) * g_ref[rows, :] - raw * column(weight[n : n + 1, span])
            out_ref[rows, :] = out.astype(BF16)


def local(q_raw, k_raw, values, out, d_out, q_gain, k_gain, order):
    block = struct((ROWS, WIDTH), BF16)
    wide = struct((ROWS, WIDTH), F32)
    pair = struct((2 * ROWS, WIDTH), BF16)
    message = struct((HEADS, 2, ROWS), BF16)
    place = jnp.stack([lax.axis_index("y"), lax.axis_index("x")]).astype(jnp.int32)
    q_gain = q_gain.reshape(1, WIDTH)
    k_gain = k_gain.reshape(1, WIDTH)

    squares = call(squares_kernel, message, limit=60)(q_raw, k_raw)
    squares = lax.all_to_all(squares, HEAD, 0, 0)
    gain = struct((1, WIDTH), F32)
    q_raw, k_raw, d_out, values, lines, q_gain, k_gain = call(
        ready_kernel,
        (block, block, block, block, struct((LINES, WIDTH), BF16), gain, gain),
        spaces="ss",
    )(place, order, q_raw, k_raw, d_out, values, out, q_gain, k_gain)
    rate, queries, keys = call(
        norms_kernel,
        (
            struct((2, ROWS), F32),
            struct((SIDE, 2 * ROWS + LINES, WIDTH), BF16),
            struct((2 * ROWS + LINES, WIDTH), BF16),
        ),
    )(squares, q_raw, k_raw, d_out, values, lines, q_gain, k_gain)
    queries = lax.all_to_all(queries, "x", 0, 0)
    keys = lax.all_gather(keys, "y", axis=0, tiled=True).reshape(SIDE, 2 * ROWS + LINES, WIDTH)

    totals = call(
        totals_kernel,
        struct((SIDE, 1, ROWS), F32),
        scratch=(pltpu.VMEM((SIDE * ROWS, WIDTH), BF16),),
    )(queries, keys)
    totals = lax.psum(totals, "x")

    tall = pltpu.VMEM((SIDE * ROWS, WIDTH), BF16)
    row = pltpu.VMEM((1, SIDE * ROWS), F32)
    keys, *queries = call(
        grads_kernel,
        (struct((SIDE, 2 * ROWS, WIDTH), BF16), block, block, block, block),
        scratch=(tall, tall, tall, tall, row, row, row, pltpu.VMEM((WIDTH, SIDE * ROWS), F32)),
        spaces="s",
    )(place, totals, queries, keys)
    keys = lax.all_to_all(keys, "y", 0, 0)
    queries[1:] = [swap(part, "x", d) for d, part in enumerate(queries[1:], 1)]

    gq, gk, dv, inner = call(
        sums_kernel, (wide, wide, block, message)
    )(keys, *queries, q_raw, k_raw, q_gain, k_gain)
    inner = lax.all_to_all(inner, HEAD, 0, 0)
    d_q, d_k = call(final_kernel, (block, block))(inner, rate, gq, gk, q_raw, k_raw)
    return d_q, d_k, dv


def solution(mesh):
    fine = Mesh(mesh.devices.reshape(SIDE, SIDE, 16, 2), ("y", "x", "z", "c"))
    both = P(SEQ, HEAD)
    return jax.shard_map(
        local,
        mesh=fine,
        in_specs=(both,) * 5 + (P(HEAD), P(HEAD), P()),
        out_specs=(both,) * 3,
        check_vma=False,
    )
```

time: 117 us -> 109 us (0.932)
  waiting for transfers between devices: 16 us -> 11.5 us
  Pallas kernels: 19.3 us -> 15.1 us
  starting transfers between devices: 35.3 us -> 34 us
  blocking collectives: 42.7 us -> 43.9 us
    all_to_all x1, waiting for transfers between devices: 13.8 us -> 9.27 us  [local(): squares = lax.all_to_all(squares, HEAD, 0, 0)]
    pallas_call x7, Pallas kernels: 19.3 us -> 15.1 us  [run(): pl.pallas_call(kernel, out_shape=out_shape, in_specs=specs, out_specs=jax...]
    psum x1, blocking collectives: 6.98 us -> 8.96 us  [local(): totals = lax.psum(totals, 'x')]
    all_to_all x1, starting transfers between devices: 4.85 us -> 3.49 us  [local(): keys = lax.all_to_all(keys, 'y', 0, 0)]
  transfers between devices with their start and end apart: 6 -> 6, of which waited for: 2 -> 2; matrix products, arithmetic and copies ran while one was open for 0% -> 0% of each run, Pallas kernels for 0% -> 1%
where the time goes in v4:
time: 109 us; the launch traced here: 108 us
  blocking collectives  43.9 us (40%)
  starting transfers between devices  34 us (31%)
  Pallas kernels  15.1 us (14%)
  waiting for transfers between devices  11.5 us (11%)
  local copies, waits for them, and re-layouts  2.46 us (2%)
    all_to_all x1, blocking collectives, local(): inner = lax.all_to_all(inner, HEAD, 0, 0)  22.6 us
    all_to_all x1, starting transfers between devices, local(): squares = lax.all_to_all(squares, HEAD, 0, 0)  16.9 us
    pallas_call x7, Pallas kernels, run(): pl.pallas_call(kernel, out_shape=out_shape, in_specs=specs, out_specs=jax...  15.1 us
    all_gather x1, blocking collectives, local(): lax.all_gather(keys, 'y', axis=0, tiled=True)  12.4 us
    ppermute x3, starting transfers between devices, swap(): return lax.ppermute(value, axis, [(i, i ^ mask) for i in range(SIDE)])  9.58 us
    all_to_all x1, waiting for transfers between devices, local(): squares = lax.all_to_all(squares, HEAD, 0, 0)  9.27 us
    psum x1, blocking collectives, local(): totals = lax.psum(totals, 'x')  8.96 us
    all_to_all x1, starting transfers between devices, local(): queries = lax.all_to_all(queries, 'x', 0, 0)  4.01 us
  transfers between devices with their start and end apart: 6, of which 2 were waited for; matrix products, arithmetic and copies ran while one was open for 0% of the time, Pallas kernels for 1%

profile of v4, /device:TPU:1, one launch (start us, length us, event | category | flops | bytes accessed | tf_op | source)
XLA Modules:
  0.0 107.9 jit_solution(9635564009883688726)
XLA Ops:
  0.6 0.0 copy-start.1
  0.6 0.0 copy-start.2
  0.7 1.8 %shard_map.103 = bf16[32,2,384]{2,1,0:T(2,128)(2,1)} custom-call(bf16[384,128]{1,0:T(8,128)(2,1)} %q_ref.3, bf16[384,128]{1,0:T(8,128)(2,1)} %k_ref.3), custom_call_target="tpu_custom_call" | custom-call | tf_op jit(solution)/shard_map/pallas_call | solution.py:39
  2.5 0.0 copy-start
  2.5 16.9 %all-to-all-start = ((bf16[32,2,384]{2,1,0:T(2,128)(2,1)}), bf16[32,2,384]{2,1,0:T(2,128)(2,1)S(1)}, u32[]{:S(2)}, u32[]{:S(2)}) async-start(bf16[32,2,384]{2,1,0:T(2,128)(2,1)} %shard_map.103), calls=%async_computation | async-start | bytes 98304 | tf_op jit(solution)/shard_map/all_to_all | solution.py:255
  19.3 0.1 pad_add_fusion.place_ref
  19.4 0.0 copy-start.5
  19.4 0.0 copy-start.6
  19.4 0.0 copy-start.7
  19.4 0.0 copy-done.1
  19.4 0.0 copy-done.2
  19.4 0.0 copy-done
  19.5 0.6 copy-done.5
  20.1 0.0 copy-done.6
  20.1 0.0 copy-done.7
  20.1 0.0 copy-start.3
  20.1 0.9 copy-done.3
  21.0 0.0 copy-start.4
  21.0 0.9 copy-done.4
  21.9 0.7 shard_map.104
  22.6 9.3 %all-to-all-done.sums_ref = bf16[32,2,384]{2,1,0:T(2,128)(2,1)S(1)} async-done(((bf16[32,2,384]{2,1,0:T(2,128)(2,1)}), bf16[32,2,384]{2,1,0:T(2,128)(2,1)S(1)}, u32[]{:S(2)}, u32[]{:S(2)}) %all-to-all-start) | async-done | bytes 49184 | tf_op jit(solution)/shard_map/all_to_all | solution.py:255
  31.8 1.2 %shard_map.105 = (f32[2,384]{1,0:T(2,128)S(1)}, bf16[4,784,128]{2,1,0:T(8,128)(2,1)}, bf16[784,128]{1,0:T(8,128)(2,1)S(1)}) custom-call(bf16[32,2,384]{2,1,0:T(2,128)(2,1)S(1)} %all-to-all-done.sums_ref, bf16[384,128]{1,0:T(8,128)(2,1)S(1)} %get-tuple-element.24.q_ref, bf16[384,128]{1,0:T(8,128)(2,1)S(1)} %get-tuple-element.25.k_ref, ...), custom_call_target="tpu_custom_call" | custom-call | tf_op jit(solution)/shard_map/pallas_call | solution.py:39
  33.0 4.0 %all-to-all-start.1 = ((bf16[4,784,128]{2,1,0:T(8,128)(2,1)}), bf16[4,784,128]{2,1,0:T(8,128)(2,1)S(1)}, u32[]{:S(2)}, u32[]{:S(2)}) async-start(bf16[4,784,128]{2,1,0:T(8,128)(2,1)} %get-tuple-element.31), calls=%async_computation.1 | async-start | bytes 1605632 | tf_op jit(solution)/shard_map/all_to_all | solution.py:270
  37.0 12.4 %all_gather.3 = bf16[3136,128]{1,0:T(8,128)(2,1)S(1)} all-gather(bf16[784,128]{1,0:T(8,128)(2,1)S(1)} %get-tuple-element.32), channel_id=1, replica_groups=mesh['y'=4,'x'=4,'z'=16,'c'=2] {'y'}, dimensions={0}, use_global_device_ids=true | all-gather | bytes 1003520 | tf_op jit(solution)/shard_map/all_gather | solution.py:271
  49.4 0.0 all-to-all-done.1.qall_ref
  49.4 2.0 %shard_map.106 = f32[4,1,384]{2,1,0:T(1,128)S(1)} custom-call(bf16[4,784,128]{2,1,0:T(8,128)(2,1)S(1)} %all-to-all-done.1.qall_ref, bf16[4,784,128]{2,1,0:T(8,128)(2,1)S(1)} %bitcast.5), custom_call_target="tpu_custom_call" | custom-call | tf_op jit(solution)/shard_map/pallas_call | solution.py:39
  51.4 9.0 %psum.7.total_ref = f32[4,1,384]{2,1,0:T(1,128)S(1)} all-reduce(f32[4,1,384]{2,1,0:T(1,128)S(1)} %shard_map.106), channel_id=1, replica_groups=mesh['y'=4,'x'=4,'z'=16,'c'=2] {'x'}, use_global_device_ids=true, to_apply=%region_0.0 | all-reduce | flops 1536 | bytes 12288 | tf_op jit(solution)/shard_map/psum | solution.py:278
  60.4 7.7 %shard_map.107 = (bf16[4,768,128]{2,1,0:T(8,128)(2,1)}, bf16[384,128]{1,0:T(8,128)(2,1)S(1)}, bf16[384,128]{1,0:T(8,128)(2,1)S(1)}, bf16[384,128]{1,0:T(8,128)(2,1)S(1)}, bf16[384,128]{1,0:T(8,128)(2,1)S(1)}) custom-call(s32[2]{0:T(128)S(1)} %pad_add_fusion.place_ref, f32[4,1,384]{2,1,0:T(1,128)S(1)} %psum.7.total_ref, ...), custom_call_target="tpu_custom_call" | custom-call | tf_op jit(solution)/shard_map/pallas_call | solution.py:39
  68.1 3.5 %all-to-all-start.2 = ((bf16[4,768,128]{2,1,0:T(8,128)(2,1)}), bf16[4,768,128]{2,1,0:T(8,128)(2,1)S(1)}, u32[]{:S(2)}, u32[]{:S(2)}) async-start(bf16[4,768,128]{2,1,0:T(8,128)(2,1)} %get-tuple-element.33), calls=%async_computation.2 | async-start | bytes 1572864 | tf_op jit(solution)/shard_map/all_to_all | solution.py:288
  71.6 1.9 %collective-permute-start = (bf16[384,128]{1,0:T(8,128)(2,1)S(1)}, bf16[384,128]{1,0:T(8,128)(2,1)S(1)}, u32[]{:S(2)}, u32[]{:S(2)}) collective-permute-start(bf16[384,128]{1,0:T(8,128)(2,1)S(1)} %get-tuple-element.35), channel_id=1, source_target_pairs={{0,32},{32,0},{64,96},{96,64},{1,33},{33,1},{65,97},{97,65},{2,34}... | collective-permute-start | bytes 294920 | tf_op jit(solution)/shard_map/ppermute | solution.py:28
  73.5 2.8 %collective-permute-start.1 = (bf16[384,128]{1,0:T(8,128)(2,1)S(1)}, bf16[384,128]{1,0:T(8,128)(2,1)S(1)}, u32[]{:S(2)}, u32[]{:S(2)}) collective-permute-start(bf16[384,128]{1,0:T(8,128)(2,1)S(1)} %get-tuple-element.36), channel_id=1, source_target_pairs={{0,64},{32,96},{64,0},{96,32},{1,65},{33,97},{65,1},{97,33},{2,66}... | collective-permute-start | bytes 294920 | tf_op jit(solution)/shard_map/ppermute | solution.py:28
  76.3 4.8 %collective-permute-start.2 = (bf16[384,128]{1,0:T(8,128)(2,1)S(1)}, bf16[384,128]{1,0:T(8,128)(2,1)S(1)}, u32[]{:S(2)}, u32[]{:S(2)}) collective-permute-start(bf16[384,128]{1,0:T(8,128)(2,1)S(1)} %get-tuple-element.37), channel_id=1, source_target_pairs={{0,96},{32,64},{64,32},{96,0},{1,97},{33,65},{65,33},{97,1},{2,98}... | collective-permute-start | bytes 294920 | tf_op jit(solution)/shard_map/ppermute | solution.py:28
  81.2 0.0 collective-permute-done.dq1_ref
  81.2 0.0 collective-permute-done.1.dq2_ref
  81.2 2.3 %collective-permute-done.2.dq3_ref = bf16[384,128]{1,0:T(8,128)(2,1)S(1)} collective-permute-done((bf16[384,128]{1,0:T(8,128)(2,1)S(1)}, bf16[384,128]{1,0:T(8,128)(2,1)S(1)}, u32[]{:S(2)}, u32[]{:S(2)}) %collective-permute-start.2) | collective-permute-done | bytes 98336 | tf_op jit(solution)/shard_map/ppermute | solution.py:28
  83.5 0.0 all-to-all-done.2.dkv_ref
  83.5 0.8 shard_map.108
  84.3 22.6 %all_to_all.20.sums_ref = bf16[32,2,384]{2,1,0:T(2,128)(2,1)S(1)} all-to-all(bf16[32,2,384]{2,1,0:T(2,128)(2,1)S(1)} %get-tuple-element.38), channel_id=1, replica_groups=mesh['y'=4,'x'=4,'z'=16,'c'=2] {'z','c'}, dimensions={0} | all-to-all | bytes 98304 | tf_op jit(solution)/shard_map/all_to_all | solution.py:294
  106.9 1.0 shard_map.109
Async XLA Ops:
  0.6 18.8 %copy-start.1 = (bf16[384,128]{1,0:T(8,128)(2,1)S(1)}, bf16[384,128]{1,0:T(8,128)(2,1)}, u32[]{:S(2)}) copy-start(bf16[384,128]{1,0:T(8,128)(2,1)} %k_ref.3) | copy-start | bytes 294916
  0.6 18.8 %copy-start.2 = (bf16[384,128]{1,0:T(8,128)(2,1)S(1)}, bf16[384,128]{1,0:T(8,128)(2,1)}, u32[]{:S(2)}) copy-start(bf16[384,128]{1,0:T(8,128)(2,1)} %g_ref.1) | copy-start | bytes 294916
  2.5 17.0 %copy-start = (bf16[384,128]{1,0:T(8,128)(2,1)S(1)}, bf16[384,128]{1,0:T(8,128)(2,1)}, u32[]{:S(2)}) copy-start(bf16[384,128]{1,0:T(8,128)(2,1)} %q_ref.3) | copy-start | bytes 294916
  2.5 29.4 %all-to-all-start = ((bf16[32,2,384]{2,1,0:T(2,128)(2,1)}), bf16[32,2,384]{2,1,0:T(2,128)(2,1)S(1)}, u32[]{:S(2)}, u32[]{:S(2)}) async-start(bf16[32,2,384]{2,1,0:T(2,128)(2,1)} %shard_map.103), calls=%async_computation | async-start | bytes 98304 | tf_op jit(solution)/shard_map/all_to_all | solution.py:255
  19.4 0.7 copy-start.5
  19.4 0.7 copy-start.6
  19.4 0.7 copy-start.7
  20.1 0.9 copy-start.3
  21.0 0.9 copy-start.4
  33.0 16.4 %all-to-all-start.1 = ((bf16[4,784,128]{2,1,0:T(8,128)(2,1)}), bf16[4,784,128]{2,1,0:T(8,128)(2,1)S(1)}, u32[]{:S(2)}, u32[]{:S(2)}) async-start(bf16[4,784,128]{2,1,0:T(8,128)(2,1)} %get-tuple-element.31), calls=%async_computation.1 | async-start | bytes 1605632 | tf_op jit(solution)/shard_map/all_to_all | solution.py:270
  68.1 15.4 %all-to-all-start.2 = ((bf16[4,768,128]{2,1,0:T(8,128)(2,1)}), bf16[4,768,128]{2,1,0:T(8,128)(2,1)S(1)}, u32[]{:S(2)}, u32[]{:S(2)}) async-start(bf16[4,768,128]{2,1,0:T(8,128)(2,1)} %get-tuple-element.33), calls=%async_computation.2 | async-start | bytes 1572864 | tf_op jit(solution)/shard_map/all_to_all | solution.py:288
  71.6 9.6 %collective-permute-start = (bf16[384,128]{1,0:T(8,128)(2,1)S(1)}, bf16[384,128]{1,0:T(8,128)(2,1)S(1)}, u32[]{:S(2)}, u32[]{:S(2)}) collective-permute-start(bf16[384,128]{1,0:T(8,128)(2,1)S(1)} %get-tuple-element.35), channel_id=1, source_target_pairs={{0,32},{32,0},{64,96},{96,64},{1,33},{33,1},{65,97},{97,65},{2,34}... | collective-permute-start | bytes 294920 | tf_op jit(solution)/shard_map/ppermute | solution.py:28
  73.5 7.7 %collective-permute-start.1 = (bf16[384,128]{1,0:T(8,128)(2,1)S(1)}, bf16[384,128]{1,0:T(8,128)(2,1)S(1)}, u32[]{:S(2)}, u32[]{:S(2)}) collective-permute-start(bf16[384,128]{1,0:T(8,128)(2,1)S(1)} %get-tuple-element.36), channel_id=1, source_target_pairs={{0,64},{32,96},{64,0},{96,32},{1,65},{33,97},{65,1},{97,33},{2,66}... | collective-permute-start | bytes 294920 | tf_op jit(solution)/shard_map/ppermute | solution.py:28
  76.3 7.1 %collective-permute-start.2 = (bf16[384,128]{1,0:T(8,128)(2,1)S(1)}, bf16[384,128]{1,0:T(8,128)(2,1)S(1)}, u32[]{:S(2)}, u32[]{:S(2)}) collective-permute-start(bf16[384,128]{1,0:T(8,128)(2,1)S(1)} %get-tuple-element.37), channel_id=1, source_target_pairs={{0,96},{32,64},{64,32},{96,0},{1,97},{33,65},{65,33},{97,1},{2,98}... | collective-permute-start | bytes 294920 | tf_op jit(solution)/shard_map/ppermute | solution.py:28

commit v5 on v4

--- a/solution.py
+++ b/solution.py
@@ -152,7 +152,7 @@
 
 def grads_kernel(
     place_ref, total_ref, qall_ref, kall_ref,
-    dkv_ref, dq0_ref, dq1_ref, dq2_ref, dq3_ref,
+    inner_ref, dkv_ref, dq0_ref, dq1_ref, dq2_ref, dq3_ref,
     q_all, g_all, k_all, v_all, logs, deltas, groups, dq_acc,
 ):
     for i in range(SIDE):
@@ -166,6 +166,7 @@
         logs[:, span] = jnp.log2(total_ref[i])
     groups[...] = query_groups(qall_ref)
     dq_acc[...] = jnp.zeros_like(dq_acc)
+    inner_ref[...] = jnp.zeros_like(inner_ref)
     half = SIDE * ROWS // 2
 
     def key_pair(m, carry):
@@ -180,12 +181,15 @@
             span = slice(h * half, (h + 1) * half)
             queries = q_all[span, :]
             grad = g_all[span, :]
-            scores = dot(keys, queries, NT) * (ROOT * LOG2E)
-            upper = scores[:ROWS] - shifts[0][:, span]
-            lower = scores[ROWS:] - shifts[1][:, span]
+            scores = dot(keys, queries, NT)
+            scaled = scores * (ROOT * LOG2E)
+            upper = scaled[:ROWS] - shifts[0][:, span]
+            lower = scaled[ROWS:] - shifts[1][:, span]
             probs = jnp.exp2(jnp.concatenate([upper, lower], axis=0))
             dprobs = dot(vals, grad, NT)
-            dscores = (probs * (dprobs - deltas[:, span])).astype(BF16)
+            dscores = probs * (dprobs - deltas[:, span])
+            inner_ref[:, span] += jnp.sum(dscores * scores, axis=0, keepdims=True)
+            dscores = dscores.astype(BF16)
             dq_acc[:, span] += dot(keys, dscores, TN)
             return dot(dscores, queries), dot(probs.astype(BF16), grad)
 
@@ -198,6 +202,7 @@
         return carry
 
     lax.fori_loop(0, SIDE // 2, key_pair, 0)
+    inner_ref[...] = inner_ref[...] * ROOT
     x = place_ref[1]
     for d, ref in enumerate((dq0_ref, dq1_ref, dq2_ref, dq3_ref)):
         span = pl.ds(pl.multiple_of((x ^ d) * ROWS, ROWS), ROWS)
@@ -205,41 +210,48 @@
 
 
 def sums_kernel(
-    dkv_ref, dq0_ref, dq1_ref, dq2_ref, dq3_ref, q_ref, k_ref, qscale_ref, kscale_ref,
-    gq_ref, gk_ref, dv_ref, msg_ref,
-):
-    parts = (dq0_ref, dq1_ref, dq2_ref, dq3_ref)
-    q_lines = []
+    place_ref, inner_ref, dkv_ref, dq1_ref, dq2_ref, dq3_ref, k_ref, kscale_ref,
+    gk_ref, dv_ref, msg_ref, out1_ref, out2_ref, out3_ref,
+):
     k_lines = []
     for i in range(PIECES):
         rows = pl.ds(i * WIDTH, WIDTH)
         later = pl.ds(ROWS + i * WIDTH, WIDTH)
-        gq = sum(part[rows, :].astype(F32) for part in parts) * qscale_ref[...]
         gk = sum(dkv_ref[j, rows, :].astype(F32) for j in range(SIDE)) * kscale_ref[...]
-        gq_ref[rows, :] = gq
         gk_ref[rows, :] = gk
         dv_ref[rows, :] = sum(dkv_ref[j, later, :].astype(F32) for j in range(SIDE)).astype(BF16)
-        q_lines.append(row_sums(gq * q_ref[rows, :].astype(F32)))
         k_lines.append(row_sums(gk * k_ref[rows, :].astype(F32)))
-    both = [jnp.concatenate(lines, axis=1) for lines in (q_lines, k_lines)]
-    coded = jnp.concatenate(both, axis=0).astype(BF16)
+    q_line = jnp.zeros((1, ROWS), F32)
+    for i in range(SIDE):
+        q_line = jnp.where(place_ref[1] == i, inner_ref[:, i * ROWS : (i + 1) * ROWS], q_line)
+    coded = jnp.concatenate([q_line, jnp.concatenate(k_lines, axis=1)], axis=0).astype(BF16)
     for h in range(HEADS):
         msg_ref[h] = coded
-
-
-def final_kernel(sums_ref, rate_ref, gq_ref, gk_ref, q_ref, k_ref, dq_ref, dk_ref):
+    for source, target in ((dq1_ref, out1_ref), (dq2_ref, out2_ref), (dq3_ref, out3_ref)):
+        target[...] = source[...]
+
+
+def final_kernel(
+    sums_ref, rate_ref, dq0_ref, dq1_ref, dq2_ref, dq3_ref, gk_ref, q_ref, k_ref, qscale_ref,
+    dq_ref, dk_ref,
+):
     inner = jnp.zeros((2, ROWS), F32)
     for h in range(HEADS):
         inner = inner + sums_ref[h].astype(F32)
     rate = rate_ref[...]
-    weight = rate * rate * rate * inner / (HEADS * WIDTH)
-    for n, (g_ref, raw_ref, out_ref) in enumerate(((gq_ref, q_ref, dq_ref), (gk_ref, k_ref, dk_ref))):
-        for i in range(PIECES):
-            rows = pl.ds(i * WIDTH, WIDTH)
-            span = slice(i * WIDTH, (i + 1) * WIDTH)
-            raw = raw_ref[rows, :].astype(F32)
-            out = column(rate[n : n + 1, span]) * g_ref[rows, :] - raw * column(weight[n : n + 1, span])
-            out_ref[rows, :] = out.astype(BF16)
+    weight = rate * rate * inner / (HEADS * WIDTH)
+    q_weight = weight[0:1, :]
+    k_weight = weight[1:2, :] * rate[1:2, :]
+    for i in range(PIECES):
+        rows = pl.ds(i * WIDTH, WIDTH)
+        span = slice(i * WIDTH, (i + 1) * WIDTH)
+        gq = sum(part[rows, :].astype(F32) for part in (dq0_ref, dq1_ref, dq2_ref, dq3_ref))
+        gq = gq * qscale_ref[...]
+        gk = gk_ref[rows, :]
+        q = q_ref[rows, :].astype(F32)
+        k = k_ref[rows, :].astype(F32)
+        dq_ref[rows, :] = (column(rate[0:1, span]) * gq - q * column(q_weight[:, span])).astype(BF16)
+        dk_ref[rows, :] = (column(rate[1:2, span]) * gk - k * column(k_weight[:, span])).astype(BF16)
 
 
 def local(q_raw, k_raw, values, out, d_out, q_gain, k_gain, order):
@@ -279,20 +291,26 @@
 
     tall = pltpu.VMEM((SIDE * ROWS, WIDTH), BF16)
     row = pltpu.VMEM((1, SIDE * ROWS), F32)
-    keys, *queries = call(
+    inner, keys, *queries = call(
         grads_kernel,
-        (struct((SIDE, 2 * ROWS, WIDTH), BF16), block, block, block, block),
+        (
+            struct((1, SIDE * ROWS), F32),
+            struct((SIDE, 2 * ROWS, WIDTH), BF16),
+            block, block, block, block,
+        ),
         scratch=(tall, tall, tall, tall, row, row, row, pltpu.VMEM((WIDTH, SIDE * ROWS), F32)),
         spaces="s",
     )(place, totals, queries, keys)
     keys = lax.all_to_all(keys, "y", 0, 0)
+    inner = lax.psum(inner, "x")
+    gk, dv, inner, *queries[1:] = call(
+        sums_kernel, (wide, block, message, block, block, block), spaces="s"
+    )(place, inner, keys, *queries[1:], k_raw, k_gain)
+    inner = lax.all_to_all(inner, HEAD, 0, 0)
     queries[1:] = [swap(part, "x", d) for d, part in enumerate(queries[1:], 1)]
-
-    gq, gk, dv, inner = call(
-        sums_kernel, (wide, wide, block, message)
-    )(keys, *queries, q_raw, k_raw, q_gain, k_gain)
-    inner = lax.all_to_all(inner, HEAD, 0, 0)
-    d_q, d_k = call(final_kernel, (block, block))(inner, rate, gq, gk, q_raw, k_raw)
+    d_q, d_k = call(final_kernel, (block, block))(
+        inner, rate, *queries, gk, q_raw, k_raw, q_gain
+    )
     return d_q, d_k, dv
 
 

time: 109 us -> 107 us (0.982)
  blocking collectives: 43.9 us -> 27.4 us
  starting transfers between devices: 34 us -> 44.8 us
  waiting for transfers between devices: 11.5 us -> 14.5 us
  Pallas kernels: 15.1 us -> 16.3 us
    all_to_all x1 -> x0, blocking collectives: 22.6 us -> none  [local(): inner = lax.all_to_all(inner, HEAD, 0, 0)]
    all_to_all x0 -> x1, starting transfers between devices: none -> 10.9 us  [local(): inner = lax.all_to_all(inner, HEAD, 0, 0)]
    psum x0 -> x1, blocking collectives: none -> 6.1 us  [local(): inner = lax.psum(inner, 'x')]
    all_to_all x1, waiting for transfers between devices: 0.01 us -> 2.2 us  [local(): keys = lax.all_to_all(keys, 'y', 0, 0)]
    pallas_call x7, Pallas kernels: 15.1 us -> 16.3 us  [run(): pl.pallas_call(kernel, out_shape=out_shape, in_specs=specs, out_specs=jax...]
  transfers between devices with their start and end apart: 6 -> 7, of which waited for: 2 -> 4; matrix products, arithmetic and copies ran while one was open for 0% -> 0% of each run, Pallas kernels for 1% -> 1%
where the time goes in v5:
time: 107 us; the launch traced here: 106 us
  starting transfers between devices  44.8 us (42%)
  blocking collectives  27.4 us (26%)
  Pallas kernels  16.3 us (15%)
  waiting for transfers between devices  14.5 us (14%)
  local copies, waits for them, and re-layouts  2.46 us (2%)
    all_to_all x1, starting transfers between devices, local(): squares = lax.all_to_all(squares, HEAD, 0, 0)  16.9 us
    pallas_call x7, Pallas kernels, run(): pl.pallas_call(kernel, out_shape=out_shape, in_specs=specs, out_specs=jax...  16.3 us
    all_gather x1, blocking collectives, local(): lax.all_gather(keys, 'y', axis=0, tiled=True)  12.4 us
    all_to_all x1, starting transfers between devices, local(): inner = lax.all_to_all(inner, HEAD, 0, 0)  10.9 us
    ppermute x3, starting transfers between devices, swap(): return lax.ppermute(value, axis, [(i, i ^ mask) for i in range(SIDE)])  9.58 us
    all_to_all x1, waiting for transfers between devices, local(): squares = lax.all_to_all(squares, HEAD, 0, 0)  9.27 us
    psum x1, blocking collectives, local(): totals = lax.psum(totals, 'x')  8.96 us
    psum x1, blocking collectives, local(): inner = lax.psum(inner, 'x')  6.1 us
  transfers between devices with their start and end apart: 7, of which 4 were waited for; matrix products, arithmetic and copies ran while one was open for 0% of the time, Pallas kernels for 1%

profile of v5, /device:TPU:1, one launch (start us, length us, event | category | flops | bytes accessed | tf_op | source)
XLA Modules:
  0.0 106.4 jit_solution(658313359388329011)
XLA Ops:
  0.6 0.0 copy-start.1
  0.6 0.0 copy-start.2
  0.7 1.8 %shard_map.103 = bf16[32,2,384]{2,1,0:T(2,128)(2,1)} custom-call(bf16[384,128]{1,0:T(8,128)(2,1)} %q_ref.3, bf16[384,128]{1,0:T(8,128)(2,1)} %k_ref.3), custom_call_target="tpu_custom_call" | custom-call | tf_op jit(solution)/shard_map/pallas_call | solution.py:39
  2.5 0.0 copy-start
  2.5 16.9 %all-to-all-start = ((bf16[32,2,384]{2,1,0:T(2,128)(2,1)}), bf16[32,2,384]{2,1,0:T(2,128)(2,1)S(1)}, u32[]{:S(2)}, u32[]{:S(2)}) async-start(bf16[32,2,384]{2,1,0:T(2,128)(2,1)} %shard_map.103), calls=%async_computation | async-start | bytes 98304 | tf_op jit(solution)/shard_map/all_to_all | solution.py:267
  19.3 0.1 pad_add_fusion.place_ref
  19.4 0.0 copy-start.5
  19.4 0.0 copy-start.6
  19.4 0.0 copy-start.7
  19.4 0.0 copy-done.1
  19.4 0.0 copy-done.2
  19.4 0.0 copy-done
  19.5 0.6 copy-done.5
  20.1 0.0 copy-done.6
  20.1 0.0 copy-done.7
  20.1 0.0 copy-start.3
  20.1 0.9 copy-done.3
  21.0 0.0 copy-start.4
  21.0 0.9 copy-done.4
  21.9 0.7 shard_map.104
  22.6 9.3 %all-to-all-done.sums_ref = bf16[32,2,384]{2,1,0:T(2,128)(2,1)S(1)} async-done(((bf16[32,2,384]{2,1,0:T(2,128)(2,1)}), bf16[32,2,384]{2,1,0:T(2,128)(2,1)S(1)}, u32[]{:S(2)}, u32[]{:S(2)}) %all-to-all-start) | async-done | bytes 49184 | tf_op jit(solution)/shard_map/all_to_all | solution.py:267
  31.8 1.2 %shard_map.105 = (f32[2,384]{1,0:T(2,128)S(1)}, bf16[4,784,128]{2,1,0:T(8,128)(2,1)}, bf16[784,128]{1,0:T(8,128)(2,1)S(1)}) custom-call(bf16[32,2,384]{2,1,0:T(2,128)(2,1)S(1)} %all-to-all-done.sums_ref, bf16[384,128]{1,0:T(8,128)(2,1)S(1)} %get-tuple-element.27.q_ref, bf16[384,128]{1,0:T(8,128)(2,1)S(1)} %get-tuple-element.28.k_ref, ...), custom_call_target="tpu_custom_call" | custom-call | tf_op jit(solution)/shard_map/pallas_call | solution.py:39
  33.0 4.0 %all-to-all-start.1 = ((bf16[4,784,128]{2,1,0:T(8,128)(2,1)}), bf16[4,784,128]{2,1,0:T(8,128)(2,1)S(1)}, u32[]{:S(2)}, u32[]{:S(2)}) async-start(bf16[4,784,128]{2,1,0:T(8,128)(2,1)} %get-tuple-element.34), calls=%async_computation.1 | async-start | bytes 1605632 | tf_op jit(solution)/shard_map/all_to_all | solution.py:282
  37.0 12.4 %all_gather.3 = bf16[3136,128]{1,0:T(8,128)(2,1)S(1)} all-gather(bf16[784,128]{1,0:T(8,128)(2,1)S(1)} %get-tuple-element.35), channel_id=1, replica_groups=mesh['y'=4,'x'=4,'z'=16,'c'=2] {'y'}, dimensions={0}, use_global_device_ids=true | all-gather | bytes 1003520 | tf_op jit(solution)/shard_map/all_gather | solution.py:283
  49.4 0.0 all-to-all-done.1.qall_ref
  49.4 2.0 %shard_map.106 = f32[4,1,384]{2,1,0:T(1,128)S(1)} custom-call(bf16[4,784,128]{2,1,0:T(8,128)(2,1)S(1)} %all-to-all-done.1.qall_ref, bf16[4,784,128]{2,1,0:T(8,128)(2,1)S(1)} %bitcast.5), custom_call_target="tpu_custom_call" | custom-call | tf_op jit(solution)/shard_map/pallas_call | solution.py:39
  51.4 9.0 %psum.14.total_ref = f32[4,1,384]{2,1,0:T(1,128)S(1)} all-reduce(f32[4,1,384]{2,1,0:T(1,128)S(1)} %shard_map.106), channel_id=1, replica_groups=mesh['y'=4,'x'=4,'z'=16,'c'=2] {'x'}, use_global_device_ids=true, to_apply=%region_0.0 | all-reduce | flops 1536 | bytes 12288 | tf_op jit(solution)/shard_map/psum | solution.py:290
  60.4 8.4 %shard_map.107 = (f32[1,1536]{1,0:T(1,128)S(1)}, bf16[4,768,128]{2,1,0:T(8,128)(2,1)}, bf16[384,128]{1,0:T(8,128)(2,1)S(1)}, bf16[384,128]{1,0:T(8,128)(2,1)S(1)...) custom-call(s32[2]{0:T(128)S(1)} %pad_add_fusion.place_ref, f32[4,1,384]{2,1,0:T(1,128)S(1)} %psum.14.total_ref, ...), custom_call_target="tpu_custom_call" | custom-call | tf_op jit(solution)/shard_map/pallas_call | solution.py:39
  68.8 3.5 %all-to-all-start.2 = ((bf16[4,768,128]{2,1,0:T(8,128)(2,1)}), bf16[4,768,128]{2,1,0:T(8,128)(2,1)S(1)}, u32[]{:S(2)}, u32[]{:S(2)}) async-start(bf16[4,768,128]{2,1,0:T(8,128)(2,1)} %get-tuple-element.37), calls=%async_computation.2 | async-start | bytes 1572864 | tf_op jit(solution)/shard_map/all_to_all | solution.py:304
  72.3 6.1 %psum.15.inner_ref = f32[1,1536]{1,0:T(1,128)S(1)} all-reduce(f32[1,1536]{1,0:T(1,128)S(1)} %get-tuple-element.36), channel_id=1, replica_groups=mesh['y'=4,'x'=4,'z'=16,'c'=2] {'x'}, use_global_device_ids=true, to_apply=%region_1.0 | all-reduce | flops 1536 | bytes 12288 | tf_op jit(solution)/shard_map/psum | solution.py:305
  78.4 2.2 %all-to-all-done.2.dkv_ref = bf16[4,768,128]{2,1,0:T(8,128)(2,1)S(1)} async-done(((bf16[4,768,128]{2,1,0:T(8,128)(2,1)}), bf16[4,768,128]{2,1,0:T(8,128)(2,1)S(1)}, u32[]{:S(2)}, u32[]{:S(2)}) %all-to-all-start.2) | async-done | bytes 786464 | tf_op jit(solution)/shard_map/all_to_all | solution.py:304
  80.6 1.3 %shard_map.108 = (f32[384,128]{1,0:T(8,128)S(1)}, bf16[384,128]{1,0:T(8,128)(2,1)}, bf16[32,2,384]{2,1,0:T(2,128)(2,1)}, bf16[384,128]{1,0:T(8,128)(2,1)S(1)}, b...) custom-call(s32[2]{0:T(128)S(1)} %pad_add_fusion.place_ref, f32[1,1536]{1,0:T(1,128)S(1)} %psum.15.inner_ref, ...), custom_call_target="tpu_custom_call" | custom-call | tf_op jit(solution)/shard_map/pallas_call | solution.py:39
  81.9 10.9 %all-to-all-start.3 = ((bf16[32,2,384]{2,1,0:T(2,128)(2,1)}), bf16[32,2,384]{2,1,0:T(2,128)(2,1)S(1)}, u32[]{:S(2)}, u32[]{:S(2)}) async-start(bf16[32,2,384]{2,1,0:T(2,128)(2,1)} %get-tuple-element.41), calls=%async_computation.3 | async-start | bytes 98304 | tf_op jit(solution)/shard_map/all_to_all | solution.py:309
  92.8 2.0 %collective-permute-start = (bf16[384,128]{1,0:T(8,128)(2,1)S(1)}, bf16[384,128]{1,0:T(8,128)(2,1)S(1)}, u32[]{:S(2)}, u32[]{:S(2)}) collective-permute-start(bf16[384,128]{1,0:T(8,128)(2,1)S(1)} %get-tuple-element.44), channel_id=1, source_target_pairs={{0,32},{32,0},{64,96},{96,64},{1,33},{33,1},{65,97},{97,65},{2,34}... | collective-permute-start | bytes 294920 | tf_op jit(solution)/shard_map/ppermute | solution.py:28
  94.8 3.1 %collective-permute-start.1 = (bf16[384,128]{1,0:T(8,128)(2,1)S(1)}, bf16[384,128]{1,0:T(8,128)(2,1)S(1)}, u32[]{:S(2)}, u32[]{:S(2)}) collective-permute-start(bf16[384,128]{1,0:T(8,128)(2,1)S(1)} %get-tuple-element.45), channel_id=1, source_target_pairs={{0,64},{32,96},{64,0},{96,32},{1,65},{33,97},{65,1},{97,33},{2,66}... | collective-permute-start | bytes 294920 | tf_op jit(solution)/shard_map/ppermute | solution.py:28
  97.9 4.5 %collective-permute-start.2 = (bf16[384,128]{1,0:T(8,128)(2,1)S(1)}, bf16[384,128]{1,0:T(8,128)(2,1)S(1)}, u32[]{:S(2)}, u32[]{:S(2)}) collective-permute-start(bf16[384,128]{1,0:T(8,128)(2,1)S(1)} %get-tuple-element.46), channel_id=1, source_target_pairs={{0,96},{32,64},{64,32},{96,0},{1,97},{33,65},{65,33},{97,1},{2,98}... | collective-permute-start | bytes 294920 | tf_op jit(solution)/shard_map/ppermute | solution.py:28
  102.4 0.0 collective-permute-done.dq1_ref
  102.4 0.0 collective-permute-done.1.dq2_ref
  102.4 2.3 %collective-permute-done.2.dq3_ref = bf16[384,128]{1,0:T(8,128)(2,1)S(1)} collective-permute-done((bf16[384,128]{1,0:T(8,128)(2,1)S(1)}, bf16[384,128]{1,0:T(8,128)(2,1)S(1)}, u32[]{:S(2)}, u32[]{:S(2)}) %collective-permute-start.2) | collective-permute-done | bytes 98336 | tf_op jit(solution)/shard_map/ppermute | solution.py:28
  104.7 0.7 all-to-all-done.3.sums_ref
  105.5 1.0 shard_map.109
Async XLA Ops:
  0.6 18.8 %copy-start.1 = (bf16[384,128]{1,0:T(8,128)(2,1)S(1)}, bf16[384,128]{1,0:T(8,128)(2,1)}, u32[]{:S(2)}) copy-start(bf16[384,128]{1,0:T(8,128)(2,1)} %k_ref.3) | copy-start | bytes 294916
  0.6 18.8 %copy-start.2 = (bf16[384,128]{1,0:T(8,128)(2,1)S(1)}, bf16[384,128]{1,0:T(8,128)(2,1)}, u32[]{:S(2)}) copy-start(bf16[384,128]{1,0:T(8,128)(2,1)} %g_ref.1) | copy-start | bytes 294916
  2.5 17.0 %copy-start = (bf16[384,128]{1,0:T(8,128)(2,1)S(1)}, bf16[384,128]{1,0:T(8,128)(2,1)}, u32[]{:S(2)}) copy-start(bf16[384,128]{1,0:T(8,128)(2,1)} %q_ref.3) | copy-start | bytes 294916
  2.5 29.4 %all-to-all-start = ((bf16[32,2,384]{2,1,0:T(2,128)(2,1)}), bf16[32,2,384]{2,1,0:T(2,128)(2,1)S(1)}, u32[]{:S(2)}, u32[]{:S(2)}) async-start(bf16[32,2,384]{2,1,0:T(2,128)(2,1)} %shard_map.103), calls=%async_computation | async-start | bytes 98304 | tf_op jit(solution)/shard_map/all_to_all | solution.py:267
  19.4 0.7 copy-start.5
  19.4 0.7 copy-start.6
  19.4 0.7 copy-start.7
  20.1 0.9 copy-start.3
  21.0 0.9 copy-start.4
  33.0 16.4 %all-to-all-start.1 = ((bf16[4,784,128]{2,1,0:T(8,128)(2,1)}), bf16[4,784,128]{2,1,0:T(8,128)(2,1)S(1)}, u32[]{:S(2)}, u32[]{:S(2)}) async-start(bf16[4,784,128]{2,1,0:T(8,128)(2,1)} %get-tuple-element.34), calls=%async_computation.1 | async-start | bytes 1605632 | tf_op jit(solution)/shard_map/all_to_all | solution.py:282
  68.8 11.8 %all-to-all-start.2 = ((bf16[4,768,128]{2,1,0:T(8,128)(2,1)}), bf16[4,768,128]{2,1,0:T(8,128)(2,1)S(1)}, u32[]{:S(2)}, u32[]{:S(2)}) async-start(bf16[4,768,128]{2,1,0:T(8,128)(2,1)} %get-tuple-element.37), calls=%async_computation.2 | async-start | bytes 1572864 | tf_op jit(solution)/shard_map/all_to_all | solution.py:304
  81.9 23.6 %all-to-all-start.3 = ((bf16[32,2,384]{2,1,0:T(2,128)(2,1)}), bf16[32,2,384]{2,1,0:T(2,128)(2,1)S(1)}, u32[]{:S(2)}, u32[]{:S(2)}) async-start(bf16[32,2,384]{2,1,0:T(2,128)(2,1)} %get-tuple-element.41), calls=%async_computation.3 | async-start | bytes 98304 | tf_op jit(solution)/shard_map/all_to_all | solution.py:309
  92.8 9.6 %collective-permute-start = (bf16[384,128]{1,0:T(8,128)(2,1)S(1)}, bf16[384,128]{1,0:T(8,128)(2,1)S(1)}, u32[]{:S(2)}, u32[]{:S(2)}) collective-permute-start(bf16[384,128]{1,0:T(8,128)(2,1)S(1)} %get-tuple-element.44), channel_id=1, source_target_pairs={{0,32},{32,0},{64,96},{96,64},{1,33},{33,1},{65,97},{97,65},{2,34}... | collective-permute-start | bytes 294920 | tf_op jit(solution)/shard_map/ppermute | solution.py:28
  94.8 7.6 %collective-permute-start.1 = (bf16[384,128]{1,0:T(8,128)(2,1)S(1)}, bf16[384,128]{1,0:T(8,128)(2,1)S(1)}, u32[]{:S(2)}, u32[]{:S(2)}) collective-permute-start(bf16[384,128]{1,0:T(8,128)(2,1)S(1)} %get-tuple-element.45), channel_id=1, source_target_pairs={{0,64},{32,96},{64,0},{96,32},{1,65},{33,97},{65,1},{97,33},{2,66}... | collective-permute-start | bytes 294920 | tf_op jit(solution)/shard_map/ppermute | solution.py:28
  97.9 6.9 %collective-permute-start.2 = (bf16[384,128]{1,0:T(8,128)(2,1)S(1)}, bf16[384,128]{1,0:T(8,128)(2,1)S(1)}, u32[]{:S(2)}, u32[]{:S(2)}) collective-permute-start(bf16[384,128]{1,0:T(8,128)(2,1)S(1)} %get-tuple-element.46), channel_id=1, source_target_pairs={{0,96},{32,64},{64,32},{96,0},{1,97},{33,65},{65,33},{97,1},{2,98}... | collective-permute-start | bytes 294920 | tf_op jit(solution)/shard_map/ppermute | solution.py:28

commit v6 on v5

--- a/solution.py
+++ b/solution.py
@@ -32,15 +32,19 @@
     return jax.ShapeDtypeStruct(shape, dtype)
 
 
-def call(kernel, out_shape, scratch=(), spaces="", limit=32):
+def call(kernel, out_shape, scratch=(), spaces="", out_spaces="", limit=32):
     def run(*args):
-        memory = {"s": pltpu.SMEM, "v": pltpu.VMEM}
+        memory = {"s": pltpu.SMEM, "v": pltpu.VMEM, "h": pltpu.HBM}
+        leaves, tree = jax.tree.flatten(out_shape)
+        out_specs = [
+            pl.BlockSpec(memory_space=memory[s]) for s in out_spaces.ljust(len(leaves), "v")
+        ]
         specs = [pl.BlockSpec(memory_space=memory[s]) for s in spaces.ljust(len(args), "v")]
         return pl.pallas_call(
             kernel,
             out_shape=out_shape,
             in_specs=specs,
-            out_specs=jax.tree.map(lambda _: pl.BlockSpec(memory_space=pltpu.VMEM), out_shape),
+            out_specs=jax.tree.unflatten(tree, out_specs),
             scratch_shapes=scratch,
             compiler_params=pltpu.CompilerParams(vmem_limit_bytes=limit * 2**20),
         )(*args)
@@ -76,8 +80,8 @@
 
 
 def ready_kernel(
-    place_ref, order_ref, q_ref, k_ref, g_ref, v_ref, o_ref, qgain_ref, kgain_ref,
-    q_out, k_out, g_out, v_out, lines_ref, qscale_ref, kscale_ref,
+    place_ref, order_ref, g_ref, o_ref, v_ref, qgain_ref, kgain_ref,
+    g_out, v_out, lines_ref, qscale_ref, kscale_ref,
 ):
     group = order_ref[place_ref[0] * SIDE + place_ref[1]].astype(F32)
     line = lax.broadcasted_iota(jnp.int32, (LINES, WIDTH), 0)
@@ -89,36 +93,50 @@
         lines = jnp.where(line == i, high, lines)
         lines = jnp.where(line == PIECES + i, delta - high, lines)
     lines_ref[...] = lines.astype(BF16)
-    for source, target in ((q_ref, q_out), (k_ref, k_out), (g_ref, g_out), (v_ref, v_out)):
-        target[...] = source[...]
+    g_out[...] = g_ref[...]
+    v_out[...] = v_ref[...]
     qscale_ref[...] = qgain_ref[...].astype(F32)
     kscale_ref[...] = kgain_ref[...].astype(F32)
 
 
 def norms_kernel(
     sums_ref, q_ref, k_ref, g_ref, v_ref, lines_ref, qscale_ref, kscale_ref,
-    rate_ref, qmsg_ref, kmsg_ref,
-):
+    rate_ref, qmsg_hbm, kmsg_ref, q_buf, sems,
+):
+    early = pl.ds(ROWS, ROWS + LINES)
+    late = pl.ds(0, ROWS)
+    copies = [
+        [
+            pltpu.make_async_copy(q_buf.at[rows, :], qmsg_hbm.at[x, rows, :], sems.at[n, x])
+            for x in range(SIDE)
+        ]
+        for n, rows in enumerate((early, late))
+    ]
+    q_buf[ROWS : 2 * ROWS, :] = g_ref[...]
+    q_buf[2 * ROWS :, :] = lines_ref[...]
+    for copy in copies[0]:
+        copy.start()
     total = jnp.zeros((2, ROWS), F32)
     for h in range(HEADS):
-        total = total + jnp.sqrt(jnp.sqrt(jnp.maximum(sums_ref[h].astype(F32), 1e-36)))
+        total = total + lax.rsqrt(lax.rsqrt(jnp.maximum(sums_ref[h].astype(F32), 1e-36)))
     rate = lax.rsqrt(total / (HEADS * WIDTH) + EPSILON)
     rate_ref[...] = rate
     for i in range(PIECES):
         rows = pl.ds(i * WIDTH, WIDTH)
-        later = pl.ds(ROWS + i * WIDTH, WIDTH)
         span = slice(i * WIDTH, (i + 1) * WIDTH)
         q = q_ref[rows, :].astype(F32) * column(rate[0:1, span]) * qscale_ref[...]
+        q_buf[rows, :] = q.astype(BF16)
+    for copy in copies[1]:
+        copy.start()
+    for i in range(PIECES):
+        rows = pl.ds(i * WIDTH, WIDTH)
+        span = slice(i * WIDTH, (i + 1) * WIDTH)
         k = k_ref[rows, :].astype(F32) * column(rate[1:2, span]) * kscale_ref[...]
-        q = q.astype(BF16)
-        for x in range(SIDE):
-            qmsg_ref[x, rows, :] = q
-            qmsg_ref[x, later, :] = g_ref[rows, :]
         kmsg_ref[rows, :] = k.astype(BF16)
-        kmsg_ref[later, :] = v_ref[rows, :]
-    for x in range(SIDE):
-        qmsg_ref[x, 2 * ROWS :, :] = lines_ref[...]
+    kmsg_ref[ROWS : 2 * ROWS, :] = v_ref[...]
     kmsg_ref[2 * ROWS :, :] = lines_ref[...]
+    for copy in copies[0] + copies[1]:
+        copy.wait()
 
 
 def across(lines, first):
@@ -151,9 +169,9 @@
 
 
 def grads_kernel(
-    place_ref, total_ref, qall_ref, kall_ref,
-    inner_ref, dkv_ref, dq0_ref, dq1_ref, dq2_ref, dq3_ref,
-    q_all, g_all, k_all, v_all, logs, deltas, groups, dq_acc,
+    total_ref, qall_ref, kall_ref,
+    inner_ref, dkv_hbm, dq_ref,
+    q_all, g_all, k_all, v_all, logs, deltas, groups, dq_acc, dkv_buf, sems,
 ):
     for i in range(SIDE):
         span = slice(i * ROWS, (i + 1) * ROWS)
@@ -166,8 +184,11 @@
         logs[:, span] = jnp.log2(total_ref[i])
     groups[...] = query_groups(qall_ref)
     dq_acc[...] = jnp.zeros_like(dq_acc)
-    inner_ref[...] = jnp.zeros_like(inner_ref)
     half = SIDE * ROWS // 2
+
+    def leave(m):
+        pair = pl.ds(2 * m, 2)
+        return pltpu.make_async_copy(dkv_buf.at[pair], dkv_hbm.at[pair], sems.at[m])
 
     def key_pair(m, carry):
         rows = pl.ds(pl.multiple_of(m * half, half), half)
@@ -181,15 +202,12 @@
             span = slice(h * half, (h + 1) * half)
             queries = q_all[span, :]
             grad = g_all[span, :]
-            scores = dot(keys, queries, NT)
-            scaled = scores * (ROOT * LOG2E)
-            upper = scaled[:ROWS] - shifts[0][:, span]
-            lower = scaled[ROWS:] - shifts[1][:, span]
+            scores = dot(keys, queries, NT) * (ROOT * LOG2E)
+            upper = scores[:ROWS] - shifts[0][:, span]
+            lower = scores[ROWS:] - shifts[1][:, span]
             probs = jnp.exp2(jnp.concatenate([upper, lower], axis=0))
             dprobs = dot(vals, grad, NT)
-            dscores = probs * (dprobs - deltas[:, span])
-            inner_ref[:, span] += jnp.sum(dscores * scores, axis=0, keepdims=True)
-            dscores = dscores.astype(BF16)
+            dscores = (probs * (dprobs - deltas[:, span])).astype(BF16)
             dq_acc[:, span] += dot(keys, dscores, TN)
             return dot(dscores, queries), dot(probs.astype(BF16), grad)
 
@@ -197,29 +215,31 @@
         dk = ((first[0] + second[0]) * ROOT).astype(BF16)
         dv = (first[1] + second[1]).astype(BF16)
         for n in range(2):
-            dkv_ref[2 * m + n, :ROWS, :] = dk[n * ROWS : (n + 1) * ROWS]
-            dkv_ref[2 * m + n, ROWS:, :] = dv[n * ROWS : (n + 1) * ROWS]
+            dkv_buf[2 * m + n, :ROWS, :] = dk[n * ROWS : (n + 1) * ROWS]
+            dkv_buf[2 * m + n, ROWS:, :] = dv[n * ROWS : (n + 1) * ROWS]
+        leave(m).start()
         return carry
 
     lax.fori_loop(0, SIDE // 2, key_pair, 0)
-    inner_ref[...] = inner_ref[...] * ROOT
-    x = place_ref[1]
-    for d, ref in enumerate((dq0_ref, dq1_ref, dq2_ref, dq3_ref)):
-        span = pl.ds(pl.multiple_of((x ^ d) * ROWS, ROWS), ROWS)
-        ref[...] = (dq_acc[:, span].T * ROOT).astype(BF16)
+    for p in range(SIDE * PIECES):
+        span = slice(p * WIDTH, (p + 1) * WIDTH)
+        product = dq_acc[:, span] * q_all[span, :].astype(F32).T
+        inner_ref[:, span] = jnp.sum(product, axis=0, keepdims=True) * ROOT
+    for i in range(SIDE):
+        dq_ref[i] = (dq_acc[:, i * ROWS : (i + 1) * ROWS].T * ROOT).astype(BF16)
+    for m in range(SIDE // 2):
+        leave(m).wait()
 
 
 def sums_kernel(
-    place_ref, inner_ref, dkv_ref, dq1_ref, dq2_ref, dq3_ref, k_ref, kscale_ref,
-    gk_ref, dv_ref, msg_ref, out1_ref, out2_ref, out3_ref,
+    place_ref, inner_ref, dkv_ref, dq_ref, k_ref, kscale_ref,
+    gk_ref, msg_ref, out0_ref, out1_ref, out2_ref, out3_ref,
 ):
     k_lines = []
     for i in range(PIECES):
         rows = pl.ds(i * WIDTH, WIDTH)
-        later = pl.ds(ROWS + i * WIDTH, WIDTH)
         gk = sum(dkv_ref[j, rows, :].astype(F32) for j in range(SIDE)) * kscale_ref[...]
         gk_ref[rows, :] = gk
-        dv_ref[rows, :] = sum(dkv_ref[j, later, :].astype(F32) for j in range(SIDE)).astype(BF16)
         k_lines.append(row_sums(gk * k_ref[rows, :].astype(F32)))
     q_line = jnp.zeros((1, ROWS), F32)
     for i in range(SIDE):
@@ -227,8 +247,12 @@
     coded = jnp.concatenate([q_line, jnp.concatenate(k_lines, axis=1)], axis=0).astype(BF16)
     for h in range(HEADS):
         msg_ref[h] = coded
-    for source, target in ((dq1_ref, out1_ref), (dq2_ref, out2_ref), (dq3_ref, out3_ref)):
-        target[...] = source[...]
+    for d, target in enumerate((out0_ref, out1_ref, out2_ref, out3_ref)):
+        target[...] = dq_ref[place_ref[1] ^ d]
+
+
+def values_kernel(dkv_ref, dv_ref):
+    dv_ref[...] = sum(dkv_ref[j, ROWS:, :].astype(F32) for j in range(SIDE)).astype(BF16)
 
 
 def final_kernel(
@@ -266,11 +290,11 @@
     squares = call(squares_kernel, message, limit=60)(q_raw, k_raw)
     squares = lax.all_to_all(squares, HEAD, 0, 0)
     gain = struct((1, WIDTH), F32)
-    q_raw, k_raw, d_out, values, lines, q_gain, k_gain = call(
+    d_out, values, lines, q_gain, k_gain = call(
         ready_kernel,
-        (block, block, block, block, struct((LINES, WIDTH), BF16), gain, gain),
+        (block, block, struct((LINES, WIDTH), BF16), gain, gain),
         spaces="ss",
-    )(place, order, q_raw, k_raw, d_out, values, out, q_gain, k_gain)
+    )(place, order, d_out, out, values, q_gain, k_gain)
     rate, queries, keys = call(
         norms_kernel,
         (
@@ -278,6 +302,11 @@
             struct((SIDE, 2 * ROWS + LINES, WIDTH), BF16),
             struct((2 * ROWS + LINES, WIDTH), BF16),
         ),
+        scratch=(
+            pltpu.VMEM((2 * ROWS + LINES, WIDTH), BF16),
+            pltpu.SemaphoreType.DMA((2, SIDE)),
+        ),
+        out_spaces="vh",
     )(squares, q_raw, k_raw, d_out, values, lines, q_gain, k_gain)
     queries = lax.all_to_all(queries, "x", 0, 0)
     keys = lax.all_gather(keys, "y", axis=0, tiled=True).reshape(SIDE, 2 * ROWS + LINES, WIDTH)
@@ -291,21 +320,27 @@
 
     tall = pltpu.VMEM((SIDE * ROWS, WIDTH), BF16)
     row = pltpu.VMEM((1, SIDE * ROWS), F32)
-    inner, keys, *queries = call(
+    inner, keys, queries = call(
         grads_kernel,
         (
             struct((1, SIDE * ROWS), F32),
             struct((SIDE, 2 * ROWS, WIDTH), BF16),
-            block, block, block, block,
+            struct((SIDE, ROWS, WIDTH), BF16),
         ),
-        scratch=(tall, tall, tall, tall, row, row, row, pltpu.VMEM((WIDTH, SIDE * ROWS), F32)),
-        spaces="s",
-    )(place, totals, queries, keys)
+        scratch=(
+            tall, tall, tall, tall, row, row, row,
+            pltpu.VMEM((WIDTH, SIDE * ROWS), F32),
+            pltpu.VMEM((SIDE, 2 * ROWS, WIDTH), BF16),
+            pltpu.SemaphoreType.DMA((SIDE // 2,)),
+        ),
+        out_spaces="vh",
+    )(totals, queries, keys)
     keys = lax.all_to_all(keys, "y", 0, 0)
     inner = lax.psum(inner, "x")
-    gk, dv, inner, *queries[1:] = call(
-        sums_kernel, (wide, block, message, block, block, block), spaces="s"
-    )(place, inner, keys, *queries[1:], k_raw, k_gain)
+    dv = call(values_kernel, block)(keys)
+    gk, inner, *queries = call(
+        sums_kernel, (wide, message, block, block, block, block), spaces="s"
+    )(place, inner, keys, queries, k_raw, k_gain)
     inner = lax.all_to_all(inner, HEAD, 0, 0)
     queries[1:] = [swap(part, "x", d) for d, part in enumerate(queries[1:], 1)]
     d_q, d_k = call(final_kernel, (block, block))(

time: 107 us -> 106 us (level)
  local copies, waits for them, and re-layouts: 2.46 us -> 0.68 us
  waiting for transfers between devices: 14.5 us -> 15.6 us
    all_to_all x1, waiting for transfers between devices: 9.27 us -> 11 us  [local(): squares = lax.all_to_all(squares, HEAD, 0, 0)]
    unnamed x16, local copies, waits for them, and re-layouts: 2.46 us -> 0.68 us
    pallas_call x7 -> x8, Pallas kernels: 16.3 us -> 15.7 us  [run(): pl.pallas_call(kernel, out_shape=out_shape, in_specs=specs, out_specs=jax...]
where the time goes in v6:
time: 106 us; the launch traced here: 105 us
  starting transfers between devices  44.9 us (42%)
  blocking collectives  27.4 us (26%)
  Pallas kernels  15.7 us (15%)
  waiting for transfers between devices  15.6 us (15%)
    all_to_all x1, starting transfers between devices, local(): squares = lax.all_to_all(squares, HEAD, 0, 0)  16.9 us
    pallas_call x8, Pallas kernels, run(): pl.pallas_call(kernel, out_shape=out_shape, in_specs=specs, out_specs=jax...  15.7 us
    all_gather x1, blocking collectives, local(): lax.all_gather(keys, 'y', axis=0, tiled=True)  12.4 us
    all_to_all x1, waiting for transfers between devices, local(): squares = lax.all_to_all(squares, HEAD, 0, 0)  11 us
    all_to_all x1, starting transfers between devices, local(): inner = lax.all_to_all(inner, HEAD, 0, 0)  10.9 us
    ppermute x3, starting transfers between devices, swap(): return lax.ppermute(value, axis, [(i, i ^ mask) for i in range(SIDE)])  9.58 us
    psum x1, blocking collectives, local(): totals = lax.psum(totals, 'x')  8.96 us
    psum x1, blocking collectives, local(): inner = lax.psum(inner, 'x')  6.1 us
  transfers between devices with their start and end apart: 7, of which 4 were waited for; matrix products, arithmetic and copies ran while one was open for 0% of the time, Pallas kernels for 1%

profile of v6, /device:TPU:1, one launch (start us, length us, event | category | flops | bytes accessed | tf_op | source)
XLA Modules:
  0.0 105.1 jit_solution(15139933851982360347)
XLA Ops:
  0.6 0.0 copy-start.3
  0.6 0.0 copy-start.4
  0.7 1.8 %shard_map.103 = bf16[32,2,384]{2,1,0:T(2,128)(2,1)} custom-call(bf16[384,128]{1,0:T(8,128)(2,1)} %q_ref.5, bf16[384,128]{1,0:T(8,128)(2,1)} %k_ref.7), custom_call_target="tpu_custom_call" | custom-call | tf_op jit(solution)/shard_map/pallas_call | solution.py:43
  2.5 0.0 copy-start.2
  2.5 16.9 %all-to-all-start = ((bf16[32,2,384]{2,1,0:T(2,128)(2,1)}), bf16[32,2,384]{2,1,0:T(2,128)(2,1)S(1)}, u32[]{:S(2)}, u32[]{:S(2)}) async-start(bf16[32,2,384]{2,1,0:T(2,128)(2,1)} %shard_map.103), calls=%async_computation | async-start | bytes 98304 | tf_op jit(solution)/shard_map/all_to_all | solution.py:291
  19.3 0.1 pad_add_fusion.place_ref
  19.4 0.0 copy-start.5
  19.4 0.0 copy-start.6
  19.4 0.0 copy-start.7
  19.4 0.0 copy-done.3
  19.4 0.0 copy-done.4
  19.4 0.0 copy-done.2
  19.5 0.6 copy-done.5
  20.1 0.0 copy-done.6
  20.1 0.0 copy-done.7
  20.1 0.0 copy-start
  20.1 0.0 copy-start.1
  20.1 0.7 shard_map.104
  20.8 11.0 %all-to-all-done.sums_ref = bf16[32,2,384]{2,1,0:T(2,128)(2,1)S(1)} async-done(((bf16[32,2,384]{2,1,0:T(2,128)(2,1)}), bf16[32,2,384]{2,1,0:T(2,128)(2,1)S(1)}, u32[]{:S(2)}, u32[]{:S(2)}) %all-to-all-start) | async-done | bytes 49184 | tf_op jit(solution)/shard_map/all_to_all | solution.py:291
  31.9 0.0 copy-done
  31.9 0.0 copy-done.1
  31.9 1.0 shard_map.105
  32.9 4.0 %all-to-all-start.1 = ((bf16[4,784,128]{2,1,0:T(8,128)(2,1)}), bf16[4,784,128]{2,1,0:T(8,128)(2,1)S(1)}, u32[]{:S(2)}, u32[]{:S(2)}) async-start(bf16[4,784,128]{2,1,0:T(8,128)(2,1)} %get-tuple-element.27), calls=%async_computation.1 | async-start | bytes 1605632 | tf_op jit(solution)/shard_map/all_to_all | solution.py:311
  36.9 12.4 %all_gather.3 = bf16[3136,128]{1,0:T(8,128)(2,1)S(1)} all-gather(bf16[784,128]{1,0:T(8,128)(2,1)S(1)} %get-tuple-element.28), channel_id=1, replica_groups=mesh['y'=4,'x'=4,'z'=16,'c'=2] {'y'}, dimensions={0}, use_global_device_ids=true | all-gather | bytes 1003520 | tf_op jit(solution)/shard_map/all_gather | solution.py:312
  49.3 0.0 all-to-all-done.1.qall_ref
  49.3 2.0 %shard_map.106 = f32[4,1,384]{2,1,0:T(1,128)S(1)} custom-call(bf16[4,784,128]{2,1,0:T(8,128)(2,1)S(1)} %all-to-all-done.1.qall_ref, bf16[4,784,128]{2,1,0:T(8,128)(2,1)S(1)} %bitcast.5), custom_call_target="tpu_custom_call" | custom-call | tf_op jit(solution)/shard_map/pallas_call | solution.py:43
  51.3 9.0 %psum.14.total_ref = f32[4,1,384]{2,1,0:T(1,128)S(1)} all-reduce(f32[4,1,384]{2,1,0:T(1,128)S(1)} %shard_map.106), channel_id=1, replica_groups=mesh['y'=4,'x'=4,'z'=16,'c'=2] {'x'}, use_global_device_ids=true, to_apply=%region_0.0 | all-reduce | flops 1536 | bytes 12288 | tf_op jit(solution)/shard_map/psum | solution.py:319
  60.2 7.2 %shard_map.107 = (f32[1,1536]{1,0:T(1,128)S(1)}, bf16[4,768,128]{2,1,0:T(8,128)(2,1)}, bf16[4,384,128]{2,1,0:T(8,128)(2,1)S(1)}) custom-call(f32[4,1,384]{2,1,0:T(1,128)S(1)} %psum.14.total_ref, bf16[4,784,128]{2,1,0:T(8,128)(2,1)S(1)} %all-to-all-done.1.qall_ref, bf16[4,784,128]{2,1,0:T(8,128)(2,1)S(1)} %bitcast.6), custom_call_target="tpu_custom_call" | custom-call | tf_op jit(solution)/shard_map/pallas_call | solution.py:43
  67.4 3.5 %all-to-all-start.2 = ((bf16[4,768,128]{2,1,0:T(8,128)(2,1)}), bf16[4,768,128]{2,1,0:T(8,128)(2,1)S(1)}, u32[]{:S(2)}, u32[]{:S(2)}) async-start(bf16[4,768,128]{2,1,0:T(8,128)(2,1)} %get-tuple-element.30), calls=%async_computation.2 | async-start | bytes 1572864 | tf_op jit(solution)/shard_map/all_to_all | solution.py:338
  70.9 6.1 %psum.15.inner_ref = f32[1,1536]{1,0:T(1,128)S(1)} all-reduce(f32[1,1536]{1,0:T(1,128)S(1)} %get-tuple-element.29), channel_id=1, replica_groups=mesh['y'=4,'x'=4,'z'=16,'c'=2] {'x'}, use_global_device_ids=true, to_apply=%region_1.0 | all-reduce | flops 1536 | bytes 12288 | tf_op jit(solution)/shard_map/psum | solution.py:339
  77.0 2.2 %all-to-all-done.2.dkv_ref = bf16[4,768,128]{2,1,0:T(8,128)(2,1)S(1)} async-done(((bf16[4,768,128]{2,1,0:T(8,128)(2,1)}), bf16[4,768,128]{2,1,0:T(8,128)(2,1)S(1)}, u32[]{:S(2)}, u32[]{:S(2)}) %all-to-all-start.2) | async-done | bytes 786464 | tf_op jit(solution)/shard_map/all_to_all | solution.py:338
  79.2 1.3 %shard_map.108 = (f32[384,128]{1,0:T(8,128)S(1)}, bf16[32,2,384]{2,1,0:T(2,128)(2,1)}, bf16[384,128]{1,0:T(8,128)(2,1)S(1)}, bf16[384,128]{1,0:T(8,128)(2,1)S(1)...) custom-call(s32[2]{0:T(128)S(1)} %pad_add_fusion.place_ref, f32[1,1536]{1,0:T(1,128)S(1)} %psum.15.inner_ref, ...), custom_call_target="tpu_custom_call" | custom-call | tf_op jit(solution)/shard_map/pallas_call | solution.py:43
  80.6 10.9 %all-to-all-start.3 = ((bf16[32,2,384]{2,1,0:T(2,128)(2,1)}), bf16[32,2,384]{2,1,0:T(2,128)(2,1)S(1)}, u32[]{:S(2)}, u32[]{:S(2)}) async-start(bf16[32,2,384]{2,1,0:T(2,128)(2,1)} %get-tuple-element.32), calls=%async_computation.3 | async-start | bytes 98304 | tf_op jit(solution)/shard_map/all_to_all | solution.py:344
  91.4 2.0 %collective-permute-start = (bf16[384,128]{1,0:T(8,128)(2,1)S(1)}, bf16[384,128]{1,0:T(8,128)(2,1)S(1)}, u32[]{:S(2)}, u32[]{:S(2)}) collective-permute-start(bf16[384,128]{1,0:T(8,128)(2,1)S(1)} %get-tuple-element.35), channel_id=1, source_target_pairs={{0,32},{32,0},{64,96},{96,64},{1,33},{33,1},{65,97},{97,65},{2,34}... | collective-permute-start | bytes 294920 | tf_op jit(solution)/shard_map/ppermute | solution.py:28
  93.4 3.1 %collective-permute-start.1 = (bf16[384,128]{1,0:T(8,128)(2,1)S(1)}, bf16[384,128]{1,0:T(8,128)(2,1)S(1)}, u32[]{:S(2)}, u32[]{:S(2)}) collective-permute-start(bf16[384,128]{1,0:T(8,128)(2,1)S(1)} %get-tuple-element.36), channel_id=1, source_target_pairs={{0,64},{32,96},{64,0},{96,32},{1,65},{33,97},{65,1},{97,33},{2,66}... | collective-permute-start | bytes 294920 | tf_op jit(solution)/shard_map/ppermute | solution.py:28
  96.5 4.5 %collective-permute-start.2 = (bf16[384,128]{1,0:T(8,128)(2,1)S(1)}, bf16[384,128]{1,0:T(8,128)(2,1)S(1)}, u32[]{:S(2)}, u32[]{:S(2)}) collective-permute-start(bf16[384,128]{1,0:T(8,128)(2,1)S(1)} %get-tuple-element.37), channel_id=1, source_target_pairs={{0,96},{32,64},{64,32},{96,0},{1,97},{33,65},{65,33},{97,1},{2,98}... | collective-permute-start | bytes 294920 | tf_op jit(solution)/shard_map/ppermute | solution.py:28
  101.1 0.7 shard_map.110
  101.7 0.0 collective-permute-done.dq1_ref
  101.7 0.0 collective-permute-done.1.dq2_ref
  101.8 1.6 %collective-permute-done.2.dq3_ref = bf16[384,128]{1,0:T(8,128)(2,1)S(1)} collective-permute-done((bf16[384,128]{1,0:T(8,128)(2,1)S(1)}, bf16[384,128]{1,0:T(8,128)(2,1)S(1)}, u32[]{:S(2)}, u32[]{:S(2)}) %collective-permute-start.2) | collective-permute-done | bytes 98336 | tf_op jit(solution)/shard_map/ppermute | solution.py:28
  103.4 0.7 all-to-all-done.3.sums_ref
  104.1 1.0 shard_map.109
Async XLA Ops:
  0.6 18.8 %copy-start.3 = (bf16[384,128]{1,0:T(8,128)(2,1)S(1)}, bf16[384,128]{1,0:T(8,128)(2,1)}, u32[]{:S(2)}) copy-start(bf16[384,128]{1,0:T(8,128)(2,1)} %o_ref.1) | copy-start | bytes 294916
  0.6 18.8 %copy-start.4 = (bf16[384,128]{1,0:T(8,128)(2,1)S(1)}, bf16[384,128]{1,0:T(8,128)(2,1)}, u32[]{:S(2)}) copy-start(bf16[384,128]{1,0:T(8,128)(2,1)} %v_ref.1) | copy-start | bytes 294916
  2.5 17.0 %copy-start.2 = (bf16[384,128]{1,0:T(8,128)(2,1)S(1)}, bf16[384,128]{1,0:T(8,128)(2,1)}, u32[]{:S(2)}) copy-start(bf16[384,128]{1,0:T(8,128)(2,1)} %g_ref.1) | copy-start | bytes 294916
  2.5 29.4 %all-to-all-start = ((bf16[32,2,384]{2,1,0:T(2,128)(2,1)}), bf16[32,2,384]{2,1,0:T(2,128)(2,1)S(1)}, u32[]{:S(2)}, u32[]{:S(2)}) async-start(bf16[32,2,384]{2,1,0:T(2,128)(2,1)} %shard_map.103), calls=%async_computation | async-start | bytes 98304 | tf_op jit(solution)/shard_map/all_to_all | solution.py:291
  19.4 0.7 copy-start.5
  19.4 0.7 copy-start.6
  19.4 0.7 copy-start.7
  20.1 11.7 %copy-start = (bf16[384,128]{1,0:T(8,128)(2,1)S(1)}, bf16[384,128]{1,0:T(8,128)(2,1)}, u32[]{:S(2)}) copy-start(bf16[384,128]{1,0:T(8,128)(2,1)} %k_ref.7) | copy-start | bytes 294916
  20.1 11.7 %copy-start.1 = (bf16[384,128]{1,0:T(8,128)(2,1)S(1)}, bf16[384,128]{1,0:T(8,128)(2,1)}, u32[]{:S(2)}) copy-start(bf16[384,128]{1,0:T(8,128)(2,1)} %q_ref.5) | copy-start | bytes 294916
  32.9 16.4 %all-to-all-start.1 = ((bf16[4,784,128]{2,1,0:T(8,128)(2,1)}), bf16[4,784,128]{2,1,0:T(8,128)(2,1)S(1)}, u32[]{:S(2)}, u32[]{:S(2)}) async-start(bf16[4,784,128]{2,1,0:T(8,128)(2,1)} %get-tuple-element.27), calls=%async_computation.1 | async-start | bytes 1605632 | tf_op jit(solution)/shard_map/all_to_all | solution.py:311
  67.4 11.8 %all-to-all-start.2 = ((bf16[4,768,128]{2,1,0:T(8,128)(2,1)}), bf16[4,768,128]{2,1,0:T(8,128)(2,1)S(1)}, u32[]{:S(2)}, u32[]{:S(2)}) async-start(bf16[4,768,128]{2,1,0:T(8,128)(2,1)} %get-tuple-element.30), calls=%async_computation.2 | async-start | bytes 1572864 | tf_op jit(solution)/shard_map/all_to_all | solution.py:338
  80.6 23.6 %all-to-all-start.3 = ((bf16[32,2,384]{2,1,0:T(2,128)(2,1)}), bf16[32,2,384]{2,1,0:T(2,128)(2,1)S(1)}, u32[]{:S(2)}, u32[]{:S(2)}) async-start(bf16[32,2,384]{2,1,0:T(2,128)(2,1)} %get-tuple-element.32), calls=%async_computation.3 | async-start | bytes 98304 | tf_op jit(solution)/shard_map/all_to_all | solution.py:344
  91.4 10.3 %collective-permute-start = (bf16[384,128]{1,0:T(8,128)(2,1)S(1)}, bf16[384,128]{1,0:T(8,128)(2,1)S(1)}, u32[]{:S(2)}, u32[]{:S(2)}) collective-permute-start(bf16[384,128]{1,0:T(8,128)(2,1)S(1)} %get-tuple-element.35), channel_id=1, source_target_pairs={{0,32},{32,0},{64,96},{96,64},{1,33},{33,1},{65,97},{97,65},{2,34}... | collective-permute-start | bytes 294920 | tf_op jit(solution)/shard_map/ppermute | solution.py:28
  93.4 8.3 %collective-permute-start.1 = (bf16[384,128]{1,0:T(8,128)(2,1)S(1)}, bf16[384,128]{1,0:T(8,128)(2,1)S(1)}, u32[]{:S(2)}, u32[]{:S(2)}) collective-permute-start(bf16[384,128]{1,0:T(8,128)(2,1)S(1)} %get-tuple-element.36), channel_id=1, source_target_pairs={{0,64},{32,96},{64,0},{96,32},{1,65},{33,97},{65,1},{97,33},{2,66}... | collective-permute-start | bytes 294920 | tf_op jit(solution)/shard_map/ppermute | solution.py:28
  96.5 6.9 %collective-permute-start.2 = (bf16[384,128]{1,0:T(8,128)(2,1)S(1)}, bf16[384,128]{1,0:T(8,128)(2,1)S(1)}, u32[]{:S(2)}, u32[]{:S(2)}) collective-permute-start(bf16[384,128]{1,0:T(8,128)(2,1)S(1)} %get-tuple-element.37), channel_id=1, source_target_pairs={{0,96},{32,64},{64,32},{96,0},{1,97},{33,65},{65,33},{97,1},{2,98}... | collective-permute-start | bytes 294920 | tf_op jit(solution)/shard_map/ppermute | solution.py:28

commit v7 on v6

--- a/solution.py
+++ b/solution.py
@@ -64,7 +64,16 @@
     return lax.dot_general(a, b, dims, preferred_element_type=F32)
 
 
-def squares_kernel(q_ref, k_ref, msg_ref):
+def encode(value):
+    square = value * value
+    return (square * square).astype(BF16)
+
+
+def decode(coded):
+    return lax.rsqrt(lax.rsqrt(jnp.maximum(coded.astype(F32), 1e-36)))
+
+
+def squares_kernel(q_ref, k_ref, msg_ref, own_ref):
     sums = []
     for ref in (q_ref, k_ref):
         parts = []
@@ -73,15 +82,15 @@
             parts.append(row_sums(block * block))
         sums.append(jnp.concatenate(parts, axis=1))
     both = jnp.concatenate(sums, axis=0)
-    square = both * both
-    coded = (square * square).astype(BF16)
+    own_ref[...] = both
+    coded = encode(both)
     for h in range(HEADS):
         msg_ref[h] = coded
 
 
 def ready_kernel(
-    place_ref, order_ref, g_ref, o_ref, v_ref, qgain_ref, kgain_ref,
-    g_out, v_out, lines_ref, qscale_ref, kscale_ref,
+    place_ref, order_ref, own_ref, g_ref, o_ref, v_ref, qgain_ref, kgain_ref,
+    own_out, g_out, v_out, lines_ref, qscale_ref, kscale_ref,
 ):
     group = order_ref[place_ref[0] * SIDE + place_ref[1]].astype(F32)
     line = lax.broadcasted_iota(jnp.int32, (LINES, WIDTH), 0)
@@ -93,6 +102,7 @@
         lines = jnp.where(line == i, high, lines)
         lines = jnp.where(line == PIECES + i, delta - high, lines)
     lines_ref[...] = lines.astype(BF16)
+    own_out[...] = own_ref[...]
     g_out[...] = g_ref[...]
     v_out[...] = v_ref[...]
     qscale_ref[...] = qgain_ref[...].astype(F32)
@@ -100,7 +110,7 @@
 
 
 def norms_kernel(
-    sums_ref, q_ref, k_ref, g_ref, v_ref, lines_ref, qscale_ref, kscale_ref,
+    sums_ref, own_ref, q_ref, k_ref, g_ref, v_ref, lines_ref, qscale_ref, kscale_ref,
     rate_ref, qmsg_hbm, kmsg_ref, q_buf, sems,
 ):
     early = pl.ds(ROWS, ROWS + LINES)
@@ -116,9 +126,10 @@
     q_buf[2 * ROWS :, :] = lines_ref[...]
     for copy in copies[0]:
         copy.start()
-    total = jnp.zeros((2, ROWS), F32)
+    total = own_ref[...] - decode(encode(own_ref[...]))
     for h in range(HEADS):
-        total = total + lax.rsqrt(lax.rsqrt(jnp.maximum(sums_ref[h].astype(F32), 1e-36)))
+        total = total + decode(sums_ref[h])
+    total = jnp.maximum(total, own_ref[...])
     rate = lax.rsqrt(total / (HEADS * WIDTH) + EPSILON)
     rate_ref[...] = rate
     for i in range(PIECES):
@@ -233,7 +244,7 @@
 
 def sums_kernel(
     place_ref, inner_ref, dkv_ref, dq_ref, k_ref, kscale_ref,
-    gk_ref, msg_ref, out0_ref, out1_ref, out2_ref, out3_ref,
+    gk_ref, msg_ref, own_ref, out0_ref, out1_ref, out2_ref, out3_ref,
 ):
     k_lines = []
     for i in range(PIECES):
@@ -244,7 +255,9 @@
     q_line = jnp.zeros((1, ROWS), F32)
     for i in range(SIDE):
         q_line = jnp.where(place_ref[1] == i, inner_ref[:, i * ROWS : (i + 1) * ROWS], q_line)
-    coded = jnp.concatenate([q_line, jnp.concatenate(k_lines, axis=1)], axis=0).astype(BF16)
+    both = jnp.concatenate([q_line, jnp.concatenate(k_lines, axis=1)], axis=0)
+    own_ref[...] = both
+    coded = both.astype(BF16)
     for h in range(HEADS):
         msg_ref[h] = coded
     for d, target in enumerate((out0_ref, out1_ref, out2_ref, out3_ref)):
@@ -256,10 +269,10 @@
 
 
 def final_kernel(
-    sums_ref, rate_ref, dq0_ref, dq1_ref, dq2_ref, dq3_ref, gk_ref, q_ref, k_ref, qscale_ref,
+    sums_ref, own_ref, rate_ref, dq0_ref, dq1_ref, dq2_ref, dq3_ref, gk_ref, q_ref, k_ref, qscale_ref,
     dq_ref, dk_ref,
 ):
-    inner = jnp.zeros((2, ROWS), F32)
+    inner = own_ref[...] - own_ref[...].astype(BF16).astype(F32)
     for h in range(HEADS):
         inner = inner + sums_ref[h].astype(F32)
     rate = rate_ref[...]
@@ -287,14 +300,15 @@
     q_gain = q_gain.reshape(1, WIDTH)
     k_gain = k_gain.reshape(1, WIDTH)
 
-    squares = call(squares_kernel, message, limit=60)(q_raw, k_raw)
+    exact = struct((2, ROWS), F32)
+    squares, own_squares = call(squares_kernel, (message, exact), limit=60)(q_raw, k_raw)
     squares = lax.all_to_all(squares, HEAD, 0, 0)
     gain = struct((1, WIDTH), F32)
-    d_out, values, lines, q_gain, k_gain = call(
+    own_squares, d_out, values, lines, q_gain, k_gain = call(
         ready_kernel,
-        (block, block, struct((LINES, WIDTH), BF16), gain, gain),
+        (exact, block, block, struct((LINES, WIDTH), BF16), gain, gain),
         spaces="ss",
-    )(place, order, d_out, out, values, q_gain, k_gain)
+    )(place, order, own_squares, d_out, out, values, q_gain, k_gain)
     rate, queries, keys = call(
         norms_kernel,
         (
@@ -307,7 +321,7 @@
             pltpu.SemaphoreType.DMA((2, SIDE)),
         ),
         out_spaces="vh",
-    )(squares, q_raw, k_raw, d_out, values, lines, q_gain, k_gain)
+    )(squares, own_squares, q_raw, k_raw, d_out, values, lines, q_gain, k_gain)
     queries = lax.all_to_all(queries, "x", 0, 0)
     keys = lax.all_gather(keys, "y", axis=0, tiled=True).reshape(SIDE, 2 * ROWS + LINES, WIDTH)
 
@@ -338,13 +352,13 @@
     keys = lax.all_to_all(keys, "y", 0, 0)
     inner = lax.psum(inner, "x")
     dv = call(values_kernel, block)(keys)
-    gk, inner, *queries = call(
-        sums_kernel, (wide, message, block, block, block, block), spaces="s"
+    gk, inner, own_inner, *queries = call(
+        sums_kernel, (wide, message, exact, block, block, block, block), spaces="s"
     )(place, inner, keys, queries, k_raw, k_gain)
     inner = lax.all_to_all(inner, HEAD, 0, 0)
     queries[1:] = [swap(part, "x", d) for d, part in enumerate(queries[1:], 1)]
     d_q, d_k = call(final_kernel, (block, block))(
-        inner, rate, *queries, gk, q_raw, k_raw, q_gain
+        inner, own_inner, rate, *queries, gk, q_raw, k_raw, q_gain
     )
     return d_q, d_k, dv
 

time: 106 us -> 106 us (level)
  no operation moved by 1% of the time
where the time goes in v7:
time: 106 us; the launch traced here: 105 us
  starting transfers between devices  44.9 us (42%)
  blocking collectives  27.4 us (26%)
  Pallas kernels  15.7 us (15%)
  waiting for transfers between devices  15.6 us (15%)
    all_to_all x1, starting transfers between devices, local(): squares = lax.all_to_all(squares, HEAD, 0, 0)  16.9 us
    pallas_call x8, Pallas kernels, run(): pl.pallas_call(kernel, out_shape=out_shape, in_specs=specs, out_specs=jax...  15.7 us
    all_gather x1, blocking collectives, local(): lax.all_gather(keys, 'y', axis=0, tiled=True)  12.4 us
    all_to_all x1, waiting for transfers between devices, local(): squares = lax.all_to_all(squares, HEAD, 0, 0)  11 us
    all_to_all x1, starting transfers between devices, local(): inner = lax.all_to_all(inner, HEAD, 0, 0)  10.9 us
    ppermute x3, starting transfers between devices, swap(): return lax.ppermute(value, axis, [(i, i ^ mask) for i in range(SIDE)])  9.58 us
    psum x1, blocking collectives, local(): totals = lax.psum(totals, 'x')  8.96 us
    psum x1, blocking collectives, local(): inner = lax.psum(inner, 'x')  6.1 us
  transfers between devices with their start and end apart: 7, of which 4 were waited for; matrix products, arithmetic and copies ran while one was open for 0% of the time, Pallas kernels for 1%

profile of v7, /device:TPU:1, one launch (start us, length us, event | category | flops | bytes accessed | tf_op | source)
XLA Modules:
  0.0 105.2 jit_solution(8601848505219686717)
XLA Ops:
  0.6 0.0 copy-start.3
  0.6 0.0 copy-start.4
  0.7 1.8 %shard_map.103 = (bf16[32,2,384]{2,1,0:T(2,128)(2,1)}, f32[2,384]{1,0:T(2,128)}) custom-call(bf16[384,128]{1,0:T(8,128)(2,1)} %q_ref.5, bf16[384,128]{1,0:T(8,128)(2,1)} %k_ref.7), custom_call_target="tpu_custom_call" | custom-call | tf_op jit(solution)/shard_map/pallas_call | solution.py:43
  2.5 0.0 copy-start.2
  2.5 16.9 %all-to-all-start = ((bf16[32,2,384]{2,1,0:T(2,128)(2,1)}), bf16[32,2,384]{2,1,0:T(2,128)(2,1)S(1)}, u32[]{:S(2)}, u32[]{:S(2)}) async-start(bf16[32,2,384]{2,1,0:T(2,128)(2,1)} %get-tuple-element.26), calls=%async_computation | async-start | bytes 98304 | tf_op jit(solution)/shard_map/all_to_all | solution.py:305
  19.4 0.1 pad_add_fusion.place_ref
  19.4 0.0 copy-start.5
  19.4 0.0 copy-start.6
  19.4 0.0 copy-start.7
  19.4 0.0 copy-start.8
  19.4 0.0 copy-done.3
  19.4 0.0 copy-done.4
  19.5 0.0 copy-done.2
  19.5 0.6 copy-done.5
  20.1 0.0 copy-done.6
  20.1 0.0 copy-done.7
  20.1 0.0 copy-done.8
  20.1 0.0 copy-start
  20.1 0.0 copy-start.1
  20.1 0.7 shard_map.104
  20.8 11.0 %all-to-all-done.sums_ref = bf16[32,2,384]{2,1,0:T(2,128)(2,1)S(1)} async-done(((bf16[32,2,384]{2,1,0:T(2,128)(2,1)}), bf16[32,2,384]{2,1,0:T(2,128)(2,1)S(1)}, u32[]{:S(2)}, u32[]{:S(2)}) %all-to-all-start) | async-done | bytes 49184 | tf_op jit(solution)/shard_map/all_to_all | solution.py:305
  31.9 0.0 copy-done
  31.9 0.0 copy-done.1
  31.9 1.0 shard_map.105
  32.9 4.0 %all-to-all-start.1 = ((bf16[4,784,128]{2,1,0:T(8,128)(2,1)}), bf16[4,784,128]{2,1,0:T(8,128)(2,1)S(1)}, u32[]{:S(2)}, u32[]{:S(2)}) async-start(bf16[4,784,128]{2,1,0:T(8,128)(2,1)} %get-tuple-element.34), calls=%async_computation.1 | async-start | bytes 1605632 | tf_op jit(solution)/shard_map/all_to_all | solution.py:325
  36.9 12.4 %all_gather.3 = bf16[3136,128]{1,0:T(8,128)(2,1)S(1)} all-gather(bf16[784,128]{1,0:T(8,128)(2,1)S(1)} %get-tuple-element.35), channel_id=1, replica_groups=mesh['y'=4,'x'=4,'z'=16,'c'=2] {'y'}, dimensions={0}, use_global_device_ids=true | all-gather | bytes 1003520 | tf_op jit(solution)/shard_map/all_gather | solution.py:326
  49.3 0.0 all-to-all-done.1.qall_ref
  49.3 2.0 %shard_map.106 = f32[4,1,384]{2,1,0:T(1,128)S(1)} custom-call(bf16[4,784,128]{2,1,0:T(8,128)(2,1)S(1)} %all-to-all-done.1.qall_ref, bf16[4,784,128]{2,1,0:T(8,128)(2,1)S(1)} %bitcast.5), custom_call_target="tpu_custom_call" | custom-call | tf_op jit(solution)/shard_map/pallas_call | solution.py:43
  51.3 9.0 %psum.14.total_ref = f32[4,1,384]{2,1,0:T(1,128)S(1)} all-reduce(f32[4,1,384]{2,1,0:T(1,128)S(1)} %shard_map.106), channel_id=1, replica_groups=mesh['y'=4,'x'=4,'z'=16,'c'=2] {'x'}, use_global_device_ids=true, to_apply=%region_0.0 | all-reduce | flops 1536 | bytes 12288 | tf_op jit(solution)/shard_map/psum | solution.py:333
  60.3 7.2 %shard_map.107 = (f32[1,1536]{1,0:T(1,128)S(1)}, bf16[4,768,128]{2,1,0:T(8,128)(2,1)}, bf16[4,384,128]{2,1,0:T(8,128)(2,1)S(1)}) custom-call(f32[4,1,384]{2,1,0:T(1,128)S(1)} %psum.14.total_ref, bf16[4,784,128]{2,1,0:T(8,128)(2,1)S(1)} %all-to-all-done.1.qall_ref, bf16[4,784,128]{2,1,0:T(8,128)(2,1)S(1)} %bitcast.6), custom_call_target="tpu_custom_call" | custom-call | tf_op jit(solution)/shard_map/pallas_call | solution.py:43
  67.5 3.5 %all-to-all-start.2 = ((bf16[4,768,128]{2,1,0:T(8,128)(2,1)}), bf16[4,768,128]{2,1,0:T(8,128)(2,1)S(1)}, u32[]{:S(2)}, u32[]{:S(2)}) async-start(bf16[4,768,128]{2,1,0:T(8,128)(2,1)} %get-tuple-element.37), calls=%async_computation.2 | async-start | bytes 1572864 | tf_op jit(solution)/shard_map/all_to_all | solution.py:352
  71.0 6.1 %psum.15.inner_ref = f32[1,1536]{1,0:T(1,128)S(1)} all-reduce(f32[1,1536]{1,0:T(1,128)S(1)} %get-tuple-element.36), channel_id=1, replica_groups=mesh['y'=4,'x'=4,'z'=16,'c'=2] {'x'}, use_global_device_ids=true, to_apply=%region_1.0 | all-reduce | flops 1536 | bytes 12288 | tf_op jit(solution)/shard_map/psum | solution.py:353
  77.1 2.2 %all-to-all-done.2.dkv_ref = bf16[4,768,128]{2,1,0:T(8,128)(2,1)S(1)} async-done(((bf16[4,768,128]{2,1,0:T(8,128)(2,1)}), bf16[4,768,128]{2,1,0:T(8,128)(2,1)S(1)}, u32[]{:S(2)}, u32[]{:S(2)}) %all-to-all-start.2) | async-done | bytes 786464 | tf_op jit(solution)/shard_map/all_to_all | solution.py:352
  79.3 1.3 %shard_map.108 = (f32[384,128]{1,0:T(8,128)S(1)}, bf16[32,2,384]{2,1,0:T(2,128)(2,1)}, f32[2,384]{1,0:T(2,128)S(1)}, bf16[384,128]{1,0:T(8,128)(2,1)S(1)}, bf16[...) custom-call(s32[2]{0:T(128)S(1)} %pad_add_fusion.place_ref, ...), custom_call_target="tpu_custom_call" | custom-call | tf_op jit(solution)/shard_map/pallas_call | solution.py:43
  80.6 10.9 %all-to-all-start.3 = ((bf16[32,2,384]{2,1,0:T(2,128)(2,1)}), bf16[32,2,384]{2,1,0:T(2,128)(2,1)S(1)}, u32[]{:S(2)}, u32[]{:S(2)}) async-start(bf16[32,2,384]{2,1,0:T(2,128)(2,1)} %get-tuple-element.39), calls=%async_computation.3 | async-start | bytes 98304 | tf_op jit(solution)/shard_map/all_to_all | solution.py:358
  91.5 2.0 %collective-permute-start = (bf16[384,128]{1,0:T(8,128)(2,1)S(1)}, bf16[384,128]{1,0:T(8,128)(2,1)S(1)}, u32[]{:S(2)}, u32[]{:S(2)}) collective-permute-start(bf16[384,128]{1,0:T(8,128)(2,1)S(1)} %get-tuple-element.43), channel_id=1, source_target_pairs={{0,32},{32,0},{64,96},{96,64},{1,33},{33,1},{65,97},{97,65},{2,34}... | collective-permute-start | bytes 294920 | tf_op jit(solution)/shard_map/ppermute | solution.py:28
  93.5 3.1 %collective-permute-start.1 = (bf16[384,128]{1,0:T(8,128)(2,1)S(1)}, bf16[384,128]{1,0:T(8,128)(2,1)S(1)}, u32[]{:S(2)}, u32[]{:S(2)}) collective-permute-start(bf16[384,128]{1,0:T(8,128)(2,1)S(1)} %get-tuple-element.44), channel_id=1, source_target_pairs={{0,64},{32,96},{64,0},{96,32},{1,65},{33,97},{65,1},{97,33},{2,66}... | collective-permute-start | bytes 294920 | tf_op jit(solution)/shard_map/ppermute | solution.py:28
  96.6 4.5 %collective-permute-start.2 = (bf16[384,128]{1,0:T(8,128)(2,1)S(1)}, bf16[384,128]{1,0:T(8,128)(2,1)S(1)}, u32[]{:S(2)}, u32[]{:S(2)}) collective-permute-start(bf16[384,128]{1,0:T(8,128)(2,1)S(1)} %get-tuple-element.45), channel_id=1, source_target_pairs={{0,96},{32,64},{64,32},{96,0},{1,97},{33,65},{65,33},{97,1},{2,98}... | collective-permute-start | bytes 294920 | tf_op jit(solution)/shard_map/ppermute | solution.py:28
  101.1 0.7 shard_map.110
  101.8 0.0 collective-permute-done.dq1_ref
  101.8 0.0 collective-permute-done.1.dq2_ref
  101.8 1.6 %collective-permute-done.2.dq3_ref = bf16[384,128]{1,0:T(8,128)(2,1)S(1)} collective-permute-done((bf16[384,128]{1,0:T(8,128)(2,1)S(1)}, bf16[384,128]{1,0:T(8,128)(2,1)S(1)}, u32[]{:S(2)}, u32[]{:S(2)}) %collective-permute-start.2) | collective-permute-done | bytes 98336 | tf_op jit(solution)/shard_map/ppermute | solution.py:28
  103.4 0.7 all-to-all-done.3.sums_ref
  104.2 1.0 shard_map.109
Async XLA Ops:
  0.6 18.8 %copy-start.3 = (bf16[384,128]{1,0:T(8,128)(2,1)S(1)}, bf16[384,128]{1,0:T(8,128)(2,1)}, u32[]{:S(2)}) copy-start(bf16[384,128]{1,0:T(8,128)(2,1)} %o_ref.1) | copy-start | bytes 294916
  0.6 18.8 %copy-start.4 = (bf16[384,128]{1,0:T(8,128)(2,1)S(1)}, bf16[384,128]{1,0:T(8,128)(2,1)}, u32[]{:S(2)}) copy-start(bf16[384,128]{1,0:T(8,128)(2,1)} %v_ref.1) | copy-start | bytes 294916
  2.5 17.0 %copy-start.2 = (bf16[384,128]{1,0:T(8,128)(2,1)S(1)}, bf16[384,128]{1,0:T(8,128)(2,1)}, u32[]{:S(2)}) copy-start(bf16[384,128]{1,0:T(8,128)(2,1)} %g_ref.1) | copy-start | bytes 294916
  2.5 29.4 %all-to-all-start = ((bf16[32,2,384]{2,1,0:T(2,128)(2,1)}), bf16[32,2,384]{2,1,0:T(2,128)(2,1)S(1)}, u32[]{:S(2)}, u32[]{:S(2)}) async-start(bf16[32,2,384]{2,1,0:T(2,128)(2,1)} %get-tuple-element.26), calls=%async_computation | async-start | bytes 98304 | tf_op jit(solution)/shard_map/all_to_all | solution.py:305
  19.4 0.7 copy-start.5
  19.4 0.7 copy-start.6
  19.4 0.7 copy-start.7
  19.4 0.7 copy-start.8
  20.1 11.7 %copy-start = (bf16[384,128]{1,0:T(8,128)(2,1)S(1)}, bf16[384,128]{1,0:T(8,128)(2,1)}, u32[]{:S(2)}) copy-start(bf16[384,128]{1,0:T(8,128)(2,1)} %k_ref.7) | copy-start | bytes 294916
  20.1 11.7 %copy-start.1 = (bf16[384,128]{1,0:T(8,128)(2,1)S(1)}, bf16[384,128]{1,0:T(8,128)(2,1)}, u32[]{:S(2)}) copy-start(bf16[384,128]{1,0:T(8,128)(2,1)} %q_ref.5) | copy-start | bytes 294916
  32.9 16.4 %all-to-all-start.1 = ((bf16[4,784,128]{2,1,0:T(8,128)(2,1)}), bf16[4,784,128]{2,1,0:T(8,128)(2,1)S(1)}, u32[]{:S(2)}, u32[]{:S(2)}) async-start(bf16[4,784,128]{2,1,0:T(8,128)(2,1)} %get-tuple-element.34), calls=%async_computation.1 | async-start | bytes 1605632 | tf_op jit(solution)/shard_map/all_to_all | solution.py:325
  67.5 11.8 %all-to-all-start.2 = ((bf16[4,768,128]{2,1,0:T(8,128)(2,1)}), bf16[4,768,128]{2,1,0:T(8,128)(2,1)S(1)}, u32[]{:S(2)}, u32[]{:S(2)}) async-start(bf16[4,768,128]{2,1,0:T(8,128)(2,1)} %get-tuple-element.37), calls=%async_computation.2 | async-start | bytes 1572864 | tf_op jit(solution)/shard_map/all_to_all | solution.py:352
  80.6 23.6 %all-to-all-start.3 = ((bf16[32,2,384]{2,1,0:T(2,128)(2,1)}), bf16[32,2,384]{2,1,0:T(2,128)(2,1)S(1)}, u32[]{:S(2)}, u32[]{:S(2)}) async-start(bf16[32,2,384]{2,1,0:T(2,128)(2,1)} %get-tuple-element.39), calls=%async_computation.3 | async-start | bytes 98304 | tf_op jit(solution)/shard_map/all_to_all | solution.py:358
  91.5 10.3 %collective-permute-start = (bf16[384,128]{1,0:T(8,128)(2,1)S(1)}, bf16[384,128]{1,0:T(8,128)(2,1)S(1)}, u32[]{:S(2)}, u32[]{:S(2)}) collective-permute-start(bf16[384,128]{1,0:T(8,128)(2,1)S(1)} %get-tuple-element.43), channel_id=1, source_target_pairs={{0,32},{32,0},{64,96},{96,64},{1,33},{33,1},{65,97},{97,65},{2,34}... | collective-permute-start | bytes 294920 | tf_op jit(solution)/shard_map/ppermute | solution.py:28
  93.5 8.3 %collective-permute-start.1 = (bf16[384,128]{1,0:T(8,128)(2,1)S(1)}, bf16[384,128]{1,0:T(8,128)(2,1)S(1)}, u32[]{:S(2)}, u32[]{:S(2)}) collective-permute-start(bf16[384,128]{1,0:T(8,128)(2,1)S(1)} %get-tuple-element.44), channel_id=1, source_target_pairs={{0,64},{32,96},{64,0},{96,32},{1,65},{33,97},{65,1},{97,33},{2,66}... | collective-permute-start | bytes 294920 | tf_op jit(solution)/shard_map/ppermute | solution.py:28
  96.6 6.9 %collective-permute-start.2 = (bf16[384,128]{1,0:T(8,128)(2,1)S(1)}, bf16[384,128]{1,0:T(8,128)(2,1)S(1)}, u32[]{:S(2)}, u32[]{:S(2)}) collective-permute-start(bf16[384,128]{1,0:T(8,128)(2,1)S(1)} %get-tuple-element.45), channel_id=1, source_target_pairs={{0,96},{32,64},{64,32},{96,0},{1,97},{33,65},{65,33},{97,1},{2,98}... | collective-permute-start | bytes 294920 | tf_op jit(solution)/shard_map/ppermute | solution.py:28

commit v8 on v7

--- a/solution.py
+++ b/solution.py
@@ -180,13 +180,12 @@
 
 
 def grads_kernel(
-    total_ref, qall_ref, kall_ref,
+    total_ref, q_all, qall_ref, kall_ref,
     inner_ref, dkv_hbm, dq_ref,
-    q_all, g_all, k_all, v_all, logs, deltas, groups, dq_acc, dkv_buf, sems,
+    g_all, k_all, v_all, logs, deltas, groups, dq_acc, dkv_buf, sems,
 ):
     for i in range(SIDE):
         span = slice(i * ROWS, (i + 1) * ROWS)
-        q_all[span, :] = qall_ref[i, :ROWS, :]
         g_all[span, :] = qall_ref[i, ROWS : 2 * ROWS, :]
         k_all[span, :] = kall_ref[i, :ROWS, :]
         v_all[span, :] = kall_ref[i, ROWS : 2 * ROWS, :]
@@ -264,13 +263,17 @@
         target[...] = dq_ref[place_ref[1] ^ d]
 
 
-def values_kernel(dkv_ref, dv_ref):
+def values_kernel(dkv_ref, gk_ref, rate_ref, dv_ref, scaled_ref):
+    for i in range(PIECES):
+        rows = pl.ds(i * WIDTH, WIDTH)
+        span = slice(i * WIDTH, (i + 1) * WIDTH)
+        scaled_ref[rows, :] = column(rate_ref[1:2, span]) * gk_ref[rows, :]
     dv_ref[...] = sum(dkv_ref[j, ROWS:, :].astype(F32) for j in range(SIDE)).astype(BF16)
 
 
 def final_kernel(
     sums_ref, own_ref, rate_ref, dq0_ref, dq1_ref, dq2_ref, dq3_ref, gk_ref, q_ref, k_ref, qscale_ref,
-    dq_ref, dk_ref,
+    dq_hbm, dk_hbm, dq_ref, dk_ref, sems,
 ):
     inner = own_ref[...] - own_ref[...].astype(BF16).astype(F32)
     for h in range(HEADS):
@@ -279,16 +282,26 @@
     weight = rate * rate * inner / (HEADS * WIDTH)
     q_weight = weight[0:1, :]
     k_weight = weight[1:2, :] * rate[1:2, :]
+    copies = [
+        pltpu.make_async_copy(source, target, sems.at[n])
+        for n, (source, target) in enumerate(((dk_ref, dk_hbm), (dq_ref, dq_hbm)))
+    ]
+    for i in range(PIECES):
+        rows = pl.ds(i * WIDTH, WIDTH)
+        span = slice(i * WIDTH, (i + 1) * WIDTH)
+        k = k_ref[rows, :].astype(F32)
+        dk_ref[rows, :] = (gk_ref[rows, :] - k * column(k_weight[:, span])).astype(BF16)
+    copies[0].start()
     for i in range(PIECES):
         rows = pl.ds(i * WIDTH, WIDTH)
         span = slice(i * WIDTH, (i + 1) * WIDTH)
         gq = sum(part[rows, :].astype(F32) for part in (dq0_ref, dq1_ref, dq2_ref, dq3_ref))
         gq = gq * qscale_ref[...]
-        gk = gk_ref[rows, :]
         q = q_ref[rows, :].astype(F32)
-        k = k_ref[rows, :].astype(F32)
         dq_ref[rows, :] = (column(rate[0:1, span]) * gq - q * column(q_weight[:, span])).astype(BF16)
-        dk_ref[rows, :] = (column(rate[1:2, span]) * gk - k * column(k_weight[:, span])).astype(BF16)
+    copies[1].start()
+    for copy in copies:
+        copy.wait()
 
 
 def local(q_raw, k_raw, values, out, d_out, q_gain, k_gain, order):
@@ -325,10 +338,8 @@
     queries = lax.all_to_all(queries, "x", 0, 0)
     keys = lax.all_gather(keys, "y", axis=0, tiled=True).reshape(SIDE, 2 * ROWS + LINES, WIDTH)
 
-    totals = call(
-        totals_kernel,
-        struct((SIDE, 1, ROWS), F32),
-        scratch=(pltpu.VMEM((SIDE * ROWS, WIDTH), BF16),),
+    totals, q_all = call(
+        totals_kernel, (struct((SIDE, 1, ROWS), F32), struct((SIDE * ROWS, WIDTH), BF16))
     )(queries, keys)
     totals = lax.psum(totals, "x")
 
@@ -342,22 +353,31 @@
             struct((SIDE, ROWS, WIDTH), BF16),
         ),
         scratch=(
-            tall, tall, tall, tall, row, row, row,
+            tall, tall, tall, row, row, row,
             pltpu.VMEM((WIDTH, SIDE * ROWS), F32),
             pltpu.VMEM((SIDE, 2 * ROWS, WIDTH), BF16),
             pltpu.SemaphoreType.DMA((SIDE // 2,)),
         ),
         out_spaces="vh",
-    )(totals, queries, keys)
+    )(totals, q_all, queries, keys)
     keys = lax.all_to_all(keys, "y", 0, 0)
     inner = lax.psum(inner, "x")
-    dv = call(values_kernel, block)(keys)
     gk, inner, own_inner, *queries = call(
         sums_kernel, (wide, message, exact, block, block, block, block), spaces="s"
     )(place, inner, keys, queries, k_raw, k_gain)
     inner = lax.all_to_all(inner, HEAD, 0, 0)
+    dv, gk = call(values_kernel, (block, wide))(keys, gk, rate)
     queries[1:] = [swap(part, "x", d) for d, part in enumerate(queries[1:], 1)]
-    d_q, d_k = call(final_kernel, (block, block))(
+    d_q, d_k = call(
+        final_kernel,
+        (block, block),
+        scratch=(
+            pltpu.VMEM((ROWS, WIDTH), BF16),
+            pltpu.VMEM((ROWS, WIDTH), BF16),
+            pltpu.SemaphoreType.DMA((2,)),
+        ),
+        out_spaces="hh",
+    )(
         inner, own_inner, rate, *queries, gk, q_raw, k_raw, q_gain
     )
     return d_q, d_k, dv

time: 106 us -> 106 us (level)
  no operation moved by 1% of the time
where the time goes in v8:
time: 106 us; the launch traced here: 105 us
  starting transfers between devices  44.9 us (42%)
  blocking collectives  27.4 us (26%)
  Pallas kernels  15.6 us (15%)
  waiting for transfers between devices  15.5 us (15%)
    all_to_all x1, starting transfers between devices, local(): squares = lax.all_to_all(squares, HEAD, 0, 0)  16.9 us
    pallas_call x8, Pallas kernels, run(): pl.pallas_call(kernel, out_shape=out_shape, in_specs=specs, out_specs=jax...  15.6 us
    all_gather x1, blocking collectives, local(): lax.all_gather(keys, 'y', axis=0, tiled=True)  12.4 us
    all_to_all x1, waiting for transfers between devices, local(): squares = lax.all_to_all(squares, HEAD, 0, 0)  11 us
    all_to_all x1, starting transfers between devices, local(): inner = lax.all_to_all(inner, HEAD, 0, 0)  10.9 us
    ppermute x3, starting transfers between devices, swap(): return lax.ppermute(value, axis, [(i, i ^ mask) for i in range(SIDE)])  9.58 us
    psum x1, blocking collectives, local(): totals = lax.psum(totals, 'x')  8.96 us
    psum x1, blocking collectives, local(): inner = lax.psum(inner, 'x')  6.1 us
  transfers between devices with their start and end apart: 7, of which 4 were waited for; matrix products, arithmetic and copies ran while one was open for 0% of the time, Pallas kernels for 1%

profile of v8, /device:TPU:1, one launch (start us, length us, event | category | flops | bytes accessed | tf_op | source)
XLA Modules:
  0.0 105.0 jit_solution(11234834477939000519)
XLA Ops:
  0.6 0.0 copy-start.3
  0.6 0.0 copy-start.4
  0.7 1.8 %shard_map.103 = (bf16[32,2,384]{2,1,0:T(2,128)(2,1)}, f32[2,384]{1,0:T(2,128)}) custom-call(bf16[384,128]{1,0:T(8,128)(2,1)} %q_ref.5, bf16[384,128]{1,0:T(8,128)(2,1)} %k_ref.7), custom_call_target="tpu_custom_call" | custom-call | tf_op jit(solution)/shard_map/pallas_call | solution.py:43
  2.5 0.0 copy-start.2
  2.5 16.9 %all-to-all-start = ((bf16[32,2,384]{2,1,0:T(2,128)(2,1)}), bf16[32,2,384]{2,1,0:T(2,128)(2,1)S(1)}, u32[]{:S(2)}, u32[]{:S(2)}) async-start(bf16[32,2,384]{2,1,0:T(2,128)(2,1)} %get-tuple-element.30), calls=%async_computation | async-start | bytes 98304 | tf_op jit(solution)/shard_map/all_to_all | solution.py:318
  19.4 0.1 pad_add_fusion.place_ref
  19.4 0.0 copy-start.5
  19.4 0.0 copy-start.6
  19.4 0.0 copy-start.7
  19.4 0.0 copy-start.8
  19.4 0.0 copy-done.3
  19.4 0.0 copy-done.4
  19.5 0.0 copy-done.2
  19.5 0.6 copy-done.5
  20.1 0.0 copy-done.6
  20.1 0.0 copy-done.7
  20.1 0.0 copy-done.8
  20.1 0.0 copy-start
  20.1 0.0 copy-start.1
  20.1 0.7 shard_map.104
  20.8 11.0 %all-to-all-done.sums_ref = bf16[32,2,384]{2,1,0:T(2,128)(2,1)S(1)} async-done(((bf16[32,2,384]{2,1,0:T(2,128)(2,1)}), bf16[32,2,384]{2,1,0:T(2,128)(2,1)S(1)}, u32[]{:S(2)}, u32[]{:S(2)}) %all-to-all-start) | async-done | bytes 49184 | tf_op jit(solution)/shard_map/all_to_all | solution.py:318
  31.9 0.0 copy-done
  31.9 0.0 copy-done.1
  31.9 1.0 shard_map.105
  32.9 4.0 %all-to-all-start.1 = ((bf16[4,784,128]{2,1,0:T(8,128)(2,1)}), bf16[4,784,128]{2,1,0:T(8,128)(2,1)S(1)}, u32[]{:S(2)}, u32[]{:S(2)}) async-start(bf16[4,784,128]{2,1,0:T(8,128)(2,1)} %get-tuple-element.38), calls=%async_computation.1 | async-start | bytes 1605632 | tf_op jit(solution)/shard_map/all_to_all | solution.py:338
  36.9 12.4 %all_gather.3 = bf16[3136,128]{1,0:T(8,128)(2,1)S(1)} all-gather(bf16[784,128]{1,0:T(8,128)(2,1)S(1)} %get-tuple-element.39), channel_id=1, replica_groups=mesh['y'=4,'x'=4,'z'=16,'c'=2] {'y'}, dimensions={0}, use_global_device_ids=true | all-gather | bytes 1003520 | tf_op jit(solution)/shard_map/all_gather | solution.py:339
  49.3 0.0 all-to-all-done.1.qall_ref
  49.3 2.0 %shard_map.106 = (f32[4,1,384]{2,1,0:T(1,128)S(1)}, bf16[1536,128]{1,0:T(8,128)(2,1)S(1)}) custom-call(bf16[4,784,128]{2,1,0:T(8,128)(2,1)S(1)} %all-to-all-done.1.qall_ref, bf16[4,784,128]{2,1,0:T(8,128)(2,1)S(1)} %bitcast.5), custom_call_target="tpu_custom_call" | custom-call | tf_op jit(solution)/shard_map/pallas_call | solution.py:43
  51.3 9.0 %psum.14.total_ref = f32[4,1,384]{2,1,0:T(1,128)S(1)} all-reduce(f32[4,1,384]{2,1,0:T(1,128)S(1)} %get-tuple-element.40), channel_id=1, replica_groups=mesh['y'=4,'x'=4,'z'=16,'c'=2] {'x'}, use_global_device_ids=true, to_apply=%region_0.0 | all-reduce | flops 1536 | bytes 12288 | tf_op jit(solution)/shard_map/psum | solution.py:344
  60.3 7.1 %shard_map.107 = (f32[1,1536]{1,0:T(1,128)S(1)}, bf16[4,768,128]{2,1,0:T(8,128)(2,1)}, bf16[4,384,128]{2,1,0:T(8,128)(2,1)S(1)}) custom-call(f32[4,1,384]{2,1,0:T(1,128)S(1)} %psum.14.total_ref, bf16[1536,128]{1,0:T(8,128)(2,1)S(1)} %get-tuple-element.41.q_all, bf16[4,784,128]{2,1,0:T(8,128)(2,1)S(1)} %all-to-all-done.1.qall_ref, ...), custom_call_target="tpu_custom_call" | custom-call | tf_op jit(solution)/shard_map/pallas_call | solution.py:43
  67.3 3.5 %all-to-all-start.2 = ((bf16[4,768,128]{2,1,0:T(8,128)(2,1)}), bf16[4,768,128]{2,1,0:T(8,128)(2,1)S(1)}, u32[]{:S(2)}, u32[]{:S(2)}) async-start(bf16[4,768,128]{2,1,0:T(8,128)(2,1)} %get-tuple-element.43), calls=%async_computation.2 | async-start | bytes 1572864 | tf_op jit(solution)/shard_map/all_to_all | solution.py:363
  70.8 6.1 %psum.15.inner_ref = f32[1,1536]{1,0:T(1,128)S(1)} all-reduce(f32[1,1536]{1,0:T(1,128)S(1)} %get-tuple-element.42), channel_id=1, replica_groups=mesh['y'=4,'x'=4,'z'=16,'c'=2] {'x'}, use_global_device_ids=true, to_apply=%region_1.0 | all-reduce | flops 1536 | bytes 12288 | tf_op jit(solution)/shard_map/psum | solution.py:364
  76.9 2.2 %all-to-all-done.2.dkv_ref = bf16[4,768,128]{2,1,0:T(8,128)(2,1)S(1)} async-done(((bf16[4,768,128]{2,1,0:T(8,128)(2,1)}), bf16[4,768,128]{2,1,0:T(8,128)(2,1)S(1)}, u32[]{:S(2)}, u32[]{:S(2)}) %all-to-all-start.2) | async-done | bytes 786464 | tf_op jit(solution)/shard_map/all_to_all | solution.py:363
  79.1 1.3 %shard_map.108 = (f32[384,128]{1,0:T(8,128)S(1)}, bf16[32,2,384]{2,1,0:T(2,128)(2,1)}, f32[2,384]{1,0:T(2,128)S(1)}, bf16[384,128]{1,0:T(8,128)(2,1)S(1)}, bf16[...) custom-call(s32[2]{0:T(128)S(1)} %pad_add_fusion.place_ref, ...), custom_call_target="tpu_custom_call" | custom-call | tf_op jit(solution)/shard_map/pallas_call | solution.py:43
  80.5 10.9 %all-to-all-start.3 = ((bf16[32,2,384]{2,1,0:T(2,128)(2,1)}), bf16[32,2,384]{2,1,0:T(2,128)(2,1)S(1)}, u32[]{:S(2)}, u32[]{:S(2)}) async-start(bf16[32,2,384]{2,1,0:T(2,128)(2,1)} %get-tuple-element.45), calls=%async_computation.3 | async-start | bytes 98304 | tf_op jit(solution)/shard_map/all_to_all | solution.py:368
  91.3 2.0 %collective-permute-start = (bf16[384,128]{1,0:T(8,128)(2,1)S(1)}, bf16[384,128]{1,0:T(8,128)(2,1)S(1)}, u32[]{:S(2)}, u32[]{:S(2)}) collective-permute-start(bf16[384,128]{1,0:T(8,128)(2,1)S(1)} %get-tuple-element.49), channel_id=1, source_target_pairs={{0,32},{32,0},{64,96},{96,64},{1,33},{33,1},{65,97},{97,65},{2,34}... | collective-permute-start | bytes 294920 | tf_op jit(solution)/shard_map/ppermute | solution.py:28
  93.3 3.1 %collective-permute-start.1 = (bf16[384,128]{1,0:T(8,128)(2,1)S(1)}, bf16[384,128]{1,0:T(8,128)(2,1)S(1)}, u32[]{:S(2)}, u32[]{:S(2)}) collective-permute-start(bf16[384,128]{1,0:T(8,128)(2,1)S(1)} %get-tuple-element.50), channel_id=1, source_target_pairs={{0,64},{32,96},{64,0},{96,32},{1,65},{33,97},{65,1},{97,33},{2,66}... | collective-permute-start | bytes 294920 | tf_op jit(solution)/shard_map/ppermute | solution.py:28
  96.4 4.5 %collective-permute-start.2 = (bf16[384,128]{1,0:T(8,128)(2,1)S(1)}, bf16[384,128]{1,0:T(8,128)(2,1)S(1)}, u32[]{:S(2)}, u32[]{:S(2)}) collective-permute-start(bf16[384,128]{1,0:T(8,128)(2,1)S(1)} %get-tuple-element.51), channel_id=1, source_target_pairs={{0,96},{32,64},{64,32},{96,0},{1,97},{33,65},{65,33},{97,1},{2,98}... | collective-permute-start | bytes 294920 | tf_op jit(solution)/shard_map/ppermute | solution.py:28
  101.0 0.8 shard_map.109
  101.7 0.0 collective-permute-done.dq1_ref
  101.7 0.0 collective-permute-done.1.dq2_ref
  101.7 1.6 %collective-permute-done.2.dq3_ref = bf16[384,128]{1,0:T(8,128)(2,1)S(1)} collective-permute-done((bf16[384,128]{1,0:T(8,128)(2,1)S(1)}, bf16[384,128]{1,0:T(8,128)(2,1)S(1)}, u32[]{:S(2)}, u32[]{:S(2)}) %collective-permute-start.2) | collective-permute-done | bytes 98336 | tf_op jit(solution)/shard_map/ppermute | solution.py:28
  103.3 0.7 all-to-all-done.3.sums_ref
  104.0 0.9 shard_map.110
Async XLA Ops:
  0.6 18.8 %copy-start.3 = (bf16[384,128]{1,0:T(8,128)(2,1)S(1)}, bf16[384,128]{1,0:T(8,128)(2,1)}, u32[]{:S(2)}) copy-start(bf16[384,128]{1,0:T(8,128)(2,1)} %o_ref.1) | copy-start | bytes 294916
  0.6 18.8 %copy-start.4 = (bf16[384,128]{1,0:T(8,128)(2,1)S(1)}, bf16[384,128]{1,0:T(8,128)(2,1)}, u32[]{:S(2)}) copy-start(bf16[384,128]{1,0:T(8,128)(2,1)} %v_ref.1) | copy-start | bytes 294916
  2.5 17.0 %copy-start.2 = (bf16[384,128]{1,0:T(8,128)(2,1)S(1)}, bf16[384,128]{1,0:T(8,128)(2,1)}, u32[]{:S(2)}) copy-start(bf16[384,128]{1,0:T(8,128)(2,1)} %g_ref.1) | copy-start | bytes 294916
  2.5 29.4 %all-to-all-start = ((bf16[32,2,384]{2,1,0:T(2,128)(2,1)}), bf16[32,2,384]{2,1,0:T(2,128)(2,1)S(1)}, u32[]{:S(2)}, u32[]{:S(2)}) async-start(bf16[32,2,384]{2,1,0:T(2,128)(2,1)} %get-tuple-element.30), calls=%async_computation | async-start | bytes 98304 | tf_op jit(solution)/shard_map/all_to_all | solution.py:318
  19.4 0.7 copy-start.5
  19.4 0.7 copy-start.6
  19.4 0.7 copy-start.7
  19.4 0.7 copy-start.8
  20.1 11.7 %copy-start = (bf16[384,128]{1,0:T(8,128)(2,1)S(1)}, bf16[384,128]{1,0:T(8,128)(2,1)}, u32[]{:S(2)}) copy-start(bf16[384,128]{1,0:T(8,128)(2,1)} %k_ref.7) | copy-start | bytes 294916
  20.1 11.7 %copy-start.1 = (bf16[384,128]{1,0:T(8,128)(2,1)S(1)}, bf16[384,128]{1,0:T(8,128)(2,1)}, u32[]{:S(2)}) copy-start(bf16[384,128]{1,0:T(8,128)(2,1)} %q_ref.5) | copy-start | bytes 294916
  32.9 16.4 %all-to-all-start.1 = ((bf16[4,784,128]{2,1,0:T(8,128)(2,1)}), bf16[4,784,128]{2,1,0:T(8,128)(2,1)S(1)}, u32[]{:S(2)}, u32[]{:S(2)}) async-start(bf16[4,784,128]{2,1,0:T(8,128)(2,1)} %get-tuple-element.38), calls=%async_computation.1 | async-start | bytes 1605632 | tf_op jit(solution)/shard_map/all_to_all | solution.py:338
  67.3 11.8 %all-to-all-start.2 = ((bf16[4,768,128]{2,1,0:T(8,128)(2,1)}), bf16[4,768,128]{2,1,0:T(8,128)(2,1)S(1)}, u32[]{:S(2)}, u32[]{:S(2)}) async-start(bf16[4,768,128]{2,1,0:T(8,128)(2,1)} %get-tuple-element.43), calls=%async_computation.2 | async-start | bytes 1572864 | tf_op jit(solution)/shard_map/all_to_all | solution.py:363
  80.5 23.6 %all-to-all-start.3 = ((bf16[32,2,384]{2,1,0:T(2,128)(2,1)}), bf16[32,2,384]{2,1,0:T(2,128)(2,1)S(1)}, u32[]{:S(2)}, u32[]{:S(2)}) async-start(bf16[32,2,384]{2,1,0:T(2,128)(2,1)} %get-tuple-element.45), calls=%async_computation.3 | async-start | bytes 98304 | tf_op jit(solution)/shard_map/all_to_all | solution.py:368
  91.3 10.4 %collective-permute-start = (bf16[384,128]{1,0:T(8,128)(2,1)S(1)}, bf16[384,128]{1,0:T(8,128)(2,1)S(1)}, u32[]{:S(2)}, u32[]{:S(2)}) collective-permute-start(bf16[384,128]{1,0:T(8,128)(2,1)S(1)} %get-tuple-element.49), channel_id=1, source_target_pairs={{0,32},{32,0},{64,96},{96,64},{1,33},{33,1},{65,97},{97,65},{2,34}... | collective-permute-start | bytes 294920 | tf_op jit(solution)/shard_map/ppermute | solution.py:28
  93.3 8.4 %collective-permute-start.1 = (bf16[384,128]{1,0:T(8,128)(2,1)S(1)}, bf16[384,128]{1,0:T(8,128)(2,1)S(1)}, u32[]{:S(2)}, u32[]{:S(2)}) collective-permute-start(bf16[384,128]{1,0:T(8,128)(2,1)S(1)} %get-tuple-element.50), channel_id=1, source_target_pairs={{0,64},{32,96},{64,0},{96,32},{1,65},{33,97},{65,1},{97,33},{2,66}... | collective-permute-start | bytes 294920 | tf_op jit(solution)/shard_map/ppermute | solution.py:28
  96.4 6.9 %collective-permute-start.2 = (bf16[384,128]{1,0:T(8,128)(2,1)S(1)}, bf16[384,128]{1,0:T(8,128)(2,1)S(1)}, u32[]{:S(2)}, u32[]{:S(2)}) collective-permute-start(bf16[384,128]{1,0:T(8,128)(2,1)S(1)} %get-tuple-element.51), channel_id=1, source_target_pairs={{0,96},{32,64},{64,32},{96,0},{1,97},{33,65},{65,33},{97,1},{2,98}... | collective-permute-start | bytes 294920 | tf_op jit(solution)/shard_map/ppermute | solution.py:28

commit v9 on v7

--- a/solution.py
+++ b/solution.py
@@ -74,13 +74,14 @@
 
 
 def squares_kernel(q_ref, k_ref, msg_ref, own_ref):
+    ones = jnp.ones((16, WIDTH), BF16)
     sums = []
     for ref in (q_ref, k_ref):
-        parts = []
-        for i in range(PIECES):
-            block = ref[pl.ds(i * WIDTH, WIDTH), :].astype(F32)
-            parts.append(row_sums(block * block))
-        sums.append(jnp.concatenate(parts, axis=1))
+        value = ref[...].astype(F32)
+        square = value * value
+        high = square.astype(BF16)
+        low = (square - high.astype(F32)).astype(BF16)
+        sums.append((dot(ones, high, NT) + dot(ones, low, NT))[:1, :])
     both = jnp.concatenate(sums, axis=0)
     own_ref[...] = both
     coded = encode(both)

time: 106 us -> 106 us (level)
  no operation moved by 1% of the time
where the time goes in v9:
time: 106 us; the launch traced here: 105 us
  starting transfers between devices  44.9 us (42%)
  blocking collectives  27.4 us (26%)
  Pallas kernels  15.8 us (15%)
  waiting for transfers between devices  15.6 us (15%)
    all_to_all x1, starting transfers between devices, local(): squares = lax.all_to_all(squares, HEAD, 0, 0)  16.9 us
    pallas_call x8, Pallas kernels, run(): pl.pallas_call(kernel, out_shape=out_shape, in_specs=specs, out_specs=jax...  15.8 us
    all_gather x1, blocking collectives, local(): lax.all_gather(keys, 'y', axis=0, tiled=True)  12.4 us
    all_to_all x1, waiting for transfers between devices, local(): squares = lax.all_to_all(squares, HEAD, 0, 0)  11 us
    all_to_all x1, starting transfers between devices, local(): inner = lax.all_to_all(inner, HEAD, 0, 0)  10.9 us
    ppermute x3, starting transfers between devices, swap(): return lax.ppermute(value, axis, [(i, i ^ mask) for i in range(SIDE)])  9.58 us
    psum x1, blocking collectives, local(): totals = lax.psum(totals, 'x')  8.96 us
    psum x1, blocking collectives, local(): inner = lax.psum(inner, 'x')  6.1 us
  transfers between devices with their start and end apart: 7, of which 4 were waited for; matrix products, arithmetic and copies ran while one was open for 0% of the time, Pallas kernels for 1%

profile of v9, /device:TPU:1, one launch (start us, length us, event | category | flops | bytes accessed | tf_op | source)
XLA Modules:
  0.0 105.2 jit_solution(9401234157140886010)
XLA Ops:
  0.6 0.0 copy-start.3
  0.6 0.0 copy-start.4
  0.7 1.9 %shard_map.103 = (bf16[32,2,384]{2,1,0:T(2,128)(2,1)}, f32[2,384]{1,0:T(2,128)}) custom-call(bf16[384,128]{1,0:T(8,128)(2,1)} %q_ref.5, bf16[384,128]{1,0:T(8,128)(2,1)} %k_ref.7), custom_call_target="tpu_custom_call" | custom-call | tf_op jit(solution)/shard_map/pallas_call | solution.py:43
  2.5 0.0 copy-start.2
  2.5 16.9 %all-to-all-start = ((bf16[32,2,384]{2,1,0:T(2,128)(2,1)}), bf16[32,2,384]{2,1,0:T(2,128)(2,1)S(1)}, u32[]{:S(2)}, u32[]{:S(2)}) async-start(bf16[32,2,384]{2,1,0:T(2,128)(2,1)} %get-tuple-element.26), calls=%async_computation | async-start | bytes 98304 | tf_op jit(solution)/shard_map/all_to_all | solution.py:306
  19.4 0.1 pad_add_fusion.place_ref
  19.5 0.0 copy-start.5
  19.5 0.0 copy-start.6
  19.5 0.0 copy-start.7
  19.5 0.0 copy-start.8
  19.5 0.0 copy-done.3
  19.5 0.0 copy-done.4
  19.5 0.0 copy-done.2
  19.5 0.6 copy-done.5
  20.2 0.0 copy-done.6
  20.2 0.0 copy-done.7
  20.2 0.0 copy-done.8
  20.2 0.0 copy-start
  20.2 0.0 copy-start.1
  20.2 0.7 shard_map.104
  20.9 11.0 %all-to-all-done.sums_ref = bf16[32,2,384]{2,1,0:T(2,128)(2,1)S(1)} async-done(((bf16[32,2,384]{2,1,0:T(2,128)(2,1)}), bf16[32,2,384]{2,1,0:T(2,128)(2,1)S(1)}, u32[]{:S(2)}, u32[]{:S(2)}) %all-to-all-start) | async-done | bytes 49184 | tf_op jit(solution)/shard_map/all_to_all | solution.py:306
  31.9 0.0 copy-done
  31.9 0.0 copy-done.1
  31.9 1.0 shard_map.105
  33.0 4.0 %all-to-all-start.1 = ((bf16[4,784,128]{2,1,0:T(8,128)(2,1)}), bf16[4,784,128]{2,1,0:T(8,128)(2,1)S(1)}, u32[]{:S(2)}, u32[]{:S(2)}) async-start(bf16[4,784,128]{2,1,0:T(8,128)(2,1)} %get-tuple-element.34), calls=%async_computation.1 | async-start | bytes 1605632 | tf_op jit(solution)/shard_map/all_to_all | solution.py:326
  37.0 12.4 %all_gather.3 = bf16[3136,128]{1,0:T(8,128)(2,1)S(1)} all-gather(bf16[784,128]{1,0:T(8,128)(2,1)S(1)} %get-tuple-element.35), channel_id=1, replica_groups=mesh['y'=4,'x'=4,'z'=16,'c'=2] {'y'}, dimensions={0}, use_global_device_ids=true | all-gather | bytes 1003520 | tf_op jit(solution)/shard_map/all_gather | solution.py:327
  49.4 0.0 all-to-all-done.1.qall_ref
  49.4 2.0 %shard_map.106 = f32[4,1,384]{2,1,0:T(1,128)S(1)} custom-call(bf16[4,784,128]{2,1,0:T(8,128)(2,1)S(1)} %all-to-all-done.1.qall_ref, bf16[4,784,128]{2,1,0:T(8,128)(2,1)S(1)} %bitcast.5), custom_call_target="tpu_custom_call" | custom-call | tf_op jit(solution)/shard_map/pallas_call | solution.py:43
  51.4 9.0 %psum.14.total_ref = f32[4,1,384]{2,1,0:T(1,128)S(1)} all-reduce(f32[4,1,384]{2,1,0:T(1,128)S(1)} %shard_map.106), channel_id=1, replica_groups=mesh['y'=4,'x'=4,'z'=16,'c'=2] {'x'}, use_global_device_ids=true, to_apply=%region_0.0 | all-reduce | flops 1536 | bytes 12288 | tf_op jit(solution)/shard_map/psum | solution.py:334
  60.3 7.2 %shard_map.107 = (f32[1,1536]{1,0:T(1,128)S(1)}, bf16[4,768,128]{2,1,0:T(8,128)(2,1)}, bf16[4,384,128]{2,1,0:T(8,128)(2,1)S(1)}) custom-call(f32[4,1,384]{2,1,0:T(1,128)S(1)} %psum.14.total_ref, bf16[4,784,128]{2,1,0:T(8,128)(2,1)S(1)} %all-to-all-done.1.qall_ref, bf16[4,784,128]{2,1,0:T(8,128)(2,1)S(1)} %bitcast.6), custom_call_target="tpu_custom_call" | custom-call | tf_op jit(solution)/shard_map/pallas_call | solution.py:43
  67.5 3.5 %all-to-all-start.2 = ((bf16[4,768,128]{2,1,0:T(8,128)(2,1)}), bf16[4,768,128]{2,1,0:T(8,128)(2,1)S(1)}, u32[]{:S(2)}, u32[]{:S(2)}) async-start(bf16[4,768,128]{2,1,0:T(8,128)(2,1)} %get-tuple-element.37), calls=%async_computation.2 | async-start | bytes 1572864 | tf_op jit(solution)/shard_map/all_to_all | solution.py:353
  71.1 6.1 %psum.15.inner_ref = f32[1,1536]{1,0:T(1,128)S(1)} all-reduce(f32[1,1536]{1,0:T(1,128)S(1)} %get-tuple-element.36), channel_id=1, replica_groups=mesh['y'=4,'x'=4,'z'=16,'c'=2] {'x'}, use_global_device_ids=true, to_apply=%region_1.0 | all-reduce | flops 1536 | bytes 12288 | tf_op jit(solution)/shard_map/psum | solution.py:354
  77.2 2.2 %all-to-all-done.2.dkv_ref = bf16[4,768,128]{2,1,0:T(8,128)(2,1)S(1)} async-done(((bf16[4,768,128]{2,1,0:T(8,128)(2,1)}), bf16[4,768,128]{2,1,0:T(8,128)(2,1)S(1)}, u32[]{:S(2)}, u32[]{:S(2)}) %all-to-all-start.2) | async-done | bytes 786464 | tf_op jit(solution)/shard_map/all_to_all | solution.py:353
  79.4 1.3 %shard_map.108 = (f32[384,128]{1,0:T(8,128)S(1)}, bf16[32,2,384]{2,1,0:T(2,128)(2,1)}, f32[2,384]{1,0:T(2,128)S(1)}, bf16[384,128]{1,0:T(8,128)(2,1)S(1)}, bf16[...) custom-call(s32[2]{0:T(128)S(1)} %pad_add_fusion.place_ref, ...), custom_call_target="tpu_custom_call" | custom-call | tf_op jit(solution)/shard_map/pallas_call | solution.py:43
  80.7 10.9 %all-to-all-start.3 = ((bf16[32,2,384]{2,1,0:T(2,128)(2,1)}), bf16[32,2,384]{2,1,0:T(2,128)(2,1)S(1)}, u32[]{:S(2)}, u32[]{:S(2)}) async-start(bf16[32,2,384]{2,1,0:T(2,128)(2,1)} %get-tuple-element.39), calls=%async_computation.3 | async-start | bytes 98304 | tf_op jit(solution)/shard_map/all_to_all | solution.py:359
  91.6 2.0 %collective-permute-start = (bf16[384,128]{1,0:T(8,128)(2,1)S(1)}, bf16[384,128]{1,0:T(8,128)(2,1)S(1)}, u32[]{:S(2)}, u32[]{:S(2)}) collective-permute-start(bf16[384,128]{1,0:T(8,128)(2,1)S(1)} %get-tuple-element.43), channel_id=1, source_target_pairs={{0,32},{32,0},{64,96},{96,64},{1,33},{33,1},{65,97},{97,65},{2,34}... | collective-permute-start | bytes 294920 | tf_op jit(solution)/shard_map/ppermute | solution.py:28
  93.6 3.1 %collective-permute-start.1 = (bf16[384,128]{1,0:T(8,128)(2,1)S(1)}, bf16[384,128]{1,0:T(8,128)(2,1)S(1)}, u32[]{:S(2)}, u32[]{:S(2)}) collective-permute-start(bf16[384,128]{1,0:T(8,128)(2,1)S(1)} %get-tuple-element.44), channel_id=1, source_target_pairs={{0,64},{32,96},{64,0},{96,32},{1,65},{33,97},{65,1},{97,33},{2,66}... | collective-permute-start | bytes 294920 | tf_op jit(solution)/shard_map/ppermute | solution.py:28
  96.7 4.5 %collective-permute-start.2 = (bf16[384,128]{1,0:T(8,128)(2,1)S(1)}, bf16[384,128]{1,0:T(8,128)(2,1)S(1)}, u32[]{:S(2)}, u32[]{:S(2)}) collective-permute-start(bf16[384,128]{1,0:T(8,128)(2,1)S(1)} %get-tuple-element.45), channel_id=1, source_target_pairs={{0,96},{32,64},{64,32},{96,0},{1,97},{33,65},{65,33},{97,1},{2,98}... | collective-permute-start | bytes 294920 | tf_op jit(solution)/shard_map/ppermute | solution.py:28
  101.2 0.7 shard_map.110
  101.9 0.0 collective-permute-done.dq1_ref
  101.9 0.0 collective-permute-done.1.dq2_ref
  101.9 1.6 %collective-permute-done.2.dq3_ref = bf16[384,128]{1,0:T(8,128)(2,1)S(1)} collective-permute-done((bf16[384,128]{1,0:T(8,128)(2,1)S(1)}, bf16[384,128]{1,0:T(8,128)(2,1)S(1)}, u32[]{:S(2)}, u32[]{:S(2)}) %collective-permute-start.2) | collective-permute-done | bytes 98336 | tf_op jit(solution)/shard_map/ppermute | solution.py:28
  103.5 0.7 all-to-all-done.3.sums_ref
  104.3 1.0 shard_map.109
Async XLA Ops:
  0.6 18.9 %copy-start.3 = (bf16[384,128]{1,0:T(8,128)(2,1)S(1)}, bf16[384,128]{1,0:T(8,128)(2,1)}, u32[]{:S(2)}) copy-start(bf16[384,128]{1,0:T(8,128)(2,1)} %o_ref.1) | copy-start | bytes 294916
  0.6 18.9 %copy-start.4 = (bf16[384,128]{1,0:T(8,128)(2,1)S(1)}, bf16[384,128]{1,0:T(8,128)(2,1)}, u32[]{:S(2)}) copy-start(bf16[384,128]{1,0:T(8,128)(2,1)} %v_ref.1) | copy-start | bytes 294916
  2.5 17.0 %copy-start.2 = (bf16[384,128]{1,0:T(8,128)(2,1)S(1)}, bf16[384,128]{1,0:T(8,128)(2,1)}, u32[]{:S(2)}) copy-start(bf16[384,128]{1,0:T(8,128)(2,1)} %g_ref.1) | copy-start | bytes 294916
  2.5 29.4 %all-to-all-start = ((bf16[32,2,384]{2,1,0:T(2,128)(2,1)}), bf16[32,2,384]{2,1,0:T(2,128)(2,1)S(1)}, u32[]{:S(2)}, u32[]{:S(2)}) async-start(bf16[32,2,384]{2,1,0:T(2,128)(2,1)} %get-tuple-element.26), calls=%async_computation | async-start | bytes 98304 | tf_op jit(solution)/shard_map/all_to_all | solution.py:306
  19.5 0.7 copy-start.5
  19.5 0.7 copy-start.6
  19.5 0.7 copy-start.7
  19.5 0.7 copy-start.8
  20.2 11.7 %copy-start = (bf16[384,128]{1,0:T(8,128)(2,1)S(1)}, bf16[384,128]{1,0:T(8,128)(2,1)}, u32[]{:S(2)}) copy-start(bf16[384,128]{1,0:T(8,128)(2,1)} %k_ref.7) | copy-start | bytes 294916
  20.2 11.7 %copy-start.1 = (bf16[384,128]{1,0:T(8,128)(2,1)S(1)}, bf16[384,128]{1,0:T(8,128)(2,1)}, u32[]{:S(2)}) copy-start(bf16[384,128]{1,0:T(8,128)(2,1)} %q_ref.5) | copy-start | bytes 294916
  33.0 16.4 %all-to-all-start.1 = ((bf16[4,784,128]{2,1,0:T(8,128)(2,1)}), bf16[4,784,128]{2,1,0:T(8,128)(2,1)S(1)}, u32[]{:S(2)}, u32[]{:S(2)}) async-start(bf16[4,784,128]{2,1,0:T(8,128)(2,1)} %get-tuple-element.34), calls=%async_computation.1 | async-start | bytes 1605632 | tf_op jit(solution)/shard_map/all_to_all | solution.py:326
  67.5 11.8 %all-to-all-start.2 = ((bf16[4,768,128]{2,1,0:T(8,128)(2,1)}), bf16[4,768,128]{2,1,0:T(8,128)(2,1)S(1)}, u32[]{:S(2)}, u32[]{:S(2)}) async-start(bf16[4,768,128]{2,1,0:T(8,128)(2,1)} %get-tuple-element.37), calls=%async_computation.2 | async-start | bytes 1572864 | tf_op jit(solution)/shard_map/all_to_all | solution.py:353
  80.7 23.6 %all-to-all-start.3 = ((bf16[32,2,384]{2,1,0:T(2,128)(2,1)}), bf16[32,2,384]{2,1,0:T(2,128)(2,1)S(1)}, u32[]{:S(2)}, u32[]{:S(2)}) async-start(bf16[32,2,384]{2,1,0:T(2,128)(2,1)} %get-tuple-element.39), calls=%async_computation.3 | async-start | bytes 98304 | tf_op jit(solution)/shard_map/all_to_all | solution.py:359
  91.6 10.3 %collective-permute-start = (bf16[384,128]{1,0:T(8,128)(2,1)S(1)}, bf16[384,128]{1,0:T(8,128)(2,1)S(1)}, u32[]{:S(2)}, u32[]{:S(2)}) collective-permute-start(bf16[384,128]{1,0:T(8,128)(2,1)S(1)} %get-tuple-element.43), channel_id=1, source_target_pairs={{0,32},{32,0},{64,96},{96,64},{1,33},{33,1},{65,97},{97,65},{2,34}... | collective-permute-start | bytes 294920 | tf_op jit(solution)/shard_map/ppermute | solution.py:28
  93.6 8.3 %collective-permute-start.1 = (bf16[384,128]{1,0:T(8,128)(2,1)S(1)}, bf16[384,128]{1,0:T(8,128)(2,1)S(1)}, u32[]{:S(2)}, u32[]{:S(2)}) collective-permute-start(bf16[384,128]{1,0:T(8,128)(2,1)S(1)} %get-tuple-element.44), channel_id=1, source_target_pairs={{0,64},{32,96},{64,0},{96,32},{1,65},{33,97},{65,1},{97,33},{2,66}... | collective-permute-start | bytes 294920 | tf_op jit(solution)/shard_map/ppermute | solution.py:28
  96.7 6.9 %collective-permute-start.2 = (bf16[384,128]{1,0:T(8,128)(2,1)S(1)}, bf16[384,128]{1,0:T(8,128)(2,1)S(1)}, u32[]{:S(2)}, u32[]{:S(2)}) collective-permute-start(bf16[384,128]{1,0:T(8,128)(2,1)S(1)} %get-tuple-element.45), channel_id=1, source_target_pairs={{0,96},{32,64},{64,32},{96,0},{1,97},{33,65},{65,33},{97,1},{2,98}... | collective-permute-start | bytes 294920 | tf_op jit(solution)/shard_map/ppermute | solution.py:28
